TPU v7x, 32 devices: a whole 2x2x4 slice. The times are simulated.
32 devices in a mesh: grp: 2 (over y), var: 4 (over z), smp: 2 (over x), sub: 2 (over core).
Axes of the slice: x: 2, y: 2, z: 4, core: 2. Of those that a mesh axis runs over, the one named last changes fastest.
Arguments:
- dosages: int32 [2048, 8192], P('smp', ('grp', 'var', 'sub')), parts along dimension 1, may hold values from 0 to 200
- observed: int32 [2048, 8192], P('smp', ('grp', 'var', 'sub')), parts along dimension 1, may hold values from 0 to 1, as said below
Outputs:
- correlations: bfloat16 [8192, 4, 1024], P(('grp', 'var', 'smp'), None, 'sub'), parts along dimension 0
There are 2 independent parts, one for each index of `grp`. A program takes and returns all parts, laid end to end along the dimension named above; each array names one. Nothing has to cross between parts.
Inputs may be any that keep to these rules, and one draw needn't show every extreme that they name: `observed`: each variant is missing in a share of samples of its own.
All inputs are finite; a program needn't handle non-finite values.
Results may differ from a plain program's by a relative error of at most 0.0051.
Values may be sent and summed in bfloat16 or wider, within the bound.
No kernel may reach another device: no remote copies, remote signals or barrier semaphores. Data moves between devices by JAX's collectives and lax.ppermute only.
A program may use at most 64 MiB of HBM per device.

v0:
```python
import jax
import jax.numpy as jnp
from jax import lax
from jax.sharding import PartitionSpec as P

BAND = 4


def shifted(block, axis, distance):
    devices = range(lax.axis_size(axis))
    route = [(i - distance, i) for i in devices if i - distance in devices]
    return lax.ppermute(block, axis, route)


def on_device(dosages, observed):
    values = dosages.astype(jnp.float32) / 100.0
    weights = observed.astype(jnp.float32)
    counts, sums_all = lax.psum(
        (jnp.sum(weights, axis=0), jnp.sum(weights * values, axis=0)), "smp"
    )
    counts = jnp.maximum(counts, 1.0)
    means = sums_all / counts
    centered = values - means
    spreads = lax.psum(jnp.sum(weights * centered * centered, axis=0), "smp") / counts
    own_cols = (weights * centered * lax.rsqrt(spreads + 1e-05)).astype(jnp.bfloat16)
    whole_block = lax.all_gather(own_cols, "sub", axis=1, tiled=True)
    width_half = own_cols.shape[1]
    panels = [own_cols]
    for offset in range(1, BAND):
        arrived = shifted(whole_block, "var", -offset)
        panels.append(
            lax.dynamic_slice_in_dim(arrived, lax.axis_index("sub") * width_half, width_half, 1)
        )
    stacked = jnp.concatenate(panels, axis=1)
    rows_owned = whole_block.shape[1] // lax.axis_size("smp")
    factor = 1.0 / (own_cols.shape[0] * lax.axis_size("smp"))
    product = lax.dot_general(
        whole_block, stacked, (((0,), (0,)), ((), ())), preferred_element_type=jnp.float32
    )
    return lax.psum_scatter(
        (product * factor)
        .reshape(rows_owned * lax.axis_size("smp"), BAND, width_half)
        .astype(jnp.bfloat16),
        "smp",
        scatter_dimension=0,
        tiled=True,
    )


def solution(mesh):
    in_specs = (P("smp", ("grp", "var", "sub")), P("smp", ("grp", "var", "sub")))
    out_specs = P(("grp", "var", "smp"), None, "sub")
    return jax.shard_map(
        on_device, mesh=mesh, in_specs=in_specs, out_specs=out_specs, check_vma=False
    )
```

profile of v0, /device:TPU:0, one launch (start us, length us, event | category | flops | bytes accessed | tf_op | source)
XLA Modules:
  0.0 356.6 jit_solution(12693675328682105579)
XLA Ops:
  6.5 2.9 convert_reduce_fusion
  9.4 5.8 %all-reduce.1 = (f32[512]{0:T(512)S(1)}, f32[512]{0:T(512)S(1)}) all-reduce(f32[512]{0:T(512)S(1)} %get-tuple-element.6, f32[512]{0:T(512)S(1)} %get-tuple-element.5), channel_id=1, replica_groups=mesh['grp'=2,'var'=4,'smp'=2,'sub'=2] {'smp'}, use_global_device_ids=true, to_apply=%region_1.0 | all-reduce | flops 1024 | bytes 8192 | tf_op jit(solution)/shard_map/psum | solution.py:18
  15.2 2.1 multiply_reduce_fusion
  17.3 4.9 %psum.23 = f32[512]{0:T(512)S(1)} all-reduce(f32[512]{0:T(512)S(1)} %multiply_reduce_fusion), channel_id=1, replica_groups=mesh['grp'=2,'var'=4,'smp'=2,'sub'=2] {'smp'}, use_global_device_ids=true, to_apply=%region_5.0 | all-reduce | flops 512 | bytes 4096 | tf_op jit(solution)/shard_map/psum | solution.py:24
  22.3 3.1 multiply_convert_fusion.1
  25.4 0.0 all-gather.2.cloned.1.call-update
  25.4 0.0 all-reduce.4.cloned.1.call-start
  25.5 12.5 %all-gather.2.cloned.1.call-done = bf16[1024,1024]{1,0:T(8,128)(2,1)} async-done(((bf16[1024,512]{1,0:T(8,128)(2,1)}), bf16[1024,1024]{1,0:T(8,128)(2,1)}) %all-gather.2.cloned.1.call-update) | async-done | bytes 2097168 | tf_op jit(solution)/shard_map/all_gather | solution.py:26
  38.0 1.3 collective-permute-start.1
  39.3 1.3 collective-permute-start
  40.6 1.3 collective-permute-start.2
  41.9 92.6 %collective-permute-done.1 = bf16[1024,1024]{1,0:T(8,128)(2,1)} collective-permute-done((bf16[1024,1024]{1,0:T(8,128)(2,1)}, bf16[1024,1024]{1,0:T(8,128)(2,1)}, u32[]{:S(2)}, u32[]{:S(2)}) %collective-permute-start.1) | collective-permute-done | bytes 2097184 | tf_op jit(solution)/shard_map/ppermute | solution.py:12
  134.5 1.3 constant_dynamic-slice_fusion.1
  135.8 0.0 copy-start.1
  135.8 1.5 constant_dynamic-slice_fusion.2
  137.3 42.7 %collective-permute-done.2 = bf16[1024,1024]{1,0:T(8,128)(2,1)S(1)} collective-permute-done((bf16[1024,1024]{1,0:T(8,128)(2,1)}, bf16[1024,1024]{1,0:T(8,128)(2,1)S(1)}, u32[]{:S(2)}, u32[]{:S(2)}) %collective-permute-start.2) | collective-permute-done | bytes 2097184 | tf_op jit(solution)/shard_map/ppermute | solution.py:12
  180.0 0.1 constant_dynamic-slice_fusion
  180.2 6.7 %multiply_convert_fusion = bf16[1024,2048]{1,0:T(8,128)(2,1)} fusion(bf16[1024,1024]{1,0:T(8,128)(2,1)S(1)} %copy-done.2, bf16[1024,512]{1,0:T(8,128)(2,1)S(1)} %constant_dynamic-slice_fusion, bf16[1024,512]{1,0:T(8,128)(2,1)S(1)} %constant_dynamic-slice_fusion.1, bf16[1024,512]{1,0:T(8,128)(2,1)S(1)} %constant_dynamic-slice_fusion.2, ...), kind=kOutput, calls=%fused_computation | convolution fusion | flops 4315938816 | bytes 10485760 | tf_op jit(solution)/shard_map/dot_general | solution.py:37
  186.8 7.8 %convert_element_type.19 = bf16[1024,4,512]{2,1,0:T(4,128)(2,1)} reshape(bf16[1024,2048]{1,0:T(8,128)(2,1)} %multiply_convert_fusion) | data formatting | bytes 8388608 | tf_op jit(solution)/shard_map/convert_element_type | solution.py:43
  194.7 0.0 all-reduce.4.cloned.1.call-update
  194.7 0.6 copy-done.3
  195.3 0.6 dynamic-slice
  196.5 149.6 %all-reduce.4.cloned.1.call-done = bf16[1024,4,512]{2,1,0:T(4,128)(2,1)} async-done(((bf16[1024,4,512]{2,1,0:T(4,128)(2,1)}), bf16[1024,4,512]{2,1,0:T(4,128)(2,1)}) %all-reduce.4.cloned.1.call-update) | async-done | bytes 4194320
  346.1 3.6 %constant_dynamic-slice_fusion.3 = bf16[512,4,512]{2,1,0:T(4,128)(2,1)} fusion(bf16[1024,4,512]{2,1,0:T(4,128)(2,1)} %all-reduce.4.cloned.1.call-done, u32[]{:T(128)S(6)} %multiply.2), kind=kLoop, calls=%fused_computation.20 | loop fusion | bytes 4194308
  (10 shorter events, 0.0 us)
Async XLA Ops:
  6.5 8.7 %copy-start = (s32[1024,512]{1,0:T(8,128)S(1)}, s32[1024,512]{1,0:T(8,128)}, u32[]{:S(2)}) copy-start(s32[1024,512]{1,0:T(8,128)} %param.3) | copy-start | bytes 6291460
  6.5 31.5 %all-gather.2.cloned.1.call-start = ((), (), s32[]{:S(2)}) async-start(), calls=%async_computation | async-start | bytes 3145728 | tf_op jit(solution)/shard_map/all_gather | solution.py:26
  25.4 320.7 %all-reduce.4.cloned.1.call-start = ((), (), s32[]{:S(2)}) async-start(), calls=%async_computation.1 | async-start | bytes 8388608
  38.0 96.5 %collective-permute-start.1 = (bf16[1024,1024]{1,0:T(8,128)(2,1)}, bf16[1024,1024]{1,0:T(8,128)(2,1)}, u32[]{:S(2)}, u32[]{:S(2)}) collective-permute-start(bf16[1024,1024]{1,0:T(8,128)(2,1)} %all-gather.2.cloned.1.call-done), channel_id=1, source_target_pairs={{8,0},{12,4},{9,1},{13,5},{10,2},{14,6},{11,3},{15,7},{24,16},{28,... | collective-permute-start | bytes 6291464 | tf_op jit(solution)/shard_map/ppermute | solution.py:12
  39.3 96.6 %collective-permute-start = (bf16[1024,1024]{1,0:T(8,128)(2,1)}, bf16[1024,1024]{1,0:T(8,128)(2,1)}, u32[]{:S(2)}, u32[]{:S(2)}) collective-permute-start(bf16[1024,1024]{1,0:T(8,128)(2,1)} %all-gather.2.cloned.1.call-done), channel_id=1, source_target_pairs={{4,0},{8,4},{12,8},{5,1},{9,5},{13,9},{6,2},{10,6},{14,10},{7,3},{... | collective-permute-start | bytes 6291464 | tf_op jit(solution)/shard_map/ppermute | solution.py:12
  40.6 139.5 %collective-permute-start.2 = (bf16[1024,1024]{1,0:T(8,128)(2,1)}, bf16[1024,1024]{1,0:T(8,128)(2,1)S(1)}, u32[]{:S(2)}, u32[]{:S(2)}) collective-permute-start(bf16[1024,1024]{1,0:T(8,128)(2,1)} %all-gather.2.cloned.1.call-done), channel_id=1, source_target_pairs={{12,0},{13,1},{14,2},{15,3},{28,16},{29,17},{30,18},{31,19}} | collective-permute-start | bytes 6291464 | tf_op jit(solution)/shard_map/ppermute | solution.py:12
  135.8 44.3 %copy-start.1 = (bf16[1024,512]{1,0:T(8,128)(2,1)S(1)}, bf16[1024,512]{1,0:T(8,128)(2,1)}, u32[]{:S(2)}) copy-start(bf16[1024,512]{1,0:T(8,128)(2,1)} %multiply_convert_fusion.1) | copy-start | bytes 3145732
  135.8 44.3 %copy-start.2 = (bf16[1024,1024]{1,0:T(8,128)(2,1)S(1)}, bf16[1024,1024]{1,0:T(8,128)(2,1)}, u32[]{:S(2)}) copy-start(bf16[1024,1024]{1,0:T(8,128)(2,1)} %all-gather.2.cloned.1.call-done) | copy-start | bytes 6291460
  194.7 0.7 copy-start.3
Sparse Core Ops, SparseCore 0:
  25.6 12.3 all-gather.1
  194.8 151.2 all-reduce.3
where the time goes:
time: 357 us
  waiting for transfers between devices  297 us (83%)
  local copies, waits for them, and re-layouts  15.5 us (4%)
  between operations  14.1 us (4%)
  blocking collectives  10.8 us (3%)
  other arithmetic  8.1 us (2%)
  matrix products  6.67 us (2%)
  starting transfers between devices  3.91 us (1%)
    unnamed x3, waiting for transfers between devices  150 us
    ppermute x3, waiting for transfers between devices, shifted(): return lax.ppermute(block, axis, route)  135 us
    all_gather x1, waiting for transfers between devices, on_device(): whole_block = lax.all_gather(own_cols, 'sub', axis=1, tiled=True)  12.5 us
    convert_element_type x1, local copies, waits for them, and re-layouts, on_device(): return lax.psum_scatter((product * factor).reshape(rows_owned * lax.axis_...  7.82 us
  transfers between devices with their start and end apart: 5, of which 4 were waited for; matrix products, arithmetic and copies ran while one was open for 1% of the time, Pallas kernels for 0%

commit v1 on v0

v1 whole, which is shorter than its diff:
```python
import jax
import jax.numpy as jnp
from jax import lax
from jax.sharding import PartitionSpec as P

BAND = 4
CHUNKS = 2


def shifted(block, axis, distance):
    devices = range(lax.axis_size(axis))
    route = [(i - distance, i) for i in devices if i - distance in devices]
    return lax.ppermute(block, axis, route)


def rotated(block, axis, distance):
    n = lax.axis_size(axis)
    return lax.ppermute(block, axis, [(i, (i + distance) % n) for i in range(n)])


def standardize(code, stats):
    value = code.astype(jnp.float32)
    return jnp.where(value >= 0, (value - stats[0:1]) * stats[1:2], 0.0).astype(jnp.bfloat16)


def variant_stats(sums):
    counts = jnp.maximum(sums[0], 1)
    n = counts.astype(jnp.float32)
    pivot = jnp.round(sums[1].astype(jnp.float32) / n).astype(jnp.int32)
    rest = (sums[1] - pivot * counts).astype(jnp.float32)
    squares = (sums[2] - 2 * pivot * sums[1] + pivot * pivot * sums[0]).astype(jnp.float32)
    spreads = (squares - rest * rest / n) / n * 1e-4
    means = pivot.astype(jnp.float32) + rest / n
    return jnp.stack([means, lax.rsqrt(spreads + 1e-05) * 0.01])


def on_device(dosages, observed):
    n_smp = lax.axis_size("smp")
    n_sub = lax.axis_size("sub")
    me_smp = lax.axis_index("smp")
    me_sub = lax.axis_index("sub")
    samples, width = dosages.shape
    rows_owned = width * n_sub // n_smp
    factor = 1.0 / (samples * n_smp)

    kept = observed > 0
    code = jnp.where(kept, dosages, -1).astype(jnp.bfloat16)
    known = jnp.where(kept, dosages, 0)
    sums_own = jnp.stack(
        [jnp.sum(observed, axis=0), jnp.sum(known, axis=0), jnp.sum(known * known, axis=0)]
    )
    sums = sums_own
    for d in range(1, n_smp):
        sums = sums + rotated(sums_own, "smp", d)
    stats = variant_stats(sums)

    piece = width // CHUNKS
    chunks = [lax.slice_in_dim(code, c * piece, (c + 1) * piece, axis=1) for c in range(CHUNKS)]
    codes = [chunks]
    for _ in range(1, BAND):
        codes.append([shifted(x, "var", -1) for x in codes[-1]])
    all_stats = [stats] + [shifted(stats, "var", -k) for k in range(1, BAND)]

    own = standardize(code, stats)
    parts = [own] + [rotated(own, "sub", d) for d in range(1, n_sub)]
    whole = jnp.zeros((samples, n_sub * width), jnp.bfloat16)
    for d, part in enumerate(parts):
        whole = lax.dynamic_update_slice_in_dim(whole, part, (me_sub - d) % n_sub * width, 1)
    rows = [
        lax.dynamic_slice_in_dim(whole, (me_smp + d) % n_smp * rows_owned, rows_owned, 1)
        for d in range(n_smp)
    ]

    def product(left, right):
        out = lax.dot_general(
            left, right, (((0,), (0,)), ((), ())), preferred_element_type=jnp.float32
        )
        return (out * factor).astype(jnp.bfloat16)

    panels = []
    for k in range(BAND):
        cols = [
            standardize(codes[k][c], all_stats[k][:, c * piece:(c + 1) * piece])
            for c in range(CHUNKS)
        ]
        for c in range(CHUNKS):
            total = product(rows[0], cols[c]).astype(jnp.float32)
            for d in range(1, n_smp):
                total = total + rotated(product(rows[d], cols[c]), "smp", d).astype(jnp.float32)
            panels.append(total.astype(jnp.bfloat16))
    return jnp.concatenate(panels, axis=1).reshape(rows_owned, BAND, width)


def solution(mesh):
    in_specs = (P("smp", ("grp", "var", "sub")), P("smp", ("grp", "var", "sub")))
    out_specs = P(("grp", "var", "smp"), None, "sub")
    return jax.shard_map(
        on_device, mesh=mesh, in_specs=in_specs, out_specs=out_specs, check_vma=False
    )
```

time: 357 us -> 117 us (0.33)
  waiting for transfers between devices: 297 us -> 76 us
  starting transfers between devices: 3.91 us -> 25.8 us
  between operations: 14.1 us -> 0.35 us
  local copies, waits for them, and re-layouts: 15.5 us -> 3.57 us
  blocking collectives: 10.8 us -> 0 us
  other arithmetic: 8.1 us -> 3.62 us
    unnamed x3 -> x0, waiting for transfers between devices: 150 us -> none
    ppermute x3 -> x9, waiting for transfers between devices: 135 us -> 46.7 us  [shifted(): return lax.ppermute(block, axis, route)]
    ppermute x0 -> x10, waiting for transfers between devices: none -> 29.2 us  [rotated(): lax.ppermute(block, axis, [(i, (i + distance) % n) for i in range(n)])]
    ppermute x0 -> x10, starting transfers between devices: none -> 14.2 us  [rotated(): lax.ppermute(block, axis, [(i, (i + distance) % n) for i in range(n)])]
    all_gather x1 -> x0, waiting for transfers between devices: 12.5 us -> none  [on_device(): whole_block = lax.all_gather(own_cols, 'sub', axis=1, tiled=True)]
    psum x2 -> x0, blocking collectives: 10.8 us -> none  [the longest x1 5.84 us: on_device(): lax.psum((jnp.sum(weights, axis=0), jnp.sum(weights * values, axis=0)), '...]
    convert_element_type x1 -> x0, local copies, waits for them, and re-layouts: 7.82 us -> none  [on_device(): return lax.psum_scatter((product * factor).reshape(rows_owned * lax.axis_...]
    ppermute x3 -> x9, starting transfers between devices: 3.86 us -> 11.6 us  [shifted(): return lax.ppermute(block, axis, route)]
  transfers between devices with their start and end apart: 5 -> 19, of which waited for: 4 -> 13; matrix products, arithmetic and copies ran while one was open for 1% -> 6% of each run, Pallas kernels for 0% -> 0%
where the time goes in v1:
time: 117 us
  waiting for transfers between devices  76 us (65%)
  starting transfers between devices  25.8 us (22%)
  matrix products  7.84 us (7%)
  other arithmetic  3.62 us (3%)
  local copies, waits for them, and re-layouts  3.57 us (3%)
    ppermute x9, waiting for transfers between devices, shifted(): return lax.ppermute(block, axis, route)  46.7 us
    ppermute x10, waiting for transfers between devices, rotated(): lax.ppermute(block, axis, [(i, (i + distance) % n) for i in range(n)])  29.2 us
    ppermute x10, starting transfers between devices, rotated(): lax.ppermute(block, axis, [(i, (i + distance) % n) for i in range(n)])  14.2 us
    ppermute x9, starting transfers between devices, shifted(): return lax.ppermute(block, axis, route)  11.6 us
    dot_general x16, matrix products, product(): lax.dot_general(left, right, (((0,), (0,)), ((), ())), preferred_element_...  7.84 us
    reshape x1, local copies, waits for them, and re-layouts, on_device(): return jnp.concatenate(panels, axis=1).reshape(rows_owned, BAND, width)  3.07 us
    reduce_sum x1, other arithmetic, on_device(): jnp.sum(known, axis=0)  2.85 us
  transfers between devices with their start and end apart: 19, of which 13 were waited for; matrix products, arithmetic and copies ran while one was open for 6% of the time, Pallas kernels for 0%

profile of v1, /device:TPU:0, one launch (start us, length us, event | category | flops | bytes accessed | tf_op | source)
XLA Modules:
  0.0 117.1 jit_solution(6281023065628793864)
XLA Ops:
  0.0 2.9 %select_reduce_fusion = (s32[512]{0:T(512)S(1)}, s32[512]{0:T(512)S(1)}, pred[1024,512]{1,0:T(8,128)(4,1)S(1)}, s32[512]{0:T(512)S(1)}) fusion(s32[1024,512]{1,0:T(8,128)} %param.2, s32[1024,512]{1,0:T(8,128)} %param.3), kind=kLoop, calls=%fused_computation.7 | loop fusion | flops 3144192 | bytes 4724736 | tf_op jit(solution)/shard_map/reduce_sum | solution.py:50
  2.9 3.0 %collective-permute-start = (s32[3,512]{1,0:T(4,128)S(1)}, s32[3,512]{1,0:T(4,128)S(1)}, u32[]{:S(2)}, u32[]{:S(2)}) collective-permute-start(s32[3,512]{1,0:T(4,128)S(1)} %pad_add_fusion), channel_id=1, source_target_pairs={{0,2},{2,0},{1,3},{3,1},{4,6},{6,4},{5,7},{7,5},{8,10},{10,8},{9,1... | collective-permute-start | bytes 18440 | tf_op jit(solution)/shard_map/ppermute | solution.py:18
  5.9 1.6 %collective-permute-done = s32[3,512]{1,0:T(4,128)S(1)} collective-permute-done((s32[3,512]{1,0:T(4,128)S(1)}, s32[3,512]{1,0:T(4,128)S(1)}, u32[]{:S(2)}, u32[]{:S(2)}) %collective-permute-start) | collective-permute-done | bytes 6176 | tf_op jit(solution)/shard_map/ppermute | solution.py:18
  8.7 1.3 %collective-permute-start.4 = (bf16[1024,256]{1,0:T(8,128)(2,1)S(1)}, bf16[1024,256]{1,0:T(8,128)(2,1)S(1)}, u32[]{:S(2)}, u32[]{:S(2)}) collective-permute-start(bf16[1024,256]{1,0:T(8,128)(2,1)S(1)} %get-tuple-element.15), channel_id=1, source_target_pairs={{4,0},{8,4},{12,8},{5,1},{9,5},{13,9},{6,2},{10,6},{14,10},{7,3},{... | collective-permute-start | bytes 1572872 | tf_op jit(solution)/shard_map/ppermute | solution.py:13
  10.0 1.3 %collective-permute-start.7 = (bf16[1024,256]{1,0:T(8,128)(2,1)S(1)}, bf16[1024,256]{1,0:T(8,128)(2,1)S(1)}, u32[]{:S(2)}, u32[]{:S(2)}) collective-permute-start(bf16[1024,256]{1,0:T(8,128)(2,1)S(1)} %get-tuple-element.14), channel_id=1, source_target_pairs={{4,0},{8,4},{12,8},{5,1},{9,5},{13,9},{6,2},{10,6},{14,10},{7,3},{... | collective-permute-start | bytes 1572872 | tf_op jit(solution)/shard_map/ppermute | solution.py:13
  14.0 22.7 %collective-permute-done.5 = f32[2,512]{1,0:T(2,128)S(1)} collective-permute-done((f32[2,512]{1,0:T(2,128)S(1)}, f32[2,512]{1,0:T(2,128)S(1)}, u32[]{:S(2)}, u32[]{:S(2)}) %collective-permute-start.5) | collective-permute-done | bytes 4128 | tf_op jit(solution)/shard_map/ppermute | solution.py:13
  40.6 3.4 %collective-permute-done.15 = f32[2,512]{1,0:T(2,128)S(1)} collective-permute-done((f32[2,512]{1,0:T(2,128)S(1)}, f32[2,512]{1,0:T(2,128)S(1)}, u32[]{:S(2)}, u32[]{:S(2)}) %collective-permute-start.15) | collective-permute-done | bytes 4128 | tf_op jit(solution)/shard_map/ppermute | solution.py:13
  44.0 10.6 %collective-permute-done.9 = bf16[1024,256]{1,0:T(8,128)(2,1)S(1)} collective-permute-done((bf16[1024,256]{1,0:T(8,128)(2,1)S(1)}, bf16[1024,256]{1,0:T(8,128)(2,1)S(1)}, u32[]{:S(2)}, u32[]{:S(2)}) %collective-permute-start.9) | collective-permute-done | bytes 524320 | tf_op jit(solution)/shard_map/ppermute | solution.py:13
  56.0 9.9 %collective-permute-done.12 = bf16[1024,256]{1,0:T(8,128)(2,1)S(1)} collective-permute-done((bf16[1024,256]{1,0:T(8,128)(2,1)S(1)}, bf16[1024,256]{1,0:T(8,128)(2,1)S(1)}, u32[]{:S(2)}, u32[]{:S(2)}) %collective-permute-start.12) | collective-permute-done | bytes 524320 | tf_op jit(solution)/shard_map/ppermute | solution.py:13
  67.8 1.7 %collective-permute-start.2 = (bf16[512,256]{0,1:T(8,128)(2,1)S(1)}, bf16[512,256]{0,1:T(8,128)(2,1)S(1)}, u32[]{:S(2)}, u32[]{:S(2)}) collective-permute-start(bf16[512,256]{0,1:T(8,128)(2,1)S(1)} %fusion.4), channel_id=1, source_target_pairs={{0,2},{2,0},{1,3},{3,1},{4,6},{6,4},{5,7},{7,5},{8,10},{10,8},{9,1... | collective-permute-start | bytes 786440 | tf_op jit(solution)/shard_map/ppermute | solution.py:18
  71.0 1.7 %collective-permute-start.6 = (bf16[512,256]{0,1:T(8,128)(2,1)S(1)}, bf16[512,256]{0,1:T(8,128)(2,1)S(1)}, u32[]{:S(2)}, u32[]{:S(2)}) collective-permute-start(bf16[512,256]{0,1:T(8,128)(2,1)S(1)} %fusion.8), channel_id=1, source_target_pairs={{0,2},{2,0},{1,3},{3,1},{4,6},{6,4},{5,7},{7,5},{8,10},{10,8},{9,1... | collective-permute-start | bytes 786440 | tf_op jit(solution)/shard_map/ppermute | solution.py:18
  74.2 2.9 %collective-permute-done.2 = bf16[512,256]{0,1:T(8,128)(2,1)S(1)} collective-permute-done((bf16[512,256]{0,1:T(8,128)(2,1)S(1)}, bf16[512,256]{0,1:T(8,128)(2,1)S(1)}, u32[]{:S(2)}, u32[]{:S(2)}) %collective-permute-start.2) | collective-permute-done | bytes 262176 | tf_op jit(solution)/shard_map/ppermute | solution.py:18
  77.1 1.7 %collective-permute-start.8 = (bf16[512,256]{0,1:T(8,128)(2,1)S(1)}, bf16[512,256]{0,1:T(8,128)(2,1)S(1)}, u32[]{:S(2)}, u32[]{:S(2)}) collective-permute-start(bf16[512,256]{0,1:T(8,128)(2,1)S(1)} %fusion.10), channel_id=1, source_target_pairs={{0,2},{2,0},{1,3},{3,1},{4,6},{6,4},{5,7},{7,5},{8,10},{10,8},{9,1... | collective-permute-start | bytes 786440 | tf_op jit(solution)/shard_map/ppermute | solution.py:18
  79.3 3.5 %collective-permute-done.3 = bf16[512,256]{0,1:T(8,128)(2,1)S(1)} collective-permute-done((bf16[512,256]{0,1:T(8,128)(2,1)S(1)}, bf16[512,256]{0,1:T(8,128)(2,1)S(1)}, u32[]{:S(2)}, u32[]{:S(2)}) %collective-permute-start.3) | collective-permute-done | bytes 262176 | tf_op jit(solution)/shard_map/ppermute | solution.py:18
  82.8 1.7 %collective-permute-start.11 = (bf16[512,256]{0,1:T(8,128)(2,1)S(1)}, bf16[512,256]{0,1:T(8,128)(2,1)S(1)}, u32[]{:S(2)}, u32[]{:S(2)}) collective-permute-start(bf16[512,256]{0,1:T(8,128)(2,1)S(1)} %fusion.12), channel_id=1, source_target_pairs={{0,2},{2,0},{1,3},{3,1},{4,6},{6,4},{5,7},{7,5},{8,10},{10,8},{9,1... | collective-permute-start | bytes 786440 | tf_op jit(solution)/shard_map/ppermute | solution.py:18
  84.9 3.4 %collective-permute-done.6 = bf16[512,256]{0,1:T(8,128)(2,1)S(1)} collective-permute-done((bf16[512,256]{0,1:T(8,128)(2,1)S(1)}, bf16[512,256]{0,1:T(8,128)(2,1)S(1)}, u32[]{:S(2)}, u32[]{:S(2)}) %collective-permute-start.6) | collective-permute-done | bytes 262176 | tf_op jit(solution)/shard_map/ppermute | solution.py:18
  88.4 1.7 %collective-permute-start.13 = (bf16[512,256]{0,1:T(8,128)(2,1)S(1)}, bf16[512,256]{0,1:T(8,128)(2,1)S(1)}, u32[]{:S(2)}, u32[]{:S(2)}) collective-permute-start(bf16[512,256]{0,1:T(8,128)(2,1)S(1)} %fusion.14), channel_id=1, source_target_pairs={{0,2},{2,0},{1,3},{3,1},{4,6},{6,4},{5,7},{7,5},{8,10},{10,8},{9,1... | collective-permute-start | bytes 786440 | tf_op jit(solution)/shard_map/ppermute | solution.py:18
  90.6 3.4 %collective-permute-done.8 = bf16[512,256]{0,1:T(8,128)(2,1)S(1)} collective-permute-done((bf16[512,256]{0,1:T(8,128)(2,1)S(1)}, bf16[512,256]{0,1:T(8,128)(2,1)S(1)}, u32[]{:S(2)}, u32[]{:S(2)}) %collective-permute-start.8) | collective-permute-done | bytes 262176 | tf_op jit(solution)/shard_map/ppermute | solution.py:18
  94.5 5.1 %collective-permute-done.11 = bf16[512,256]{0,1:T(8,128)(2,1)S(1)} collective-permute-done((bf16[512,256]{0,1:T(8,128)(2,1)S(1)}, bf16[512,256]{0,1:T(8,128)(2,1)S(1)}, u32[]{:S(2)}, u32[]{:S(2)}) %collective-permute-start.11) | collective-permute-done | bytes 262176 | tf_op jit(solution)/shard_map/ppermute | solution.py:18
  100.6 1.7 %collective-permute-start.16 = (bf16[512,256]{0,1:T(8,128)(2,1)S(1)}, bf16[512,256]{0,1:T(8,128)(2,1)S(1)}, u32[]{:S(2)}, u32[]{:S(2)}) collective-permute-start(bf16[512,256]{0,1:T(8,128)(2,1)S(1)} %fusion.16), channel_id=1, source_target_pairs={{0,2},{2,0},{1,3},{3,1},{4,6},{6,4},{5,7},{7,5},{8,10},{10,8},{9,1... | collective-permute-start | bytes 786440 | tf_op jit(solution)/shard_map/ppermute | solution.py:18
  103.3 2.0 %collective-permute-done.13 = bf16[512,256]{0,1:T(8,128)(2,1)S(1)} collective-permute-done((bf16[512,256]{0,1:T(8,128)(2,1)S(1)}, bf16[512,256]{0,1:T(8,128)(2,1)S(1)}, u32[]{:S(2)}, u32[]{:S(2)}) %collective-permute-start.13) | collective-permute-done | bytes 262176 | tf_op jit(solution)/shard_map/ppermute | solution.py:18
  105.7 5.0 %collective-permute-done.16 = bf16[512,256]{0,1:T(8,128)(2,1)S(1)} collective-permute-done((bf16[512,256]{0,1:T(8,128)(2,1)S(1)}, bf16[512,256]{0,1:T(8,128)(2,1)S(1)}, u32[]{:S(2)}, u32[]{:S(2)}) %collective-permute-start.16) | collective-permute-done | bytes 262176 | tf_op jit(solution)/shard_map/ppermute | solution.py:18
  111.2 2.3 %collective-permute-done.18 = bf16[512,256]{0,1:T(8,128)(2,1)S(1)} collective-permute-done((bf16[512,256]{0,1:T(8,128)(2,1)S(1)}, bf16[512,256]{0,1:T(8,128)(2,1)S(1)}, u32[]{:S(2)}, u32[]{:S(2)}) %collective-permute-start.18) | collective-permute-done | bytes 262176 | tf_op jit(solution)/shard_map/ppermute | solution.py:18
  114.0 3.1 %copy.11 = bf16[512,4,512]{2,1,0:T(4,128)(2,1)} copy(bf16[512,4,512]{0,2,1:T(8,128)(2,1)S(1)} %bitcast.22) | data formatting | bytes 4194304 | tf_op jit(solution)/shard_map/reshape | solution.py:91
  (48 shorter events, 19.0 us)
Async XLA Ops:
  2.9 5.0 %copy-start = (s32[1024,512]{1,0:T(8,128)S(1)}, s32[1024,512]{1,0:T(8,128)}, u32[]{:S(2)}) copy-start(s32[1024,512]{1,0:T(8,128)} %param.2) | copy-start | bytes 6291460
  2.9 4.6 %collective-permute-start = (s32[3,512]{1,0:T(4,128)S(1)}, s32[3,512]{1,0:T(4,128)S(1)}, u32[]{:S(2)}, u32[]{:S(2)}) collective-permute-start(s32[3,512]{1,0:T(4,128)S(1)} %pad_add_fusion), channel_id=1, source_target_pairs={{0,2},{2,0},{1,3},{3,1},{4,6},{6,4},{5,7},{7,5},{8,10},{10,8},{9,1... | collective-permute-start | bytes 18440 | tf_op jit(solution)/shard_map/ppermute | solution.py:18
  8.6 58.6 %collective-permute-start.1 = (bf16[1024,512]{1,0:T(8,128)(2,1)S(1)}, bf16[1024,512]{1,0:T(8,128)(2,1)S(1)}, u32[]{:S(2)}, u32[]{:S(2)}) collective-permute-start(bf16[1024,512]{1,0:T(8,128)(2,1)S(1)} %get-tuple-element.8), channel_id=1, source_target_pairs={{0,1},{1,0},{2,3},{3,2},{4,5},{5,4},{6,7},{7,6},{8,9},{9,8},{10,11... | collective-permute-start | bytes 3145736 | tf_op jit(solution)/shard_map/ppermute | solution.py:18
  8.7 29.2 %collective-permute-start.4 = (bf16[1024,256]{1,0:T(8,128)(2,1)S(1)}, bf16[1024,256]{1,0:T(8,128)(2,1)S(1)}, u32[]{:S(2)}, u32[]{:S(2)}) collective-permute-start(bf16[1024,256]{1,0:T(8,128)(2,1)S(1)} %get-tuple-element.15), channel_id=1, source_target_pairs={{4,0},{8,4},{12,8},{5,1},{9,5},{13,9},{6,2},{10,6},{14,10},{7,3},{... | collective-permute-start | bytes 1572872 | tf_op jit(solution)/shard_map/ppermute | solution.py:13
  10.0 29.2 %collective-permute-start.7 = (bf16[1024,256]{1,0:T(8,128)(2,1)S(1)}, bf16[1024,256]{1,0:T(8,128)(2,1)S(1)}, u32[]{:S(2)}, u32[]{:S(2)}) collective-permute-start(bf16[1024,256]{1,0:T(8,128)(2,1)S(1)} %get-tuple-element.14), channel_id=1, source_target_pairs={{4,0},{8,4},{12,8},{5,1},{9,5},{13,9},{6,2},{10,6},{14,10},{7,3},{... | collective-permute-start | bytes 1572872 | tf_op jit(solution)/shard_map/ppermute | solution.py:13
  11.3 25.3 %collective-permute-start.5 = (f32[2,512]{1,0:T(2,128)S(1)}, f32[2,512]{1,0:T(2,128)S(1)}, u32[]{:S(2)}, u32[]{:S(2)}) collective-permute-start(f32[2,512]{1,0:T(2,128)S(1)} %pad_maximum_fusion), channel_id=1, source_target_pairs={{4,0},{8,4},{12,8},{5,1},{9,5},{13,9},{6,2},{10,6},{14,10},{7,3},{... | collective-permute-start | bytes 12296 | tf_op jit(solution)/shard_map/ppermute | solution.py:13
  12.7 27.9 %collective-permute-start.10 = (f32[2,512]{1,0:T(2,128)S(1)}, f32[2,512]{1,0:T(2,128)S(1)}, u32[]{:S(2)}, u32[]{:S(2)}) collective-permute-start(f32[2,512]{1,0:T(2,128)S(1)} %pad_maximum_fusion), channel_id=1, source_target_pairs={{8,0},{12,4},{9,1},{13,5},{10,2},{14,6},{11,3},{15,7},{24,16},{28,... | collective-permute-start | bytes 12296 | tf_op jit(solution)/shard_map/ppermute | solution.py:13
  36.6 7.4 %collective-permute-start.15 = (f32[2,512]{1,0:T(2,128)S(1)}, f32[2,512]{1,0:T(2,128)S(1)}, u32[]{:S(2)}, u32[]{:S(2)}) collective-permute-start(f32[2,512]{1,0:T(2,128)S(1)} %pad_maximum_fusion), channel_id=1, source_target_pairs={{12,0},{13,1},{14,2},{15,3},{28,16},{29,17},{30,18},{31,19}} | collective-permute-start | bytes 12296 | tf_op jit(solution)/shard_map/ppermute | solution.py:13
  37.9 16.7 %collective-permute-start.9 = (bf16[1024,256]{1,0:T(8,128)(2,1)S(1)}, bf16[1024,256]{1,0:T(8,128)(2,1)S(1)}, u32[]{:S(2)}, u32[]{:S(2)}) collective-permute-start(bf16[1024,256]{1,0:T(8,128)(2,1)S(1)} %collective-permute-done.4), channel_id=1, source_target_pairs={{4,0},{8,4},{12,8},{5,1},{9,5},{13,9},{6,2},{10,6},{14,10},{7,3},{... | collective-permute-start | bytes 1572872 | tf_op jit(solution)/shard_map/ppermute | solution.py:13
  39.2 26.7 %collective-permute-start.12 = (bf16[1024,256]{1,0:T(8,128)(2,1)S(1)}, bf16[1024,256]{1,0:T(8,128)(2,1)S(1)}, u32[]{:S(2)}, u32[]{:S(2)}) collective-permute-start(bf16[1024,256]{1,0:T(8,128)(2,1)S(1)} %collective-permute-done.7), channel_id=1, source_target_pairs={{4,0},{8,4},{12,8},{5,1},{9,5},{13,9},{6,2},{10,6},{14,10},{7,3},{... | collective-permute-start | bytes 1572872 | tf_op jit(solution)/shard_map/ppermute | solution.py:13
  54.7 45.5 %collective-permute-start.14 = (bf16[1024,256]{1,0:T(8,128)(2,1)S(1)}, bf16[1024,256]{1,0:T(8,128)(2,1)S(1)}, u32[]{:S(2)}, u32[]{:S(2)}) collective-permute-start(bf16[1024,256]{1,0:T(8,128)(2,1)S(1)} %collective-permute-done.9), channel_id=1, source_target_pairs={{4,0},{8,4},{12,8},{5,1},{9,5},{13,9},{6,2},{10,6},{14,10},{7,3},{... | collective-permute-start | bytes 1572872 | tf_op jit(solution)/shard_map/ppermute | solution.py:13
  65.9 36.5 %collective-permute-start.17 = (bf16[1024,256]{1,0:T(8,128)(2,1)S(1)}, bf16[1024,256]{1,0:T(8,128)(2,1)S(1)}, u32[]{:S(2)}, u32[]{:S(2)}) collective-permute-start(bf16[1024,256]{1,0:T(8,128)(2,1)S(1)} %collective-permute-done.12), channel_id=1, source_target_pairs={{4,0},{8,4},{12,8},{5,1},{9,5},{13,9},{6,2},{10,6},{14,10},{7,3},{... | collective-permute-start | bytes 1572872 | tf_op jit(solution)/shard_map/ppermute | solution.py:13
  67.8 9.3 %collective-permute-start.2 = (bf16[512,256]{0,1:T(8,128)(2,1)S(1)}, bf16[512,256]{0,1:T(8,128)(2,1)S(1)}, u32[]{:S(2)}, u32[]{:S(2)}) collective-permute-start(bf16[512,256]{0,1:T(8,128)(2,1)S(1)} %fusion.4), channel_id=1, source_target_pairs={{0,2},{2,0},{1,3},{3,1},{4,6},{6,4},{5,7},{7,5},{8,10},{10,8},{9,1... | collective-permute-start | bytes 786440 | tf_op jit(solution)/shard_map/ppermute | solution.py:18
  70.1 12.7 %collective-permute-start.3 = (bf16[512,256]{0,1:T(8,128)(2,1)S(1)}, bf16[512,256]{0,1:T(8,128)(2,1)S(1)}, u32[]{:S(2)}, u32[]{:S(2)}) collective-permute-start(bf16[512,256]{0,1:T(8,128)(2,1)S(1)} %fusion.6), channel_id=1, source_target_pairs={{0,2},{2,0},{1,3},{3,1},{4,6},{6,4},{5,7},{7,5},{8,10},{10,8},{9,1... | collective-permute-start | bytes 786440 | tf_op jit(solution)/shard_map/ppermute | solution.py:18
  71.0 17.4 %collective-permute-start.6 = (bf16[512,256]{0,1:T(8,128)(2,1)S(1)}, bf16[512,256]{0,1:T(8,128)(2,1)S(1)}, u32[]{:S(2)}, u32[]{:S(2)}) collective-permute-start(bf16[512,256]{0,1:T(8,128)(2,1)S(1)} %fusion.8), channel_id=1, source_target_pairs={{0,2},{2,0},{1,3},{3,1},{4,6},{6,4},{5,7},{7,5},{8,10},{10,8},{9,1... | collective-permute-start | bytes 786440 | tf_op jit(solution)/shard_map/ppermute | solution.py:18
  77.1 16.9 %collective-permute-start.8 = (bf16[512,256]{0,1:T(8,128)(2,1)S(1)}, bf16[512,256]{0,1:T(8,128)(2,1)S(1)}, u32[]{:S(2)}, u32[]{:S(2)}) collective-permute-start(bf16[512,256]{0,1:T(8,128)(2,1)S(1)} %fusion.10), channel_id=1, source_target_pairs={{0,2},{2,0},{1,3},{3,1},{4,6},{6,4},{5,7},{7,5},{8,10},{10,8},{9,1... | collective-permute-start | bytes 786440 | tf_op jit(solution)/shard_map/ppermute | solution.py:18
  82.8 16.9 %collective-permute-start.11 = (bf16[512,256]{0,1:T(8,128)(2,1)S(1)}, bf16[512,256]{0,1:T(8,128)(2,1)S(1)}, u32[]{:S(2)}, u32[]{:S(2)}) collective-permute-start(bf16[512,256]{0,1:T(8,128)(2,1)S(1)} %fusion.12), channel_id=1, source_target_pairs={{0,2},{2,0},{1,3},{3,1},{4,6},{6,4},{5,7},{7,5},{8,10},{10,8},{9,1... | collective-permute-start | bytes 786440 | tf_op jit(solution)/shard_map/ppermute | solution.py:18
  88.4 16.9 %collective-permute-start.13 = (bf16[512,256]{0,1:T(8,128)(2,1)S(1)}, bf16[512,256]{0,1:T(8,128)(2,1)S(1)}, u32[]{:S(2)}, u32[]{:S(2)}) collective-permute-start(bf16[512,256]{0,1:T(8,128)(2,1)S(1)} %fusion.14), channel_id=1, source_target_pairs={{0,2},{2,0},{1,3},{3,1},{4,6},{6,4},{5,7},{7,5},{8,10},{10,8},{9,1... | collective-permute-start | bytes 786440 | tf_op jit(solution)/shard_map/ppermute | solution.py:18
  100.6 10.1 %collective-permute-start.16 = (bf16[512,256]{0,1:T(8,128)(2,1)S(1)}, bf16[512,256]{0,1:T(8,128)(2,1)S(1)}, u32[]{:S(2)}, u32[]{:S(2)}) collective-permute-start(bf16[512,256]{0,1:T(8,128)(2,1)S(1)} %fusion.16), channel_id=1, source_target_pairs={{0,2},{2,0},{1,3},{3,1},{4,6},{6,4},{5,7},{7,5},{8,10},{10,8},{9,1... | collective-permute-start | bytes 786440 | tf_op jit(solution)/shard_map/ppermute | solution.py:18
  102.9 10.7 %collective-permute-start.18 = (bf16[512,256]{0,1:T(8,128)(2,1)S(1)}, bf16[512,256]{0,1:T(8,128)(2,1)S(1)}, u32[]{:S(2)}, u32[]{:S(2)}) collective-permute-start(bf16[512,256]{0,1:T(8,128)(2,1)S(1)} %fusion.18), channel_id=1, source_target_pairs={{0,2},{2,0},{1,3},{3,1},{4,6},{6,4},{5,7},{7,5},{8,10},{10,8},{9,1... | collective-permute-start | bytes 786440 | tf_op jit(solution)/shard_map/ppermute | solution.py:18

commit v2 on v0

v2 whole, which is shorter than its diff:
```python
import functools

import jax
import jax.numpy as jnp
from jax import lax
from jax.experimental import pallas as pl
from jax.experimental.pallas import tpu as pltpu
from jax.sharding import PartitionSpec as P

BAND = 4
TAIL = 16


def params(mib):
    return pltpu.CompilerParams(vmem_limit_bytes=mib * 1024 * 1024)


def split3(x):
    high = x.astype(jnp.bfloat16)
    rest = x - high.astype(jnp.float32)
    middle = rest.astype(jnp.bfloat16)
    low = (rest - middle.astype(jnp.float32)).astype(jnp.bfloat16)
    return [high, middle, low]


def encode_body(dosages, observed, first, second, sums, held_d, held_o, sems):
    steps = sems.shape[1]
    samples, width = held_d.shape
    rows = samples // steps
    spans = [pl.ds(i * rows, rows) for i in range(steps)]
    copies = [
        [
            pltpu.make_async_copy(src.at[span], dst.at[span], sems.at[j, i])
            for j, (src, dst) in enumerate(((dosages, held_d), (observed, held_o)))
        ]
        for i, span in enumerate(spans)
    ]
    for pair in copies:
        for copy in pair:
            copy.start()
    parts = [jnp.zeros((8, width), jnp.int32)] * 3
    for span, pair in zip(spans, copies):
        for copy in pair:
            copy.wait()
        weights = held_o[span]
        known = held_d[span] * weights
        code = (known + (weights - 1)).astype(jnp.float32).astype(jnp.bfloat16)
        first[span] = code[:, :first.shape[1]]
        second[span] = code[:, first.shape[1]:]
        for i, part in enumerate((weights, known, known * known)):
            parts[i] += jnp.sum(part.reshape(rows // 8, 8, width), axis=0)
    rows_out = [jnp.sum(p, axis=0, keepdims=True) for p in parts]
    sums[...] = jnp.concatenate(rows_out + [jnp.zeros((5, width), jnp.int32)], axis=0)


def call(body, name, shapes, inputs, mib=32, in_hbm=False, scratch=(), events=()):
    place = pltpu.HBM if in_hbm else pltpu.VMEM
    n = len(inputs)
    skip = len(events)

    def with_events(*refs):
        body(*refs[:n], *refs[n + skip:])

    return pl.pallas_call(
        with_events,
        in_specs=[pl.BlockSpec(memory_space=place)] * n
        + [pl.BlockSpec(memory_space=pl.ANY)] * skip,
        out_specs=[pl.BlockSpec(memory_space=pltpu.VMEM)] * len(shapes),
        out_shape=[jax.ShapeDtypeStruct(shape, kind) for shape, kind in shapes],
        scratch_shapes=scratch,
        compiler_params=params(mib),
        cost_estimate=pl.CostEstimate(flops=0, bytes_accessed=0, transcendentals=0),
        name=name,
    )(*inputs, *events)


def encode(dosages, observed):
    samples, width = dosages.shape
    steps = 8
    cut = width // 4
    return call(
        encode_body,
        "encode",
        [
            ((samples, cut), jnp.bfloat16),
            ((samples, width - cut), jnp.bfloat16),
            ((8, width), jnp.int32),
        ],
        [dosages, observed],
        in_hbm=True,
        scratch=[
            pltpu.VMEM((samples, width), jnp.int32),
            pltpu.VMEM((samples, width), jnp.int32),
            pltpu.SemaphoreType.DMA((2, steps)),
        ],
    )


def variant_stats(sums):
    counts = jnp.maximum(sums[0], 1)
    n = counts.astype(jnp.float32)
    pivot = jnp.floor(sums[1].astype(jnp.float32) / n + 0.5).astype(jnp.int32)
    rest = (sums[1] - pivot * counts).astype(jnp.float32)
    squares = (sums[2] - 2 * pivot * sums[1] + pivot * pivot * sums[0]).astype(jnp.float32)
    spreads = (squares - rest * rest / n) / n * 1e-4
    means = pivot.astype(jnp.float32) + rest / n
    return means, lax.rsqrt(spreads + 1e-05) * 0.01


def standardize(code, means, scales):
    value = code.astype(jnp.float32)
    return jnp.where(value >= 0, (value - means) * scales, 0.0).astype(jnp.bfloat16)


def finish_body(first, second, *refs):
    sums_refs, (own, for_up, for_down, last) = refs[:-4], refs[-4:]
    samples, cut = first.shape
    width = own.shape[1]
    sums = [sum(r[i:i + 1] for r in sums_refs) for i in range(3)]
    means, scales = variant_stats(sums)
    own[:, :cut] = standardize(first[...], means[:, :cut], scales[:, :cut])
    rest = standardize(second[...], means[:, cut:], scales[:, cut:])
    own[:, cut:] = rest
    for_up[:samples] = rest
    middle = for_down.shape[1]
    for_down[:samples] = rest[:, :middle]
    last[...] = rest[:, middle:]
    rows = split3(means[:, :cut]) + split3(scales[:, :cut])
    tail = jnp.concatenate(rows + [jnp.zeros((TAIL - len(rows), cut), jnp.bfloat16)], axis=0)
    for ref in (for_up, for_down):
        ref[samples:, :cut] = tail
        ref[samples:, cut:] = jnp.zeros((TAIL, ref.shape[1] - cut), jnp.bfloat16)


def finish(first, second, all_sums, events):
    samples, cut = first.shape
    rest = second.shape[1]
    shapes = [
        (samples, cut + rest),
        (samples + TAIL, rest),
        (samples + TAIL, rest - cut),
        (samples, cut),
    ]
    return call(
        finish_body,
        "finish",
        [(s, jnp.bfloat16) for s in shapes],
        [first, second, *all_sums],
        events=events,
    )


def interleave_body(*refs):
    out = refs[-1]
    for k in range(BAND):
        out[:, k, :] = refs[k][...]


def interleave(panels):
    rows, width = panels[0].shape
    tile = min(rows, 128)
    return pl.pallas_call(
        interleave_body,
        grid=(rows // tile,),
        in_specs=[pl.BlockSpec((tile, width), lambda i: (i, 0))] * BAND,
        out_specs=pl.BlockSpec((tile, BAND, width), lambda i: (i, 0, 0)),
        out_shape=jax.ShapeDtypeStruct((rows, BAND, width), jnp.bfloat16),
        compiler_params=params(32),
        name="interleave",
    )(*panels)


def product(whole, cols, distance):
    n_smp = lax.axis_size("smp")
    owned = whole.shape[1] // n_smp
    place = lax.rem(lax.axis_index("smp") + distance, n_smp)
    left = whole[:, pl.ds(pl.multiple_of(place * owned, owned), owned)]
    out = lax.dot_general(left, cols, (((0,), (0,)), ((), ())), preferred_element_type=jnp.float32)
    return out * (1.0 / (whole.shape[0] * n_smp))


def send_parts(whole, cols, parts):
    for d, ref in enumerate(parts):
        ref[...] = product(whole, cols, d + 1).astype(jnp.bfloat16)


def gather_body(n_sub, *refs):
    held, cols, whole, parts = refs[:n_sub], refs[n_sub], refs[n_sub + 1], refs[n_sub + 2:]
    width = held[0].shape[1]
    me = lax.axis_index("sub")
    for d in range(n_sub):
        place = lax.rem(me - d + n_sub, n_sub)
        whole[:, pl.ds(pl.multiple_of(place * width, width), width)] = held[d][...]
    send_parts(whole, cols[...], parts)


def from_tail(message, samples, cut):
    rows = [message[samples + i:samples + i + 1, :cut].astype(jnp.float32) for i in range(6)]
    return (rows[0] + rows[1]) + rows[2], (rows[3] + rows[4]) + rows[5]


def assemble_body(first, message, *refs):
    *rest, out = refs
    samples, cut = first.shape
    end = message.shape[1] + cut
    out[:, :cut] = standardize(first[...], *from_tail(message, samples, cut))
    out[:, cut:end] = message[:samples]
    for ref in rest:
        out[:, end:end + ref.shape[1]] = ref[...]
        end += ref.shape[1]


def cols_body(n_in, whole, *refs):
    pieces, cols, parts = refs[:n_in], refs[n_in], refs[n_in + 1:]
    assemble_body(*pieces, cols)
    send_parts(whole, cols[...], parts)


def plain_body(whole, cols, *parts):
    send_parts(whole, cols[...], parts)


def total_body(whole, cols, *refs):
    *arrived, out = refs
    total = product(whole, cols[...], 0).astype(jnp.bfloat16).astype(jnp.float32)
    for ref in arrived:
        total = total + ref[...].astype(jnp.float32)
    out[...] = total.astype(jnp.bfloat16)


def fence_body(*refs):
    refs[-1][...] = jnp.zeros_like(refs[-1])


def fence(*events):
    return pl.pallas_call(
        fence_body,
        in_specs=[pl.BlockSpec(memory_space=pl.ANY)] * len(events),
        out_specs=pl.BlockSpec(memory_space=pltpu.VMEM),
        out_shape=jax.ShapeDtypeStruct((8, 128), jnp.float32),
        compiler_params=params(1),
        cost_estimate=pl.CostEstimate(flops=2 * 10**10, bytes_accessed=0, transcendentals=0),
        name="fence",
    )(*events)


def together(*arrays):
    return lax.optimization_barrier(arrays)


def on_device(dosages, observed):
    n_var = lax.axis_size("var")
    n_smp = lax.axis_size("smp")
    n_sub = lax.axis_size("sub")
    samples, width = dosages.shape
    rows_owned = width * n_sub // n_smp

    def along(x, distance, keep):
        route = [
            (i, i + distance) for i in range(n_var) if 0 <= i + distance < n_var and keep(i)
        ]
        return lax.ppermute(x, "var", route)

    def down(x):
        return along(x, -1, lambda i: True)

    def down_again(x):
        return along(x, -1, lambda i: i + 1 < n_var)

    def up_two(x):
        return along(x, 2, lambda i: i + 3 < n_var)

    def holds_three(i):
        return i >= 2 and i + 1 < n_var

    def down_two(x):
        return along(x, -2, holds_three)

    def swapped(x, axis, distance, keep=None):
        n = lax.axis_size(axis)
        if keep is None:
            return lax.ppermute(x, axis, [(i, (i + distance) % n) for i in range(n)])
        route = [
            (v * n + i, v * n + (i + distance) % n)
            for v in range(n_var)
            if keep(v)
            for i in range(n)
        ]
        return lax.ppermute(x, ("var", axis), route)

    def others_of(part):
        return [swapped(part, "sub", d) for d in range(1, n_sub)]

    def sent(parts, keep=None):
        return [swapped(p, "smp", d + 1, keep) for d, p in enumerate(parts)]

    def part_shapes(columns):
        return [((rows_owned, columns), jnp.bfloat16)] * (n_smp - 1)

    def gather(part, others, cols, name, events):
        block = ((samples, width * n_sub), jnp.bfloat16)
        body = functools.partial(gather_body, n_sub)
        shapes = [block] + part_shapes(width)
        whole, *parts = call(body, name, shapes, [part, *others, cols], events=events)
        return whole, parts

    def columns(whole, pieces, name, events):
        span = sum(p.shape[1] for p in pieces)
        body = functools.partial(cols_body, len(pieces))
        shapes = [((samples, span), jnp.bfloat16)] + part_shapes(span)
        cols, *parts = call(body, name, shapes, [whole, *pieces], events=events)
        return cols, parts

    def total(whole, cols, arrived, name, events):
        shape = ((rows_owned, cols.shape[1]), jnp.bfloat16)
        return call(total_body, name, [shape], [whole, cols, *arrived], events=events)[0]

    cut = width // 4

    first, second, sums_own = encode(dosages, observed)
    near_a, up_a = down(first), up_two(first)
    arrived_sums = [swapped(sums_own, "smp", d) for d in range(1, n_smp)]
    step = fence(first)
    own, for_up, for_down, last = finish(first, second, [sums_own] + arrived_sums, [step])
    near_b, up_b = down(for_down), up_two(for_up)
    others = others_of(own)
    step = fence(own)

    whole, part0 = gather(own, others, own, "gather0", [near_a, up_a, step])
    last, near_a, *part0 = together(last, near_a, *part0)
    near_c = down(last)
    far_a = down_again(near_a)
    got0 = sent(part0)
    step = fence(whole, *part0)
    near_b, step = together(near_b, step)
    far_b = down_again(near_b)
    step = fence(near_b, step)
    near_c, step = together(near_c, step)
    far_c = down_again(near_c)

    (rows3,) = call(
        assemble_body,
        "rows3",
        [((samples, width), jnp.bfloat16)],
        [up_a, up_b],
        events=[near_c, step],
    )
    others3 = others_of(rows3)
    step = fence(rows3)
    cols1, part1 = columns(whole, [near_a, near_b, near_c], "columns1", [step, *got0])
    got1 = sent(part1, lambda v: not holds_three(v) and v + 1 < n_var)
    step = fence(cols1)
    panel0 = total(whole, own, got0, "total0", [step])
    whole3, part3 = gather(rows3, others3, cols1, "gather3", [panel0])
    got3 = sent(part3, holds_three)
    *part1, far_a, whole3 = together(*part1, far_a, whole3)
    got1_late = sent(part1, holds_three)
    step = fence(far_a, whole3)

    cols2, part2 = columns(whole, [far_a, far_b], "columns2", [step, *got1])
    got2 = sent(part2, lambda v: v + 2 < n_var)
    step = fence(cols2)
    panel3 = total(whole3, cols1, got3, "total3", [step])
    step = fence(panel3)
    panel3 = down_two(panel3)
    part2_c = call(plain_body, "last2", part_shapes(cut), [whole, far_c], events=[step])
    got2_c = sent(part2_c, lambda v: v + 2 < n_var)
    step = fence(*part2_c)
    panel2_ab = total(whole, cols2, got2, "total2", [step])
    panel2_c = total(whole, far_c, got2_c, "total2c", [panel2_ab])
    panel1 = total(whole, cols1, got1 + got1_late, "total1", [panel2_c])
    panel2 = jnp.concatenate([panel2_ab, panel2_c], axis=1)
    return interleave([panel0, panel1, panel2, panel3])


def solution(mesh):
    in_specs = (P("smp", ("grp", "var", "sub")), P("smp", ("grp", "var", "sub")))
    out_specs = P(("grp", "var", "smp"), None, "sub")
    return jax.shard_map(
        on_device, mesh=mesh, in_specs=in_specs, out_specs=out_specs, check_vma=False
    )
```

time: 357 us -> 89.7 us (0.25)
  waiting for transfers between devices: 297 us -> 40.9 us
  starting transfers between devices: 3.91 us -> 31.9 us
  between operations: 14.1 us -> 0.36 us
  Pallas kernels: 0 us -> 12.9 us
  local copies, waits for them, and re-layouts: 15.5 us -> 3.18 us
  blocking collectives: 10.8 us -> 0 us
  other arithmetic: 8.1 us -> 0.05 us
  matrix products: 6.67 us -> 0 us
    unnamed x3 -> x0, waiting for transfers between devices: 150 us -> none
    ppermute x3 -> x18, waiting for transfers between devices: 135 us -> 40.9 us  [the longest x9 32.4 us: along(): return lax.ppermute(x, 'var', route)]
    ppermute x3 -> x18, starting transfers between devices: 3.86 us -> 31.9 us  [the longest x9 18 us: along(): return lax.ppermute(x, 'var', route)]
    pallas_call x0 -> x24, Pallas kernels: none -> 12.9 us  [the longest x13 9.68 us: call(): pl.pallas_call(with_events, in_specs=[pl.BlockSpec(memory_space=place)] *...]
    all_gather x1 -> x0, waiting for transfers between devices: 12.5 us -> none  [on_device(): whole_block = lax.all_gather(own_cols, 'sub', axis=1, tiled=True)]
    psum x2 -> x0, blocking collectives: 10.8 us -> none  [the longest x1 5.84 us: on_device(): lax.psum((jnp.sum(weights, axis=0), jnp.sum(weights * values, axis=0)), '...]
    convert_element_type x1 -> x0, local copies, waits for them, and re-layouts: 7.82 us -> none  [on_device(): return lax.psum_scatter((product * factor).reshape(rows_owned * lax.axis_...]
    dot_general x1 -> x0, matrix products: 6.67 us -> none  [on_device(): lax.dot_general(whole_block, stacked, (((0,), (0,)), ((), ())), preferred...]
  transfers between devices with their start and end apart: 5 -> 18, of which waited for: 4 -> 8; matrix products, arithmetic and copies ran while one was open for 1% -> 0% of each run, Pallas kernels for 0% -> 10%
where the time goes in v2:
time: 89.7 us; the launch traced here: 89.3 us
  waiting for transfers between devices  40.9 us (46%)
  starting transfers between devices  31.9 us (36%)
  Pallas kernels  12.9 us (14%)
  local copies, waits for them, and re-layouts  3.18 us (4%)
    ppermute x9, waiting for transfers between devices, along(): return lax.ppermute(x, 'var', route)  32.4 us
    ppermute x9, starting transfers between devices, along(): return lax.ppermute(x, 'var', route)  18 us
    ppermute x5, starting transfers between devices, swapped(): return lax.ppermute(x, ('var', axis), route)  10.6 us
    pallas_call x13, Pallas kernels, call(): pl.pallas_call(with_events, in_specs=[pl.BlockSpec(memory_space=place)] *...  9.68 us
    ppermute x5, waiting for transfers between devices, swapped(): return lax.ppermute(x, ('var', axis), route)  6.31 us
    ppermute x4, starting transfers between devices, swapped(): return lax.ppermute(x, axis, [(i, (i + distance) % n) for i in range(n)])  3.27 us
    pallas_call x1, Pallas kernels, interleave(): pl.pallas_call(interleave_body, grid=(rows // tile,), in_specs=[pl.BlockS...  3.19 us
    unnamed x4, local copies, waits for them, and re-layouts  3.18 us
  transfers between devices with their start and end apart: 18, of which 8 were waited for; matrix products, arithmetic and copies ran while one was open for 0% of the time, Pallas kernels for 10%

profile of v2, /device:TPU:0, one launch (start us, length us, event | category | flops | bytes accessed | tf_op | source)
XLA Modules:
  0.0 89.3 jit_solution(15525795517343001377)
XLA Ops:
  0.0 1.6 %copy-done = s32[1024,512]{1,0:T(8,128)S(1)} copy-done((s32[1024,512]{1,0:T(8,128)S(1)}, s32[1024,512]{1,0:T(8,128)}, u32[]{:S(2)}) %copy-start) | copy-done | bytes 2097176
  1.6 1.6 %copy-done.1 = s32[1024,512]{1,0:T(8,128)S(1)} copy-done((s32[1024,512]{1,0:T(8,128)S(1)}, s32[1024,512]{1,0:T(8,128)}, u32[]{:S(2)}) %copy-start.1) | copy-done | bytes 2097176
  3.2 1.1 %encode.1 = (bf16[1024,128]{1,0:T(8,128)(2,1)S(1)}, bf16[1024,384]{1,0:T(8,128)(2,1)S(1)}, s32[8,512]{1,0:T(8,128)S(1)}) custom-call(s32[1024,512]{1,0:T(8,128)S(1)} %copy-done, s32[1024,512]{1,0:T(8,128)S(1)} %copy-done.1), custom_call_target="tpu_custom_call" | custom-call | tf_op jit(solution)/shard_map/encode/pallas_call | solution.py:64
  4.3 1.3 %collective-permute-start.2 = (bf16[1024,128]{1,0:T(8,128)(2,1)S(1)}, bf16[1024,128]{1,0:T(8,128)(2,1)S(1)}, u32[]{:S(2)}, u32[]{:S(2)}) collective-permute-start(bf16[1024,128]{1,0:T(8,128)(2,1)S(1)} %get-tuple-element.30.refs_0_), channel_id=1, source_target_pairs={{4,0},{8,4},{12,8},{5,1},{9,5},{13,9},{6,2},{10,6},{14,10},{7,3},{... | collective-permute-start | bytes 786440 | tf_op jit(solution)/shard_map/ppermute | solution.py:262
  5.6 7.0 %collective-permute-start.3 = (bf16[1024,128]{1,0:T(8,128)(2,1)S(1)}, bf16[1024,128]{1,0:T(8,128)(2,1)S(1)}, u32[]{:S(2)}, u32[]{:S(2)}) collective-permute-start(bf16[1024,128]{1,0:T(8,128)(2,1)S(1)} %get-tuple-element.30.refs_0_), channel_id=1, source_target_pairs={{0,8},{1,9},{2,10},{3,11},{16,24},{17,25},{18,26},{19,27}} | collective-permute-start | bytes 786440 | tf_op jit(solution)/shard_map/ppermute | solution.py:262
  12.6 1.6 %collective-permute-start = (s32[8,512]{1,0:T(8,128)S(1)}, s32[8,512]{1,0:T(8,128)S(1)}, u32[]{:S(2)}, u32[]{:S(2)}) collective-permute-start(s32[8,512]{1,0:T(8,128)S(1)} %get-tuple-element.32.refs_2_), channel_id=1, source_target_pairs={{0,2},{2,0},{1,3},{3,1},{4,6},{6,4},{5,7},{7,5},{8,10},{10,8},{9,1... | collective-permute-start | bytes 49160 | tf_op jit(solution)/shard_map/ppermute | solution.py:282
  14.2 2.2 %collective-permute-done.refs_3_ = s32[8,512]{1,0:T(8,128)S(1)} collective-permute-done((s32[8,512]{1,0:T(8,128)S(1)}, s32[8,512]{1,0:T(8,128)S(1)}, u32[]{:S(2)}, u32[]{:S(2)}) %collective-permute-start) | collective-permute-done | bytes 16416 | tf_op jit(solution)/shard_map/ppermute | solution.py:282
  17.1 1.3 %collective-permute-start.5 = (bf16[1040,256]{1,0:T(8,128)(2,1)S(1)}, bf16[1040,256]{1,0:T(8,128)(2,1)S(1)}, u32[]{:S(2)}, u32[]{:S(2)}) collective-permute-start(bf16[1040,256]{1,0:T(8,128)(2,1)S(1)} %get-tuple-element.39), channel_id=1, source_target_pairs={{4,0},{8,4},{12,8},{5,1},{9,5},{13,9},{6,2},{10,6},{14,10},{7,3},{... | collective-permute-start | bytes 1597448 | tf_op jit(solution)/shard_map/ppermute | solution.py:262
  18.4 2.0 %collective-permute-start.7 = (bf16[1040,384]{1,0:T(8,128)(2,1)S(1)}, bf16[1040,384]{1,0:T(8,128)(2,1)S(1)}, u32[]{:S(2)}, u32[]{:S(2)}) collective-permute-start(bf16[1040,384]{1,0:T(8,128)(2,1)S(1)} %get-tuple-element.44), channel_id=1, source_target_pairs={{0,8},{1,9},{2,10},{3,11},{16,24},{17,25},{18,26},{19,27}} | collective-permute-start | bytes 2396168 | tf_op jit(solution)/shard_map/ppermute | solution.py:262
  21.4 1.6 %collective-permute-start.4 = (bf16[512,512]{1,0:T(8,128)(2,1)S(1)}, bf16[512,512]{1,0:T(8,128)(2,1)S(1)}, u32[]{:S(2)}, u32[]{:S(2)}) collective-permute-start(bf16[512,512]{1,0:T(8,128)(2,1)S(1)} %get-tuple-element.37.refs_1_), channel_id=1, source_target_pairs={{0,2},{2,0},{1,3},{3,1},{4,6},{6,4},{5,7},{7,5},{8,10},{10,8},{9,1... | collective-permute-start | bytes 1572872 | tf_op jit(solution)/shard_map/ppermute | solution.py:282
  22.9 10.5 %collective-permute-done.5.refs_0_.refs_2_ = bf16[1040,256]{1,0:T(8,128)(2,1)S(1)} collective-permute-done((bf16[1040,256]{1,0:T(8,128)(2,1)S(1)}, bf16[1040,256]{1,0:T(8,128)(2,1)S(1)}, u32[]{:S(2)}, u32[]{:S(2)}) %collective-permute-start.5) | collective-permute-done | bytes 532512 | tf_op jit(solution)/shard_map/ppermute | solution.py:262
  33.5 1.3 %collective-permute-start.6 = (bf16[1024,128]{1,0:T(8,128)(2,1)S(1)}, bf16[1024,128]{1,0:T(8,128)(2,1)S(1)}, u32[]{:S(2)}, u32[]{:S(2)}) collective-permute-start(bf16[1024,128]{1,0:T(8,128)(2,1)S(1)} %get-tuple-element.41), channel_id=1, source_target_pairs={{4,0},{8,4},{12,8},{5,1},{9,5},{13,9},{6,2},{10,6},{14,10},{7,3},{... | collective-permute-start | bytes 786440 | tf_op jit(solution)/shard_map/ppermute | solution.py:262
  34.7 1.3 %collective-permute-start.14 = (bf16[1040,256]{1,0:T(8,128)(2,1)S(1)}, bf16[1040,256]{1,0:T(8,128)(2,1)S(1)}, u32[]{:S(2)}, u32[]{:S(2)}) collective-permute-start(bf16[1040,256]{1,0:T(8,128)(2,1)S(1)} %collective-permute-done.5.refs_0_.refs_2_), channel_id=1, source_target_pairs={{4,0},{8,4},{5,1},{9,5},{6,2},{10,6},{7,3},{11,7},{20,16},{24,20},... | collective-permute-start | bytes 1597448 | tf_op jit(solution)/shard_map/ppermute | solution.py:262
  36.1 1.3 %collective-permute-start.9 = (bf16[1024,128]{1,0:T(8,128)(2,1)S(1)}, bf16[1024,128]{1,0:T(8,128)(2,1)S(1)}, u32[]{:S(2)}, u32[]{:S(2)}) collective-permute-start(bf16[1024,128]{1,0:T(8,128)(2,1)S(1)} %collective-permute-done.2.refs_3_.refs_1_), channel_id=1, source_target_pairs={{4,0},{8,4},{5,1},{9,5},{6,2},{10,6},{7,3},{11,7},{20,16},{24,20},... | collective-permute-start | bytes 786440 | tf_op jit(solution)/shard_map/ppermute | solution.py:262
  37.4 7.2 %collective-permute-done.6.refs_2_.refs_3_ = bf16[1024,128]{1,0:T(8,128)(2,1)S(1)} collective-permute-done((bf16[1024,128]{1,0:T(8,128)(2,1)S(1)}, bf16[1024,128]{1,0:T(8,128)(2,1)S(1)}, u32[]{:S(2)}, u32[]{:S(2)}) %collective-permute-start.6) | collective-permute-done | bytes 262176 | tf_op jit(solution)/shard_map/ppermute | solution.py:262
  44.8 1.3 %collective-permute-start.12 = (bf16[1024,128]{1,0:T(8,128)(2,1)S(1)}, bf16[1024,128]{1,0:T(8,128)(2,1)S(1)}, u32[]{:S(2)}, u32[]{:S(2)}) collective-permute-start(bf16[1024,128]{1,0:T(8,128)(2,1)S(1)} %collective-permute-done.6.refs_2_.refs_3_), channel_id=1, source_target_pairs={{4,0},{8,4},{5,1},{9,5},{6,2},{10,6},{7,3},{11,7},{20,16},{24,20},... | collective-permute-start | bytes 786440 | tf_op jit(solution)/shard_map/ppermute | solution.py:262
  47.0 3.4 %collective-permute-start.8 = (bf16[512,512]{1,0:T(8,128)(2,1)S(1)}, bf16[512,512]{1,0:T(8,128)(2,1)S(1)}, u32[]{:S(2)}, u32[]{:S(2)}) collective-permute-start(bf16[512,512]{1,0:T(8,128)(2,1)S(1)} %get-tuple-element.49), channel_id=1, source_target_pairs={{0,2},{2,0},{4,6},{6,4},{1,3},{3,1},{5,7},{7,5},{16,18},{18,16},{2... | collective-permute-start | bytes 1572872 | tf_op jit(solution)/shard_map/ppermute | solution.py:289
  52.2 9.4 %collective-permute-done.9.refs_0_.refs_1_ = bf16[1024,128]{1,0:T(8,128)(2,1)S(1)} collective-permute-done((bf16[1024,128]{1,0:T(8,128)(2,1)S(1)}, bf16[1024,128]{1,0:T(8,128)(2,1)S(1)}, u32[]{:S(2)}, u32[]{:S(2)}) %collective-permute-start.9) | collective-permute-done | bytes 262176 | tf_op jit(solution)/shard_map/ppermute | solution.py:262
  64.0 3.4 %collective-permute-start.16 = (bf16[512,384]{1,0:T(8,128)(2,1)S(1)}, bf16[512,384]{1,0:T(8,128)(2,1)S(1)}, u32[]{:S(2)}, u32[]{:S(2)}) collective-permute-start(bf16[512,384]{1,0:T(8,128)(2,1)S(1)} %get-tuple-element.54), channel_id=1, source_target_pairs={{0,2},{2,0},{4,6},{6,4},{1,3},{3,1},{5,7},{7,5},{16,18},{18,16},{2... | collective-permute-start | bytes 1179656 | tf_op jit(solution)/shard_map/ppermute | solution.py:289
  68.9 1.3 %collective-permute-start.17 = (bf16[512,512]{1,0:T(8,128)(2,1)S(1)}, bf16[512,512]{1,0:T(8,128)(2,1)S(1)}, u32[]{:S(2)}, u32[]{:S(2)}) collective-permute-start(bf16[512,512]{1,0:T(8,128)(2,1)S(1)} %total3.1.refs_0_), channel_id=1, source_target_pairs={{8,0},{9,1},{10,2},{11,3},{24,16},{25,17},{26,18},{27,19}} | collective-permute-start | bytes 1572872 | tf_op jit(solution)/shard_map/ppermute | solution.py:262
  70.7 2.4 %collective-permute-start.15 = (bf16[512,128]{1,0:T(8,128)(2,1)S(1)}, bf16[512,128]{1,0:T(8,128)(2,1)S(1)}, u32[]{:S(2)}, u32[]{:S(2)}) collective-permute-start(bf16[512,128]{1,0:T(8,128)(2,1)S(1)} %last2.1.refs_0_), channel_id=1, source_target_pairs={{0,2},{2,0},{4,6},{6,4},{1,3},{3,1},{5,7},{7,5},{16,18},{18,16},{2... | collective-permute-start | bytes 393224 | tf_op jit(solution)/shard_map/ppermute | solution.py:289
  73.2 4.7 %collective-permute-done.16.refs_2_ = bf16[512,384]{1,0:T(8,128)(2,1)S(1)} collective-permute-done((bf16[512,384]{1,0:T(8,128)(2,1)S(1)}, bf16[512,384]{1,0:T(8,128)(2,1)S(1)}, u32[]{:S(2)}, u32[]{:S(2)}) %collective-permute-start.16) | collective-permute-done | bytes 393248 | tf_op jit(solution)/shard_map/ppermute | solution.py:289
  80.9 5.2 %collective-permute-done.17.refs_3_ = bf16[512,512]{1,0:T(8,128)(2,1)S(1)} collective-permute-done((bf16[512,512]{1,0:T(8,128)(2,1)S(1)}, bf16[512,512]{1,0:T(8,128)(2,1)S(1)}, u32[]{:S(2)}, u32[]{:S(2)}) %collective-permute-start.17) | collective-permute-done | bytes 524320 | tf_op jit(solution)/shard_map/ppermute | solution.py:262
  86.1 3.2 %interleave.1 = bf16[512,4,512]{2,1,0:T(4,128)(2,1)} custom-call(bf16[512,512]{1,0:T(8,128)(2,1)S(1)} %total0.1.refs_3_.refs_0_, bf16[512,512]{1,0:T(8,128)(2,1)S(1)} %total1.1.refs_1_, bf16[512,512]{1,0:T(8,128)(2,1)S(1)} %pad_maximum_fusion.refs_2_, bf16[512,512]{1,0:T(8,128)(2,1)S(1)} %collective-permute-done.17.refs_3_), custom_call_target="tpu_custom_call" | custom-call | tf_op jit(solution)/shard_map/interleave/pallas_call | solution.py:162
  (41 shorter events, 11.8 us)
Async XLA Ops:
  0.0 1.6 %copy-start = (s32[1024,512]{1,0:T(8,128)S(1)}, s32[1024,512]{1,0:T(8,128)}, u32[]{:S(2)}) copy-start(s32[1024,512]{1,0:T(8,128)} %refs_0_.1) | copy-start | bytes 6291460
  1.6 1.6 %copy-start.1 = (s32[1024,512]{1,0:T(8,128)S(1)}, s32[1024,512]{1,0:T(8,128)}, u32[]{:S(2)}) copy-start(s32[1024,512]{1,0:T(8,128)} %refs_1_.1) | copy-start | bytes 6291460
  4.3 16.1 %collective-permute-start.2 = (bf16[1024,128]{1,0:T(8,128)(2,1)S(1)}, bf16[1024,128]{1,0:T(8,128)(2,1)S(1)}, u32[]{:S(2)}, u32[]{:S(2)}) collective-permute-start(bf16[1024,128]{1,0:T(8,128)(2,1)S(1)} %get-tuple-element.30.refs_0_), channel_id=1, source_target_pairs={{4,0},{8,4},{12,8},{5,1},{9,5},{13,9},{6,2},{10,6},{14,10},{7,3},{... | collective-permute-start | bytes 786440 | tf_op jit(solution)/shard_map/ppermute | solution.py:262
  5.6 14.8 %collective-permute-start.3 = (bf16[1024,128]{1,0:T(8,128)(2,1)S(1)}, bf16[1024,128]{1,0:T(8,128)(2,1)S(1)}, u32[]{:S(2)}, u32[]{:S(2)}) collective-permute-start(bf16[1024,128]{1,0:T(8,128)(2,1)S(1)} %get-tuple-element.30.refs_0_), channel_id=1, source_target_pairs={{0,8},{1,9},{2,10},{3,11},{16,24},{17,25},{18,26},{19,27}} | collective-permute-start | bytes 786440 | tf_op jit(solution)/shard_map/ppermute | solution.py:262
  12.6 3.8 %collective-permute-start = (s32[8,512]{1,0:T(8,128)S(1)}, s32[8,512]{1,0:T(8,128)S(1)}, u32[]{:S(2)}, u32[]{:S(2)}) collective-permute-start(s32[8,512]{1,0:T(8,128)S(1)} %get-tuple-element.32.refs_2_), channel_id=1, source_target_pairs={{0,2},{2,0},{1,3},{3,1},{4,6},{6,4},{5,7},{7,5},{8,10},{10,8},{9,1... | collective-permute-start | bytes 49160 | tf_op jit(solution)/shard_map/ppermute | solution.py:282
  17.0 3.4 %collective-permute-start.1 = (bf16[1024,512]{1,0:T(8,128)(2,1)S(1)}, bf16[1024,512]{1,0:T(8,128)(2,1)S(1)}, u32[]{:S(2)}, u32[]{:S(2)}) collective-permute-start(bf16[1024,512]{1,0:T(8,128)(2,1)S(1)} %get-tuple-element.33.refs_0_.refs_2_.refs_1_), channel_id=1, source_target_pairs={{0,1},{1,0},{2,3},{3,2},{4,5},{5,4},{6,7},{7,6},{8,9},{9,8},{10,11... | collective-permute-start | bytes 3145736 | tf_op jit(solution)/shard_map/ppermute | solution.py:282
  17.1 16.4 %collective-permute-start.5 = (bf16[1040,256]{1,0:T(8,128)(2,1)S(1)}, bf16[1040,256]{1,0:T(8,128)(2,1)S(1)}, u32[]{:S(2)}, u32[]{:S(2)}) collective-permute-start(bf16[1040,256]{1,0:T(8,128)(2,1)S(1)} %get-tuple-element.39), channel_id=1, source_target_pairs={{4,0},{8,4},{12,8},{5,1},{9,5},{13,9},{6,2},{10,6},{14,10},{7,3},{... | collective-permute-start | bytes 1597448 | tf_op jit(solution)/shard_map/ppermute | solution.py:262
  18.4 26.2 %collective-permute-start.7 = (bf16[1040,384]{1,0:T(8,128)(2,1)S(1)}, bf16[1040,384]{1,0:T(8,128)(2,1)S(1)}, u32[]{:S(2)}, u32[]{:S(2)}) collective-permute-start(bf16[1040,384]{1,0:T(8,128)(2,1)S(1)} %get-tuple-element.44), channel_id=1, source_target_pairs={{0,8},{1,9},{2,10},{3,11},{16,24},{17,25},{18,26},{19,27}} | collective-permute-start | bytes 2396168 | tf_op jit(solution)/shard_map/ppermute | solution.py:262
  21.4 24.7 %collective-permute-start.4 = (bf16[512,512]{1,0:T(8,128)(2,1)S(1)}, bf16[512,512]{1,0:T(8,128)(2,1)S(1)}, u32[]{:S(2)}, u32[]{:S(2)}) collective-permute-start(bf16[512,512]{1,0:T(8,128)(2,1)S(1)} %get-tuple-element.37.refs_1_), channel_id=1, source_target_pairs={{0,2},{2,0},{1,3},{3,1},{4,6},{6,4},{5,7},{7,5},{8,10},{10,8},{9,1... | collective-permute-start | bytes 1572872 | tf_op jit(solution)/shard_map/ppermute | solution.py:282
  33.5 11.1 %collective-permute-start.6 = (bf16[1024,128]{1,0:T(8,128)(2,1)S(1)}, bf16[1024,128]{1,0:T(8,128)(2,1)S(1)}, u32[]{:S(2)}, u32[]{:S(2)}) collective-permute-start(bf16[1024,128]{1,0:T(8,128)(2,1)S(1)} %get-tuple-element.41), channel_id=1, source_target_pairs={{4,0},{8,4},{12,8},{5,1},{9,5},{13,9},{6,2},{10,6},{14,10},{7,3},{... | collective-permute-start | bytes 786440 | tf_op jit(solution)/shard_map/ppermute | solution.py:262
  34.7 27.5 %collective-permute-start.14 = (bf16[1040,256]{1,0:T(8,128)(2,1)S(1)}, bf16[1040,256]{1,0:T(8,128)(2,1)S(1)}, u32[]{:S(2)}, u32[]{:S(2)}) collective-permute-start(bf16[1040,256]{1,0:T(8,128)(2,1)S(1)} %collective-permute-done.5.refs_0_.refs_2_), channel_id=1, source_target_pairs={{4,0},{8,4},{5,1},{9,5},{6,2},{10,6},{7,3},{11,7},{20,16},{24,20},... | collective-permute-start | bytes 1597448 | tf_op jit(solution)/shard_map/ppermute | solution.py:262
  36.1 25.5 %collective-permute-start.9 = (bf16[1024,128]{1,0:T(8,128)(2,1)S(1)}, bf16[1024,128]{1,0:T(8,128)(2,1)S(1)}, u32[]{:S(2)}, u32[]{:S(2)}) collective-permute-start(bf16[1024,128]{1,0:T(8,128)(2,1)S(1)} %collective-permute-done.2.refs_3_.refs_1_), channel_id=1, source_target_pairs={{4,0},{8,4},{5,1},{9,5},{6,2},{10,6},{7,3},{11,7},{20,16},{24,20},... | collective-permute-start | bytes 786440 | tf_op jit(solution)/shard_map/ppermute | solution.py:262
  44.7 6.4 %collective-permute-start.10 = (bf16[1024,512]{1,0:T(8,128)(2,1)S(1)}, bf16[1024,512]{1,0:T(8,128)(2,1)S(1)}, u32[]{:S(2)}, u32[]{:S(2)}) collective-permute-start(bf16[1024,512]{1,0:T(8,128)(2,1)S(1)} %rows3.1.refs_0_), channel_id=1, source_target_pairs={{0,1},{1,0},{2,3},{3,2},{4,5},{5,4},{6,7},{7,6},{8,9},{9,8},{10,11... | collective-permute-start | bytes 3145736 | tf_op jit(solution)/shard_map/ppermute | solution.py:282
  44.8 25.4 %collective-permute-start.12 = (bf16[1024,128]{1,0:T(8,128)(2,1)S(1)}, bf16[1024,128]{1,0:T(8,128)(2,1)S(1)}, u32[]{:S(2)}, u32[]{:S(2)}) collective-permute-start(bf16[1024,128]{1,0:T(8,128)(2,1)S(1)} %collective-permute-done.6.refs_2_.refs_3_), channel_id=1, source_target_pairs={{4,0},{8,4},{5,1},{9,5},{6,2},{10,6},{7,3},{11,7},{20,16},{24,20},... | collective-permute-start | bytes 786440 | tf_op jit(solution)/shard_map/ppermute | solution.py:262
  47.0 16.2 %collective-permute-start.8 = (bf16[512,512]{1,0:T(8,128)(2,1)S(1)}, bf16[512,512]{1,0:T(8,128)(2,1)S(1)}, u32[]{:S(2)}, u32[]{:S(2)}) collective-permute-start(bf16[512,512]{1,0:T(8,128)(2,1)S(1)} %get-tuple-element.49), channel_id=1, source_target_pairs={{0,2},{2,0},{4,6},{6,4},{1,3},{3,1},{5,7},{7,5},{16,18},{18,16},{2... | collective-permute-start | bytes 1572872 | tf_op jit(solution)/shard_map/ppermute | solution.py:289
  61.6 6.5 %collective-permute-start.13 = (bf16[512,512]{1,0:T(8,128)(2,1)S(1)}, bf16[512,512]{1,0:T(8,128)(2,1)S(1)}, u32[]{:S(2)}, u32[]{:S(2)}) collective-permute-start(bf16[512,512]{1,0:T(8,128)(2,1)S(1)} %get-tuple-element.51), channel_id=1, source_target_pairs={{8,10},{10,8},{9,11},{11,9},{24,26},{26,24},{25,27},{27,25}} | collective-permute-start | bytes 1572872 | tf_op jit(solution)/shard_map/ppermute | solution.py:289
  64.0 13.9 %collective-permute-start.16 = (bf16[512,384]{1,0:T(8,128)(2,1)S(1)}, bf16[512,384]{1,0:T(8,128)(2,1)S(1)}, u32[]{:S(2)}, u32[]{:S(2)}) collective-permute-start(bf16[512,384]{1,0:T(8,128)(2,1)S(1)} %get-tuple-element.54), channel_id=1, source_target_pairs={{0,2},{2,0},{4,6},{6,4},{1,3},{3,1},{5,7},{7,5},{16,18},{18,16},{2... | collective-permute-start | bytes 1179656 | tf_op jit(solution)/shard_map/ppermute | solution.py:289
  67.4 12.6 %collective-permute-start.11 = (bf16[512,512]{1,0:T(8,128)(2,1)S(1)}, bf16[512,512]{1,0:T(8,128)(2,1)S(1)}, u32[]{:S(2)}, u32[]{:S(2)}) collective-permute-start(bf16[512,512]{1,0:T(8,128)(2,1)S(1)} %get-tuple-element.49), channel_id=1, source_target_pairs={{8,10},{10,8},{9,11},{11,9},{24,26},{26,24},{25,27},{27,25}} | collective-permute-start | bytes 1572872 | tf_op jit(solution)/shard_map/ppermute | solution.py:289
  68.9 17.2 %collective-permute-start.17 = (bf16[512,512]{1,0:T(8,128)(2,1)S(1)}, bf16[512,512]{1,0:T(8,128)(2,1)S(1)}, u32[]{:S(2)}, u32[]{:S(2)}) collective-permute-start(bf16[512,512]{1,0:T(8,128)(2,1)S(1)} %total3.1.refs_0_), channel_id=1, source_target_pairs={{8,0},{9,1},{10,2},{11,3},{24,16},{25,17},{26,18},{27,19}} | collective-permute-start | bytes 1572872 | tf_op jit(solution)/shard_map/ppermute | solution.py:262
  70.7 8.7 %collective-permute-start.15 = (bf16[512,128]{1,0:T(8,128)(2,1)S(1)}, bf16[512,128]{1,0:T(8,128)(2,1)S(1)}, u32[]{:S(2)}, u32[]{:S(2)}) collective-permute-start(bf16[512,128]{1,0:T(8,128)(2,1)S(1)} %last2.1.refs_0_), channel_id=1, source_target_pairs={{0,2},{2,0},{4,6},{6,4},{1,3},{3,1},{5,7},{7,5},{16,18},{18,16},{2... | collective-permute-start | bytes 393224 | tf_op jit(solution)/shard_map/ppermute | solution.py:289

commit v3 on v2

--- a/solution.py
+++ b/solution.py
@@ -77,7 +77,7 @@
 def encode(dosages, observed):
     samples, width = dosages.shape
     steps = 8
-    cut = width // 4
+    cut = width // 2
     return call(
         encode_body,
         "encode",
@@ -113,47 +113,37 @@
 
 
 def finish_body(first, second, *refs):
-    sums_refs, (own, for_up, for_down, last) = refs[:-4], refs[-4:]
+    sums_refs, (own, message) = refs[:-2], refs[-2:]
     samples, cut = first.shape
-    width = own.shape[1]
     sums = [sum(r[i:i + 1] for r in sums_refs) for i in range(3)]
     means, scales = variant_stats(sums)
     own[:, :cut] = standardize(first[...], means[:, :cut], scales[:, :cut])
     rest = standardize(second[...], means[:, cut:], scales[:, cut:])
     own[:, cut:] = rest
-    for_up[:samples] = rest
-    middle = for_down.shape[1]
-    for_down[:samples] = rest[:, :middle]
-    last[...] = rest[:, middle:]
+    message[:samples] = rest
     rows = split3(means[:, :cut]) + split3(scales[:, :cut])
-    tail = jnp.concatenate(rows + [jnp.zeros((TAIL - len(rows), cut), jnp.bfloat16)], axis=0)
-    for ref in (for_up, for_down):
-        ref[samples:, :cut] = tail
-        ref[samples:, cut:] = jnp.zeros((TAIL, ref.shape[1] - cut), jnp.bfloat16)
+    rows.append(jnp.zeros((TAIL - len(rows), cut), jnp.bfloat16))
+    message[samples:] = jnp.concatenate(rows, axis=0)
 
 
 def finish(first, second, all_sums, events):
     samples, cut = first.shape
-    rest = second.shape[1]
-    shapes = [
-        (samples, cut + rest),
-        (samples + TAIL, rest),
-        (samples + TAIL, rest - cut),
-        (samples, cut),
-    ]
     return call(
         finish_body,
         "finish",
-        [(s, jnp.bfloat16) for s in shapes],
+        [((samples, 2 * cut), jnp.bfloat16), ((samples + TAIL, cut), jnp.bfloat16)],
         [first, second, *all_sums],
         events=events,
     )
 
 
-def interleave_body(*refs):
-    out = refs[-1]
-    for k in range(BAND):
-        out[:, k, :] = refs[k][...]
+def interleave_body(first, second, third_a, third_b, fourth, out):
+    cut = third_a.shape[1]
+    out[:, 0, :] = first[...]
+    out[:, 1, :] = second[...]
+    out[:, 2, :cut] = third_a[...]
+    out[:, 2, cut:] = third_b[...]
+    out[:, 3, :] = fourth[...]
 
 
 def interleave(panels):
@@ -162,7 +152,7 @@
     return pl.pallas_call(
         interleave_body,
         grid=(rows // tile,),
-        in_specs=[pl.BlockSpec((tile, width), lambda i: (i, 0))] * BAND,
+        in_specs=[pl.BlockSpec((tile, p.shape[1]), lambda i: (i, 0)) for p in panels],
         out_specs=pl.BlockSpec((tile, BAND, width), lambda i: (i, 0, 0)),
         out_shape=jax.ShapeDtypeStruct((rows, BAND, width), jnp.bfloat16),
         compiler_params=params(32),
@@ -184,45 +174,48 @@
         ref[...] = product(whole, cols, d + 1).astype(jnp.bfloat16)
 
 
-def gather_body(n_sub, *refs):
-    held, cols, whole, parts = refs[:n_sub], refs[n_sub], refs[n_sub + 1], refs[n_sub + 2:]
+def gather_body(n_sub, n_held, *refs):
+    held, cols, whole, parts = refs[:n_held], refs[n_held], refs[n_held + 1], refs[n_held + 2:]
     width = held[0].shape[1]
+    pieces = (n_held - 1) // (n_sub - 1)
+    count = whole.shape[0] // pieces
     me = lax.axis_index("sub")
-    for d in range(n_sub):
+
+    def span(d):
         place = lax.rem(me - d + n_sub, n_sub)
-        whole[:, pl.ds(pl.multiple_of(place * width, width), width)] = held[d][...]
+        return pl.ds(pl.multiple_of(place * width, width), width)
+
+    whole[:, span(0)] = held[0][...]
+    for d in range(1, n_sub):
+        for i in range(pieces):
+            whole[i * count:(i + 1) * count, span(d)] = held[1 + (d - 1) * pieces + i][...]
     send_parts(whole, cols[...], parts)
 
 
-def from_tail(message, samples, cut):
-    rows = [message[samples + i:samples + i + 1, :cut].astype(jnp.float32) for i in range(6)]
+def from_tail(tail):
+    rows = [tail[i:i + 1].astype(jnp.float32) for i in range(6)]
     return (rows[0] + rows[1]) + rows[2], (rows[3] + rows[4]) + rows[5]
 
 
-def assemble_body(first, message, *refs):
-    *rest, out = refs
+def assemble_body(first, message, out):
     samples, cut = first.shape
-    end = message.shape[1] + cut
-    out[:, :cut] = standardize(first[...], *from_tail(message, samples, cut))
-    out[:, cut:end] = message[:samples]
-    for ref in rest:
-        out[:, end:end + ref.shape[1]] = ref[...]
-        end += ref.shape[1]
-
-
-def cols_body(n_in, whole, *refs):
-    pieces, cols, parts = refs[:n_in], refs[n_in], refs[n_in + 1:]
-    assemble_body(*pieces, cols)
+    out[:, :cut] = standardize(first[...], *from_tail(message[samples:]))
+    out[:, cut:] = message[:samples]
+
+
+def near_body(whole, first, message, cols, half, *parts):
+    assemble_body(first, message, cols)
+    half[...] = cols[:, :half.shape[1]]
     send_parts(whole, cols[...], parts)
 
 
-def plain_body(whole, cols, *parts):
-    send_parts(whole, cols[...], parts)
+def far_body(whole, cols, *parts):
+    send_parts(whole, cols[:whole.shape[0]], parts)
 
 
 def total_body(whole, cols, *refs):
     *arrived, out = refs
-    total = product(whole, cols[...], 0).astype(jnp.bfloat16).astype(jnp.float32)
+    total = product(whole, cols[:whole.shape[0]], 0).astype(jnp.bfloat16).astype(jnp.float32)
     for ref in arrived:
         total = total + ref[...].astype(jnp.float32)
     out[...] = total.astype(jnp.bfloat16)
@@ -232,14 +225,14 @@
     refs[-1][...] = jnp.zeros_like(refs[-1])
 
 
-def fence(*events):
+def fence(weight, *events):
     return pl.pallas_call(
         fence_body,
         in_specs=[pl.BlockSpec(memory_space=pl.ANY)] * len(events),
         out_specs=pl.BlockSpec(memory_space=pltpu.VMEM),
         out_shape=jax.ShapeDtypeStruct((8, 128), jnp.float32),
         compiler_params=params(1),
-        cost_estimate=pl.CostEstimate(flops=2 * 10**10, bytes_accessed=0, transcendentals=0),
+        cost_estimate=pl.CostEstimate(flops=weight * 10**9, bytes_accessed=0, transcendentals=0),
         name="fence",
     )(*events)
 
@@ -288,8 +281,10 @@
         ]
         return lax.ppermute(x, ("var", axis), route)
 
-    def others_of(part):
-        return [swapped(part, "sub", d) for d in range(1, n_sub)]
+    def others_of(part, pieces):
+        count = part.shape[0] // pieces
+        cuts = [part[i * count:(i + 1) * count] for i in range(pieces)]
+        return [swapped(c, "sub", d) for d in range(1, n_sub) for c in cuts]
 
     def sent(parts, keep=None):
         return [swapped(p, "smp", d + 1, keep) for d, p in enumerate(parts)]
@@ -299,78 +294,66 @@
 
     def gather(part, others, cols, name, events):
         block = ((samples, width * n_sub), jnp.bfloat16)
-        body = functools.partial(gather_body, n_sub)
+        body = functools.partial(gather_body, n_sub, 1 + len(others))
         shapes = [block] + part_shapes(width)
         whole, *parts = call(body, name, shapes, [part, *others, cols], events=events)
         return whole, parts
 
-    def columns(whole, pieces, name, events):
-        span = sum(p.shape[1] for p in pieces)
-        body = functools.partial(cols_body, len(pieces))
-        shapes = [((samples, span), jnp.bfloat16)] + part_shapes(span)
-        cols, *parts = call(body, name, shapes, [whole, *pieces], events=events)
-        return cols, parts
-
     def total(whole, cols, arrived, name, events):
         shape = ((rows_owned, cols.shape[1]), jnp.bfloat16)
         return call(total_body, name, [shape], [whole, cols, *arrived], events=events)[0]
 
-    cut = width // 4
-
     first, second, sums_own = encode(dosages, observed)
-    near_a, up_a = down(first), up_two(first)
+    near_a = down(first)
+    step = fence(20, first)
+    sums_own, first_up, step = together(sums_own, first, step)
+    up_a = up_two(first_up)
     arrived_sums = [swapped(sums_own, "smp", d) for d in range(1, n_smp)]
-    step = fence(first)
-    own, for_up, for_down, last = finish(first, second, [sums_own] + arrived_sums, [step])
-    near_b, up_b = down(for_down), up_two(for_up)
-    others = others_of(own)
-    step = fence(own)
-
-    whole, part0 = gather(own, others, own, "gather0", [near_a, up_a, step])
-    last, near_a, *part0 = together(last, near_a, *part0)
-    near_c = down(last)
+    step = fence(20, step)
+    own, message = finish(first, second, [sums_own] + arrived_sums, [step])
+    near_b, up_b = down(message), up_two(message)
+    others = others_of(own, 1)
+    step = fence(20, own)
+
+    whole, part0 = gather(own, others, own, "gather0", [near_a, step])
+    got0 = sent(part0)
+    near_b, whole = together(near_b, whole)
+    far_b = down_again(near_b)
+    half = ((samples, width // 2), jnp.bfloat16)
+    cols1, near_a, *part1 = call(
+        near_body,
+        "near",
+        [((samples, width), jnp.bfloat16), half] + part_shapes(width),
+        [whole, near_a, near_b],
+    )
     far_a = down_again(near_a)
-    got0 = sent(part0)
-    step = fence(whole, *part0)
-    near_b, step = together(near_b, step)
-    far_b = down_again(near_b)
-    step = fence(near_b, step)
-    near_c, step = together(near_c, step)
-    far_c = down_again(near_c)
-
     (rows3,) = call(
         assemble_body,
         "rows3",
         [((samples, width), jnp.bfloat16)],
         [up_a, up_b],
-        events=[near_c, step],
-    )
-    others3 = others_of(rows3)
-    step = fence(rows3)
-    cols1, part1 = columns(whole, [near_a, near_b, near_c], "columns1", [step, *got0])
-    got1 = sent(part1, lambda v: not holds_three(v) and v + 1 < n_var)
-    step = fence(cols1)
-    panel0 = total(whole, own, got0, "total0", [step])
-    whole3, part3 = gather(rows3, others3, cols1, "gather3", [panel0])
+        events=[cols1],
+    )
+    others3 = others_of(rows3, 2)
+    panel0 = total(whole, own, got0, "total0", [rows3])
+    whole3, part3 = gather(rows3, others3, cols1, "gather3", [fence(3, panel0)])
     got3 = sent(part3, holds_three)
-    *part1, far_a, whole3 = together(*part1, far_a, whole3)
-    got1_late = sent(part1, holds_three)
-    step = fence(far_a, whole3)
-
-    cols2, part2 = columns(whole, [far_a, far_b], "columns2", [step, *got1])
-    got2 = sent(part2, lambda v: v + 2 < n_var)
-    step = fence(cols2)
+    part2_b = call(far_body, "far_b", part_shapes(width // 2), [whole, far_b], events=[whole3])
+    got2_b = sent(part2_b)
+    step = fence(12, *part2_b)
     panel3 = total(whole3, cols1, got3, "total3", [step])
-    step = fence(panel3)
+    *part1, panel3 = together(*part1, panel3)
+    got1 = sent(part1)
     panel3 = down_two(panel3)
-    part2_c = call(plain_body, "last2", part_shapes(cut), [whole, far_c], events=[step])
-    got2_c = sent(part2_c, lambda v: v + 2 < n_var)
-    step = fence(*part2_c)
-    panel2_ab = total(whole, cols2, got2, "total2", [step])
-    panel2_c = total(whole, far_c, got2_c, "total2c", [panel2_ab])
-    panel1 = total(whole, cols1, got1 + got1_late, "total1", [panel2_c])
-    panel2 = jnp.concatenate([panel2_ab, panel2_c], axis=1)
-    return interleave([panel0, panel1, panel2, panel3])
+    part2_a = call(
+        far_body, "far_a", part_shapes(width // 2), [whole, far_a], events=[*part1]
+    )
+    got2_a = sent(part2_a, lambda v: v + 2 < n_var)
+    panel2_b = total(whole, far_b, got2_b, "total2b", [*part2_a])
+    step = fence(3, panel2_b)
+    panel1 = total(whole, cols1, got1, "total1", [step])
+    panel2_a = total(whole, far_a, got2_a, "total2a", [panel1])
+    return interleave([panel0, panel1, panel2_a, panel2_b, panel3])
 
 
 def solution(mesh):

time: 89.7 us -> 77.5 us (0.86)
  waiting for transfers between devices: 40.9 us -> 34.6 us
  starting transfers between devices: 31.9 us -> 26.3 us
    ppermute x5 -> x2, starting transfers between devices: 10.6 us -> 4.25 us  [swapped(): return lax.ppermute(x, ('var', axis), route)]
    ppermute x9 -> x7, waiting for transfers between devices: 32.4 us -> 27.5 us  [along(): return lax.ppermute(x, 'var', route)]
    ppermute x4 -> x7, starting transfers between devices: 3.27 us -> 7.81 us  [swapped(): return lax.ppermute(x, axis, [(i, (i + distance) % n) for i in range(n)])]
    ppermute x5 -> x2, waiting for transfers between devices: 6.31 us -> 2.01 us  [swapped(): return lax.ppermute(x, ('var', axis), route)]
    ppermute x9 -> x7, starting transfers between devices: 18 us -> 14.2 us  [along(): return lax.ppermute(x, 'var', route)]
    ppermute x4 -> x7, waiting for transfers between devices: 2.25 us -> 5.05 us  [swapped(): return lax.ppermute(x, axis, [(i, (i + distance) % n) for i in range(n)])]
  transfers between devices with their start and end apart: 18 -> 16, of which waited for: 8 -> 8; matrix products, arithmetic and copies ran while one was open for 0% -> 0% of each run, Pallas kernels for 10% -> 10%
where the time goes in v3:
time: 77.5 us; the launch traced here: 76.9 us
  waiting for transfers between devices  34.6 us (45%)
  starting transfers between devices  26.3 us (34%)
  Pallas kernels  12.5 us (16%)
  local copies, waits for them, and re-layouts  3.25 us (4%)
    ppermute x7, waiting for transfers between devices, along(): return lax.ppermute(x, 'var', route)  27.5 us
    ppermute x7, starting transfers between devices, along(): return lax.ppermute(x, 'var', route)  14.2 us
    pallas_call x13, Pallas kernels, call(): pl.pallas_call(with_events, in_specs=[pl.BlockSpec(memory_space=place)] *...  8.95 us
    ppermute x7, starting transfers between devices, swapped(): return lax.ppermute(x, axis, [(i, (i + distance) % n) for i in range(n)])  7.81 us
    ppermute x7, waiting for transfers between devices, swapped(): return lax.ppermute(x, axis, [(i, (i + distance) % n) for i in range(n)])  5.05 us
    ppermute x2, starting transfers between devices, swapped(): return lax.ppermute(x, ('var', axis), route)  4.25 us
    pallas_call x1, Pallas kernels, interleave(): pl.pallas_call(interleave_body, grid=(rows // tile,), in_specs=[pl.BlockS...  3.56 us
    unnamed x4, local copies, waits for them, and re-layouts  3.18 us
  transfers between devices with their start and end apart: 16, of which 8 were waited for; matrix products, arithmetic and copies ran while one was open for 0% of the time, Pallas kernels for 10%

profile of v3, /device:TPU:0, one launch (start us, length us, event | category | flops | bytes accessed | tf_op | source)
XLA Modules:
  0.0 76.9 jit_solution(9479536876736571903)
XLA Ops:
  0.0 1.6 %copy-done = s32[1024,512]{1,0:T(8,128)S(1)} copy-done((s32[1024,512]{1,0:T(8,128)S(1)}, s32[1024,512]{1,0:T(8,128)}, u32[]{:S(2)}) %copy-start) | copy-done | bytes 2097176
  1.6 1.6 %copy-done.1 = s32[1024,512]{1,0:T(8,128)S(1)} copy-done((s32[1024,512]{1,0:T(8,128)S(1)}, s32[1024,512]{1,0:T(8,128)}, u32[]{:S(2)}) %copy-start.1) | copy-done | bytes 2097176
  3.2 1.1 %encode.1 = (bf16[1024,256]{1,0:T(8,128)(2,1)S(1)}, bf16[1024,256]{1,0:T(8,128)(2,1)S(1)}, s32[8,512]{1,0:T(8,128)S(1)}) custom-call(s32[1024,512]{1,0:T(8,128)S(1)} %copy-done, s32[1024,512]{1,0:T(8,128)S(1)} %copy-done.1), custom_call_target="tpu_custom_call" | custom-call | tf_op jit(solution)/shard_map/encode/pallas_call | solution.py:64
  4.3 1.3 %collective-permute-start.3 = (bf16[1024,256]{1,0:T(8,128)(2,1)S(1)}, bf16[1024,256]{1,0:T(8,128)(2,1)S(1)}, u32[]{:S(2)}, u32[]{:S(2)}) collective-permute-start(bf16[1024,256]{1,0:T(8,128)(2,1)S(1)} %get-tuple-element.34.refs_0_), channel_id=1, source_target_pairs={{4,0},{8,4},{12,8},{5,1},{9,5},{13,9},{6,2},{10,6},{14,10},{7,3},{... | collective-permute-start | bytes 1572872 | tf_op jit(solution)/shard_map/ppermute | solution.py:255
  5.6 3.0 %collective-permute-start = (s32[8,512]{1,0:T(8,128)S(1)}, s32[8,512]{1,0:T(8,128)S(1)}, u32[]{:S(2)}, u32[]{:S(2)}) collective-permute-start(s32[8,512]{1,0:T(8,128)S(1)} %get-tuple-element.27.refs_2_), channel_id=1, source_target_pairs={{0,2},{2,0},{1,3},{3,1},{4,6},{6,4},{5,7},{7,5},{8,10},{10,8},{9,1... | collective-permute-start | bytes 49160 | tf_op jit(solution)/shard_map/ppermute | solution.py:275
  8.6 5.6 %collective-permute-start.5 = (bf16[1024,256]{1,0:T(8,128)(2,1)S(1)}, bf16[1024,256]{1,0:T(8,128)(2,1)S(1)}, u32[]{:S(2)}, u32[]{:S(2)}) collective-permute-start(bf16[1024,256]{1,0:T(8,128)(2,1)S(1)} %get-tuple-element.34.refs_0_), channel_id=1, source_target_pairs={{0,8},{1,9},{2,10},{3,11},{16,24},{17,25},{18,26},{19,27}} | collective-permute-start | bytes 1572872 | tf_op jit(solution)/shard_map/ppermute | solution.py:255
  14.6 2.2 %collective-permute-start.6 = (bf16[1040,256]{1,0:T(8,128)(2,1)S(1)}, bf16[1040,256]{1,0:T(8,128)(2,1)S(1)}, u32[]{:S(2)}, u32[]{:S(2)}) collective-permute-start(bf16[1040,256]{1,0:T(8,128)(2,1)S(1)} %get-tuple-element.29), channel_id=1, source_target_pairs={{0,8},{1,9},{2,10},{3,11},{16,24},{17,25},{18,26},{19,27}} | collective-permute-start | bytes 1597448 | tf_op jit(solution)/shard_map/ppermute | solution.py:255
  16.9 1.3 %collective-permute-start.1 = (bf16[1040,256]{1,0:T(8,128)(2,1)S(1)}, bf16[1040,256]{1,0:T(8,128)(2,1)S(1)}, u32[]{:S(2)}, u32[]{:S(2)}) collective-permute-start(bf16[1040,256]{1,0:T(8,128)(2,1)S(1)} %get-tuple-element.29), channel_id=1, source_target_pairs={{4,0},{8,4},{12,8},{5,1},{9,5},{13,9},{6,2},{10,6},{14,10},{7,3},{... | collective-permute-start | bytes 1597448 | tf_op jit(solution)/shard_map/ppermute | solution.py:255
  18.2 3.7 %collective-permute-done.3.refs_3_.refs_1_ = bf16[1024,256]{1,0:T(8,128)(2,1)S(1)} collective-permute-done((bf16[1024,256]{1,0:T(8,128)(2,1)S(1)}, bf16[1024,256]{1,0:T(8,128)(2,1)S(1)}, u32[]{:S(2)}, u32[]{:S(2)}) %collective-permute-start.3) | collective-permute-done | bytes 524320 | tf_op jit(solution)/shard_map/ppermute | solution.py:255
  21.9 1.0 %gather0.1 = (bf16[1024,1024]{1,0:T(8,128)(2,1)S(1)}, bf16[512,512]{1,0:T(8,128)(2,1)S(1)}) custom-call(bf16[1024,512]{1,0:T(8,128)(2,1)S(1)} %get-tuple-element.30.refs_0_.refs_2_.refs_1_, bf16[1024,512]{1,0:T(8,128)(2,1)S(1)} %collective-permute-done.2.refs_1_, bf16[1024,512]{1,0:T(8,128)(2,1)S(1)} %get-tuple-element.30.refs_0_.refs_2_.refs_1_, ...), custom_call_target="tpu_custom_call" | custom-call | tf_op jit(solution)/shard_map/gather0/pallas_call | solution.py:64
  22.9 2.0 %collective-permute-start.4 = (bf16[512,512]{1,0:T(8,128)(2,1)S(1)}, bf16[512,512]{1,0:T(8,128)(2,1)S(1)}, u32[]{:S(2)}, u32[]{:S(2)}) collective-permute-start(bf16[512,512]{1,0:T(8,128)(2,1)S(1)} %get-tuple-element.33), channel_id=1, source_target_pairs={{0,2},{2,0},{1,3},{3,1},{4,6},{6,4},{5,7},{7,5},{8,10},{10,8},{9,1... | collective-permute-start | bytes 1572872 | tf_op jit(solution)/shard_map/ppermute | solution.py:275
  25.0 7.6 %collective-permute-done.1.refs_2_ = bf16[1040,256]{1,0:T(8,128)(2,1)S(1)} collective-permute-done((bf16[1040,256]{1,0:T(8,128)(2,1)S(1)}, bf16[1040,256]{1,0:T(8,128)(2,1)S(1)}, u32[]{:S(2)}, u32[]{:S(2)}) %collective-permute-start.1) | collective-permute-done | bytes 532512 | tf_op jit(solution)/shard_map/ppermute | solution.py:255
  32.5 1.3 %collective-permute-start.10 = (bf16[1040,256]{1,0:T(8,128)(2,1)S(1)}, bf16[1040,256]{1,0:T(8,128)(2,1)S(1)}, u32[]{:S(2)}, u32[]{:S(2)}) collective-permute-start(bf16[1040,256]{1,0:T(8,128)(2,1)S(1)} %collective-permute-done.1.refs_2_), channel_id=1, source_target_pairs={{4,0},{8,4},{5,1},{9,5},{6,2},{10,6},{7,3},{11,7},{20,16},{24,20},... | collective-permute-start | bytes 1597448 | tf_op jit(solution)/shard_map/ppermute | solution.py:255
  34.6 1.5 %collective-permute-done.6.refs_1_ = bf16[1040,256]{1,0:T(8,128)(2,1)S(1)} collective-permute-done((bf16[1040,256]{1,0:T(8,128)(2,1)S(1)}, bf16[1040,256]{1,0:T(8,128)(2,1)S(1)}, u32[]{:S(2)}, u32[]{:S(2)}) %collective-permute-start.6) | collective-permute-done | bytes 532512 | tf_op jit(solution)/shard_map/ppermute | solution.py:255
  37.0 1.3 %collective-permute-start.13 = (bf16[1024,256]{1,0:T(8,128)(2,1)S(1)}, bf16[1024,256]{1,0:T(8,128)(2,1)S(1)}, u32[]{:S(2)}, u32[]{:S(2)}) collective-permute-start(bf16[1024,256]{1,0:T(8,128)(2,1)S(1)} %get-tuple-element.41), channel_id=1, source_target_pairs={{4,0},{8,4},{5,1},{9,5},{6,2},{10,6},{7,3},{11,7},{20,16},{24,20},... | collective-permute-start | bytes 1572872 | tf_op jit(solution)/shard_map/ppermute | solution.py:255
  40.8 8.6 %collective-permute-done.10.refs_1_ = bf16[1040,256]{1,0:T(8,128)(2,1)S(1)} collective-permute-done((bf16[1040,256]{1,0:T(8,128)(2,1)S(1)}, bf16[1040,256]{1,0:T(8,128)(2,1)S(1)}, u32[]{:S(2)}, u32[]{:S(2)}) %collective-permute-start.10) | collective-permute-done | bytes 532512 | tf_op jit(solution)/shard_map/ppermute | solution.py:255
  50.0 1.7 %collective-permute-start.12 = (bf16[512,256]{1,0:T(8,128)(2,1)S(1)}, bf16[512,256]{1,0:T(8,128)(2,1)S(1)}, u32[]{:S(2)}, u32[]{:S(2)}) collective-permute-start(bf16[512,256]{1,0:T(8,128)(2,1)S(1)} %far_b.1.refs_0_), channel_id=1, source_target_pairs={{0,2},{2,0},{1,3},{3,1},{4,6},{6,4},{5,7},{7,5},{8,10},{10,8},{9,1... | collective-permute-start | bytes 786440 | tf_op jit(solution)/shard_map/ppermute | solution.py:275
  52.9 1.3 %collective-permute-start.15 = (bf16[512,512]{1,0:T(8,128)(2,1)S(1)}, bf16[512,512]{1,0:T(8,128)(2,1)S(1)}, u32[]{:S(2)}, u32[]{:S(2)}) collective-permute-start(bf16[512,512]{1,0:T(8,128)(2,1)S(1)} %total3.1), channel_id=1, source_target_pairs={{8,0},{9,1},{10,2},{11,3},{24,16},{25,17},{26,18},{27,19}} | collective-permute-start | bytes 1572872 | tf_op jit(solution)/shard_map/ppermute | solution.py:255
  54.2 4.4 %collective-permute-done.13.refs_1_ = bf16[1024,256]{1,0:T(8,128)(2,1)S(1)} collective-permute-done((bf16[1024,256]{1,0:T(8,128)(2,1)S(1)}, bf16[1024,256]{1,0:T(8,128)(2,1)S(1)}, u32[]{:S(2)}, u32[]{:S(2)}) %collective-permute-start.13) | collective-permute-done | bytes 524320 | tf_op jit(solution)/shard_map/ppermute | solution.py:255
  59.1 3.6 %collective-permute-start.14 = (bf16[512,256]{1,0:T(8,128)(2,1)S(1)}, bf16[512,256]{1,0:T(8,128)(2,1)S(1)}, u32[]{:S(2)}, u32[]{:S(2)}) collective-permute-start(bf16[512,256]{1,0:T(8,128)(2,1)S(1)} %far_a.1.refs_3_), channel_id=1, source_target_pairs={{0,2},{2,0},{4,6},{6,4},{1,3},{3,1},{5,7},{7,5},{16,18},{18,16},{2... | collective-permute-start | bytes 786440 | tf_op jit(solution)/shard_map/ppermute | solution.py:282
  63.3 5.0 %collective-permute-done.11.refs_2_ = bf16[512,512]{1,0:T(8,128)(2,1)S(1)} collective-permute-done((bf16[512,512]{1,0:T(8,128)(2,1)S(1)}, bf16[512,512]{1,0:T(8,128)(2,1)S(1)}, u32[]{:S(2)}, u32[]{:S(2)}) %collective-permute-start.11) | collective-permute-done | bytes 524320 | tf_op jit(solution)/shard_map/ppermute | solution.py:275
  69.1 2.0 %collective-permute-done.14.refs_2_ = bf16[512,256]{1,0:T(8,128)(2,1)S(1)} collective-permute-done((bf16[512,256]{1,0:T(8,128)(2,1)S(1)}, bf16[512,256]{1,0:T(8,128)(2,1)S(1)}, u32[]{:S(2)}, u32[]{:S(2)}) %collective-permute-start.14) | collective-permute-done | bytes 262176 | tf_op jit(solution)/shard_map/ppermute | solution.py:282
  71.6 1.8 %collective-permute-done.15.fourth = bf16[512,512]{1,0:T(8,128)(2,1)S(1)} collective-permute-done((bf16[512,512]{1,0:T(8,128)(2,1)S(1)}, bf16[512,512]{1,0:T(8,128)(2,1)S(1)}, u32[]{:S(2)}, u32[]{:S(2)}) %collective-permute-start.15) | collective-permute-done | bytes 524320 | tf_op jit(solution)/shard_map/ppermute | solution.py:255
  73.4 3.6 %interleave.1 = bf16[512,4,512]{2,1,0:T(4,128)(2,1)} custom-call(bf16[512,512]{1,0:T(8,128)(2,1)S(1)} %total0.1.refs_0_.first, bf16[512,512]{1,0:T(8,128)(2,1)S(1)} %total1.1.refs_3_.second, bf16[512,256]{1,0:T(8,128)(2,1)S(1)} %total2a.1.third_a, bf16[512,256]{1,0:T(8,128)(2,1)S(1)} %total2b.1.refs_0_.third_b, ...), custom_call_target="tpu_custom_call" | custom-call | tf_op jit(solution)/shard_map/interleave/pallas_call | solution.py:152
  (33 shorter events, 8.8 us)
Async XLA Ops:
  0.0 1.6 %copy-start = (s32[1024,512]{1,0:T(8,128)S(1)}, s32[1024,512]{1,0:T(8,128)}, u32[]{:S(2)}) copy-start(s32[1024,512]{1,0:T(8,128)} %refs_0_.1) | copy-start | bytes 6291460
  1.6 1.6 %copy-start.1 = (s32[1024,512]{1,0:T(8,128)S(1)}, s32[1024,512]{1,0:T(8,128)}, u32[]{:S(2)}) copy-start(s32[1024,512]{1,0:T(8,128)} %refs_1_.1) | copy-start | bytes 6291460
  4.3 17.7 %collective-permute-start.3 = (bf16[1024,256]{1,0:T(8,128)(2,1)S(1)}, bf16[1024,256]{1,0:T(8,128)(2,1)S(1)}, u32[]{:S(2)}, u32[]{:S(2)}) collective-permute-start(bf16[1024,256]{1,0:T(8,128)(2,1)S(1)} %get-tuple-element.34.refs_0_), channel_id=1, source_target_pairs={{4,0},{8,4},{12,8},{5,1},{9,5},{13,9},{6,2},{10,6},{14,10},{7,3},{... | collective-permute-start | bytes 1572872 | tf_op jit(solution)/shard_map/ppermute | solution.py:255
  5.6 8.6 %collective-permute-start = (s32[8,512]{1,0:T(8,128)S(1)}, s32[8,512]{1,0:T(8,128)S(1)}, u32[]{:S(2)}, u32[]{:S(2)}) collective-permute-start(s32[8,512]{1,0:T(8,128)S(1)} %get-tuple-element.27.refs_2_), channel_id=1, source_target_pairs={{0,2},{2,0},{1,3},{3,1},{4,6},{6,4},{5,7},{7,5},{8,10},{10,8},{9,1... | collective-permute-start | bytes 49160 | tf_op jit(solution)/shard_map/ppermute | solution.py:275
  8.6 26.0 %collective-permute-start.5 = (bf16[1024,256]{1,0:T(8,128)(2,1)S(1)}, bf16[1024,256]{1,0:T(8,128)(2,1)S(1)}, u32[]{:S(2)}, u32[]{:S(2)}) collective-permute-start(bf16[1024,256]{1,0:T(8,128)(2,1)S(1)} %get-tuple-element.34.refs_0_), channel_id=1, source_target_pairs={{0,8},{1,9},{2,10},{3,11},{16,24},{17,25},{18,26},{19,27}} | collective-permute-start | bytes 1572872 | tf_op jit(solution)/shard_map/ppermute | solution.py:255
  14.6 21.5 %collective-permute-start.6 = (bf16[1040,256]{1,0:T(8,128)(2,1)S(1)}, bf16[1040,256]{1,0:T(8,128)(2,1)S(1)}, u32[]{:S(2)}, u32[]{:S(2)}) collective-permute-start(bf16[1040,256]{1,0:T(8,128)(2,1)S(1)} %get-tuple-element.29), channel_id=1, source_target_pairs={{0,8},{1,9},{2,10},{3,11},{16,24},{17,25},{18,26},{19,27}} | collective-permute-start | bytes 1597448 | tf_op jit(solution)/shard_map/ppermute | solution.py:255
  16.9 15.7 %collective-permute-start.1 = (bf16[1040,256]{1,0:T(8,128)(2,1)S(1)}, bf16[1040,256]{1,0:T(8,128)(2,1)S(1)}, u32[]{:S(2)}, u32[]{:S(2)}) collective-permute-start(bf16[1040,256]{1,0:T(8,128)(2,1)S(1)} %get-tuple-element.29), channel_id=1, source_target_pairs={{4,0},{8,4},{12,8},{5,1},{9,5},{13,9},{6,2},{10,6},{14,10},{7,3},{... | collective-permute-start | bytes 1597448 | tf_op jit(solution)/shard_map/ppermute | solution.py:255
  18.2 3.8 %collective-permute-start.2 = (bf16[1024,512]{1,0:T(8,128)(2,1)S(1)}, bf16[1024,512]{1,0:T(8,128)(2,1)S(1)}, u32[]{:S(2)}, u32[]{:S(2)}) collective-permute-start(bf16[1024,512]{1,0:T(8,128)(2,1)S(1)} %get-tuple-element.30.refs_0_.refs_2_.refs_1_), channel_id=1, source_target_pairs={{0,1},{1,0},{2,3},{3,2},{4,5},{5,4},{6,7},{7,6},{8,9},{9,8},{10,11... | collective-permute-start | bytes 3145736 | tf_op jit(solution)/shard_map/ppermute | solution.py:275
  22.9 15.3 %collective-permute-start.4 = (bf16[512,512]{1,0:T(8,128)(2,1)S(1)}, bf16[512,512]{1,0:T(8,128)(2,1)S(1)}, u32[]{:S(2)}, u32[]{:S(2)}) collective-permute-start(bf16[512,512]{1,0:T(8,128)(2,1)S(1)} %get-tuple-element.33), channel_id=1, source_target_pairs={{0,2},{2,0},{1,3},{3,1},{4,6},{6,4},{5,7},{7,5},{8,10},{10,8},{9,1... | collective-permute-start | bytes 1572872 | tf_op jit(solution)/shard_map/ppermute | solution.py:275
  32.5 16.9 %collective-permute-start.10 = (bf16[1040,256]{1,0:T(8,128)(2,1)S(1)}, bf16[1040,256]{1,0:T(8,128)(2,1)S(1)}, u32[]{:S(2)}, u32[]{:S(2)}) collective-permute-start(bf16[1040,256]{1,0:T(8,128)(2,1)S(1)} %collective-permute-done.1.refs_2_), channel_id=1, source_target_pairs={{4,0},{8,4},{5,1},{9,5},{6,2},{10,6},{7,3},{11,7},{20,16},{24,20},... | collective-permute-start | bytes 1597448 | tf_op jit(solution)/shard_map/ppermute | solution.py:255
  36.4 2.7 %collective-permute-start.8 = (bf16[512,512]{1,0:T(8,128)(2,1)S(1)}, bf16[512,512]{1,0:T(8,128)(2,1)S(1)}, u32[]{:S(2)}, u32[]{:S(2)}) collective-permute-start(bf16[512,512]{1,0:T(8,128)(2,1)S(1)} %get-tuple-element.43), channel_id=1, source_target_pairs={{0,1},{1,0},{2,3},{3,2},{4,5},{5,4},{6,7},{7,6},{8,9},{9,8},{10,11... | collective-permute-start | bytes 1572872 | tf_op jit(solution)/shard_map/ppermute | solution.py:275
  36.5 2.6 %collective-permute-start.7 = (bf16[512,512]{1,0:T(8,128)(2,1)S(1)}, bf16[512,512]{1,0:T(8,128)(2,1)S(1)}, u32[]{:S(2)}, u32[]{:S(2)}) collective-permute-start(bf16[512,512]{1,0:T(8,128)(2,1)S(1)} %get-tuple-element.44), channel_id=1, source_target_pairs={{0,1},{1,0},{2,3},{3,2},{4,5},{5,4},{6,7},{7,6},{8,9},{9,8},{10,11... | collective-permute-start | bytes 1572872 | tf_op jit(solution)/shard_map/ppermute | solution.py:275
  37.0 21.6 %collective-permute-start.13 = (bf16[1024,256]{1,0:T(8,128)(2,1)S(1)}, bf16[1024,256]{1,0:T(8,128)(2,1)S(1)}, u32[]{:S(2)}, u32[]{:S(2)}) collective-permute-start(bf16[1024,256]{1,0:T(8,128)(2,1)S(1)} %get-tuple-element.41), channel_id=1, source_target_pairs={{4,0},{8,4},{5,1},{9,5},{6,2},{10,6},{7,3},{11,7},{20,16},{24,20},... | collective-permute-start | bytes 1572872 | tf_op jit(solution)/shard_map/ppermute | solution.py:255
  40.1 11.5 %collective-permute-start.9 = (bf16[512,512]{1,0:T(8,128)(2,1)S(1)}, bf16[512,512]{1,0:T(8,128)(2,1)S(1)}, u32[]{:S(2)}, u32[]{:S(2)}) collective-permute-start(bf16[512,512]{1,0:T(8,128)(2,1)S(1)} %get-tuple-element.39), channel_id=1, source_target_pairs={{8,10},{10,8},{9,11},{11,9},{24,26},{26,24},{25,27},{27,25}} | collective-permute-start | bytes 1572872 | tf_op jit(solution)/shard_map/ppermute | solution.py:282
  50.0 12.7 %collective-permute-start.12 = (bf16[512,256]{1,0:T(8,128)(2,1)S(1)}, bf16[512,256]{1,0:T(8,128)(2,1)S(1)}, u32[]{:S(2)}, u32[]{:S(2)}) collective-permute-start(bf16[512,256]{1,0:T(8,128)(2,1)S(1)} %far_b.1.refs_0_), channel_id=1, source_target_pairs={{0,2},{2,0},{1,3},{3,1},{4,6},{6,4},{5,7},{7,5},{8,10},{10,8},{9,1... | collective-permute-start | bytes 786440 | tf_op jit(solution)/shard_map/ppermute | solution.py:275
  52.5 15.8 %collective-permute-start.11 = (bf16[512,512]{1,0:T(8,128)(2,1)S(1)}, bf16[512,512]{1,0:T(8,128)(2,1)S(1)}, u32[]{:S(2)}, u32[]{:S(2)}) collective-permute-start(bf16[512,512]{1,0:T(8,128)(2,1)S(1)} %get-tuple-element.40.refs_2_), channel_id=1, source_target_pairs={{0,2},{2,0},{1,3},{3,1},{4,6},{6,4},{5,7},{7,5},{8,10},{10,8},{9,1... | collective-permute-start | bytes 1572872 | tf_op jit(solution)/shard_map/ppermute | solution.py:275
  52.9 20.4 %collective-permute-start.15 = (bf16[512,512]{1,0:T(8,128)(2,1)S(1)}, bf16[512,512]{1,0:T(8,128)(2,1)S(1)}, u32[]{:S(2)}, u32[]{:S(2)}) collective-permute-start(bf16[512,512]{1,0:T(8,128)(2,1)S(1)} %total3.1), channel_id=1, source_target_pairs={{8,0},{9,1},{10,2},{11,3},{24,16},{25,17},{26,18},{27,19}} | collective-permute-start | bytes 1572872 | tf_op jit(solution)/shard_map/ppermute | solution.py:255
  59.1 11.9 %collective-permute-start.14 = (bf16[512,256]{1,0:T(8,128)(2,1)S(1)}, bf16[512,256]{1,0:T(8,128)(2,1)S(1)}, u32[]{:S(2)}, u32[]{:S(2)}) collective-permute-start(bf16[512,256]{1,0:T(8,128)(2,1)S(1)} %far_a.1.refs_3_), channel_id=1, source_target_pairs={{0,2},{2,0},{4,6},{6,4},{1,3},{3,1},{5,7},{7,5},{16,18},{18,16},{2... | collective-permute-start | bytes 786440 | tf_op jit(solution)/shard_map/ppermute | solution.py:282

commit v4 on v3

--- a/solution.py
+++ b/solution.py
@@ -138,17 +138,25 @@
 
 
 def interleave_body(first, second, third_a, third_b, fourth, out):
-    cut = third_a.shape[1]
-    out[:, 0, :] = first[...]
-    out[:, 1, :] = second[...]
-    out[:, 2, :cut] = third_a[...]
-    out[:, 2, cut:] = third_b[...]
-    out[:, 3, :] = fourth[...]
+    tile, width = first.shape
+    count = min(tile, 64)
+    size = BAND * count
+    to_row = lax.broadcasted_iota(jnp.int32, (size, size), 0)
+    from_row = lax.broadcasted_iota(jnp.int32, (size, size), 1)
+    panel = sum((from_row >= k * count).astype(jnp.int32) for k in range(1, BAND))
+    order = (to_row == (from_row - panel * count) * BAND + panel).astype(jnp.float32)
+    order = order.astype(jnp.bfloat16)
+    for i in range(tile // count):
+        span = slice(i * count, (i + 1) * count)
+        third = jnp.concatenate([third_a[span], third_b[span]], axis=1)
+        rows = jnp.concatenate([first[span], second[span], third, fourth[span]], axis=0)
+        turned = jnp.dot(order, rows, preferred_element_type=jnp.float32)
+        out[span] = turned.astype(jnp.bfloat16).reshape(count, BAND, width)
 
 
 def interleave(panels):
     rows, width = panels[0].shape
-    tile = min(rows, 128)
+    tile = min(rows, 256)
     return pl.pallas_call(
         interleave_body,
         grid=(rows // tile,),

time: 77.5 us -> 75.8 us (0.978)
  Pallas kernels: 12.5 us -> 10.8 us
    pallas_call x1, Pallas kernels: 3.56 us -> 1.87 us  [interleave(): pl.pallas_call(interleave_body, grid=(rows // tile,), in_specs=[pl.BlockS...]
  transfers between devices with their start and end apart: 16 -> 16, of which waited for: 8 -> 8; matrix products, arithmetic and copies ran while one was open for 0% -> 0% of each run, Pallas kernels for 10% -> 11%
where the time goes in v4:
time: 75.8 us; the launch traced here: 75.2 us
  waiting for transfers between devices  34.6 us (46%)
  starting transfers between devices  26.3 us (35%)
  Pallas kernels  10.8 us (14%)
  local copies, waits for them, and re-layouts  3.25 us (4%)
    ppermute x7, waiting for transfers between devices, along(): return lax.ppermute(x, 'var', route)  27.5 us
    ppermute x7, starting transfers between devices, along(): return lax.ppermute(x, 'var', route)  14.2 us
    pallas_call x13, Pallas kernels, call(): pl.pallas_call(with_events, in_specs=[pl.BlockSpec(memory_space=place)] *...  8.95 us
    ppermute x7, starting transfers between devices, swapped(): return lax.ppermute(x, axis, [(i, (i + distance) % n) for i in range(n)])  7.81 us
    ppermute x7, waiting for transfers between devices, swapped(): return lax.ppermute(x, axis, [(i, (i + distance) % n) for i in range(n)])  5.05 us
    ppermute x2, starting transfers between devices, swapped(): return lax.ppermute(x, ('var', axis), route)  4.25 us
    unnamed x4, local copies, waits for them, and re-layouts  3.18 us
    ppermute x2, waiting for transfers between devices, swapped(): return lax.ppermute(x, ('var', axis), route)  2.01 us
  transfers between devices with their start and end apart: 16, of which 8 were waited for; matrix products, arithmetic and copies ran while one was open for 0% of the time, Pallas kernels for 11%

profile of v4, /device:TPU:0, one launch (start us, length us, event | category | flops | bytes accessed | tf_op | source)
XLA Modules:
  0.0 75.2 jit_solution(18422107614246923851)
XLA Ops:
  0.0 1.6 %copy-done = s32[1024,512]{1,0:T(8,128)S(1)} copy-done((s32[1024,512]{1,0:T(8,128)S(1)}, s32[1024,512]{1,0:T(8,128)}, u32[]{:S(2)}) %copy-start) | copy-done | bytes 2097176
  1.6 1.6 %copy-done.1 = s32[1024,512]{1,0:T(8,128)S(1)} copy-done((s32[1024,512]{1,0:T(8,128)S(1)}, s32[1024,512]{1,0:T(8,128)}, u32[]{:S(2)}) %copy-start.1) | copy-done | bytes 2097176
  3.2 1.1 %encode.1 = (bf16[1024,256]{1,0:T(8,128)(2,1)S(1)}, bf16[1024,256]{1,0:T(8,128)(2,1)S(1)}, s32[8,512]{1,0:T(8,128)S(1)}) custom-call(s32[1024,512]{1,0:T(8,128)S(1)} %copy-done, s32[1024,512]{1,0:T(8,128)S(1)} %copy-done.1), custom_call_target="tpu_custom_call" | custom-call | tf_op jit(solution)/shard_map/encode/pallas_call | solution.py:64
  4.3 1.3 %collective-permute-start.3 = (bf16[1024,256]{1,0:T(8,128)(2,1)S(1)}, bf16[1024,256]{1,0:T(8,128)(2,1)S(1)}, u32[]{:S(2)}, u32[]{:S(2)}) collective-permute-start(bf16[1024,256]{1,0:T(8,128)(2,1)S(1)} %get-tuple-element.34.refs_0_), channel_id=1, source_target_pairs={{4,0},{8,4},{12,8},{5,1},{9,5},{13,9},{6,2},{10,6},{14,10},{7,3},{... | collective-permute-start | bytes 1572872 | tf_op jit(solution)/shard_map/ppermute | solution.py:263
  5.6 3.0 %collective-permute-start = (s32[8,512]{1,0:T(8,128)S(1)}, s32[8,512]{1,0:T(8,128)S(1)}, u32[]{:S(2)}, u32[]{:S(2)}) collective-permute-start(s32[8,512]{1,0:T(8,128)S(1)} %get-tuple-element.27.refs_2_), channel_id=1, source_target_pairs={{0,2},{2,0},{1,3},{3,1},{4,6},{6,4},{5,7},{7,5},{8,10},{10,8},{9,1... | collective-permute-start | bytes 49160 | tf_op jit(solution)/shard_map/ppermute | solution.py:283
  8.6 5.6 %collective-permute-start.5 = (bf16[1024,256]{1,0:T(8,128)(2,1)S(1)}, bf16[1024,256]{1,0:T(8,128)(2,1)S(1)}, u32[]{:S(2)}, u32[]{:S(2)}) collective-permute-start(bf16[1024,256]{1,0:T(8,128)(2,1)S(1)} %get-tuple-element.34.refs_0_), channel_id=1, source_target_pairs={{0,8},{1,9},{2,10},{3,11},{16,24},{17,25},{18,26},{19,27}} | collective-permute-start | bytes 1572872 | tf_op jit(solution)/shard_map/ppermute | solution.py:263
  14.6 2.2 %collective-permute-start.6 = (bf16[1040,256]{1,0:T(8,128)(2,1)S(1)}, bf16[1040,256]{1,0:T(8,128)(2,1)S(1)}, u32[]{:S(2)}, u32[]{:S(2)}) collective-permute-start(bf16[1040,256]{1,0:T(8,128)(2,1)S(1)} %get-tuple-element.29), channel_id=1, source_target_pairs={{0,8},{1,9},{2,10},{3,11},{16,24},{17,25},{18,26},{19,27}} | collective-permute-start | bytes 1597448 | tf_op jit(solution)/shard_map/ppermute | solution.py:263
  16.9 1.3 %collective-permute-start.1 = (bf16[1040,256]{1,0:T(8,128)(2,1)S(1)}, bf16[1040,256]{1,0:T(8,128)(2,1)S(1)}, u32[]{:S(2)}, u32[]{:S(2)}) collective-permute-start(bf16[1040,256]{1,0:T(8,128)(2,1)S(1)} %get-tuple-element.29), channel_id=1, source_target_pairs={{4,0},{8,4},{12,8},{5,1},{9,5},{13,9},{6,2},{10,6},{14,10},{7,3},{... | collective-permute-start | bytes 1597448 | tf_op jit(solution)/shard_map/ppermute | solution.py:263
  18.2 3.7 %collective-permute-done.3.refs_3_.refs_1_ = bf16[1024,256]{1,0:T(8,128)(2,1)S(1)} collective-permute-done((bf16[1024,256]{1,0:T(8,128)(2,1)S(1)}, bf16[1024,256]{1,0:T(8,128)(2,1)S(1)}, u32[]{:S(2)}, u32[]{:S(2)}) %collective-permute-start.3) | collective-permute-done | bytes 524320 | tf_op jit(solution)/shard_map/ppermute | solution.py:263
  21.9 1.0 %gather0.1 = (bf16[1024,1024]{1,0:T(8,128)(2,1)S(1)}, bf16[512,512]{1,0:T(8,128)(2,1)S(1)}) custom-call(bf16[1024,512]{1,0:T(8,128)(2,1)S(1)} %get-tuple-element.30.refs_0_.refs_2_.refs_1_, bf16[1024,512]{1,0:T(8,128)(2,1)S(1)} %collective-permute-done.2.refs_1_, bf16[1024,512]{1,0:T(8,128)(2,1)S(1)} %get-tuple-element.30.refs_0_.refs_2_.refs_1_, ...), custom_call_target="tpu_custom_call" | custom-call | tf_op jit(solution)/shard_map/gather0/pallas_call | solution.py:64
  22.9 2.0 %collective-permute-start.4 = (bf16[512,512]{1,0:T(8,128)(2,1)S(1)}, bf16[512,512]{1,0:T(8,128)(2,1)S(1)}, u32[]{:S(2)}, u32[]{:S(2)}) collective-permute-start(bf16[512,512]{1,0:T(8,128)(2,1)S(1)} %get-tuple-element.33), channel_id=1, source_target_pairs={{0,2},{2,0},{1,3},{3,1},{4,6},{6,4},{5,7},{7,5},{8,10},{10,8},{9,1... | collective-permute-start | bytes 1572872 | tf_op jit(solution)/shard_map/ppermute | solution.py:283
  25.0 7.6 %collective-permute-done.1.refs_2_ = bf16[1040,256]{1,0:T(8,128)(2,1)S(1)} collective-permute-done((bf16[1040,256]{1,0:T(8,128)(2,1)S(1)}, bf16[1040,256]{1,0:T(8,128)(2,1)S(1)}, u32[]{:S(2)}, u32[]{:S(2)}) %collective-permute-start.1) | collective-permute-done | bytes 532512 | tf_op jit(solution)/shard_map/ppermute | solution.py:263
  32.5 1.3 %collective-permute-start.10 = (bf16[1040,256]{1,0:T(8,128)(2,1)S(1)}, bf16[1040,256]{1,0:T(8,128)(2,1)S(1)}, u32[]{:S(2)}, u32[]{:S(2)}) collective-permute-start(bf16[1040,256]{1,0:T(8,128)(2,1)S(1)} %collective-permute-done.1.refs_2_), channel_id=1, source_target_pairs={{4,0},{8,4},{5,1},{9,5},{6,2},{10,6},{7,3},{11,7},{20,16},{24,20},... | collective-permute-start | bytes 1597448 | tf_op jit(solution)/shard_map/ppermute | solution.py:263
  34.6 1.5 %collective-permute-done.6.refs_1_ = bf16[1040,256]{1,0:T(8,128)(2,1)S(1)} collective-permute-done((bf16[1040,256]{1,0:T(8,128)(2,1)S(1)}, bf16[1040,256]{1,0:T(8,128)(2,1)S(1)}, u32[]{:S(2)}, u32[]{:S(2)}) %collective-permute-start.6) | collective-permute-done | bytes 532512 | tf_op jit(solution)/shard_map/ppermute | solution.py:263
  37.0 1.3 %collective-permute-start.13 = (bf16[1024,256]{1,0:T(8,128)(2,1)S(1)}, bf16[1024,256]{1,0:T(8,128)(2,1)S(1)}, u32[]{:S(2)}, u32[]{:S(2)}) collective-permute-start(bf16[1024,256]{1,0:T(8,128)(2,1)S(1)} %get-tuple-element.41), channel_id=1, source_target_pairs={{4,0},{8,4},{5,1},{9,5},{6,2},{10,6},{7,3},{11,7},{20,16},{24,20},... | collective-permute-start | bytes 1572872 | tf_op jit(solution)/shard_map/ppermute | solution.py:263
  40.8 8.6 %collective-permute-done.10.refs_1_ = bf16[1040,256]{1,0:T(8,128)(2,1)S(1)} collective-permute-done((bf16[1040,256]{1,0:T(8,128)(2,1)S(1)}, bf16[1040,256]{1,0:T(8,128)(2,1)S(1)}, u32[]{:S(2)}, u32[]{:S(2)}) %collective-permute-start.10) | collective-permute-done | bytes 532512 | tf_op jit(solution)/shard_map/ppermute | solution.py:263
  50.0 1.7 %collective-permute-start.12 = (bf16[512,256]{1,0:T(8,128)(2,1)S(1)}, bf16[512,256]{1,0:T(8,128)(2,1)S(1)}, u32[]{:S(2)}, u32[]{:S(2)}) collective-permute-start(bf16[512,256]{1,0:T(8,128)(2,1)S(1)} %far_b.1.refs_0_), channel_id=1, source_target_pairs={{0,2},{2,0},{1,3},{3,1},{4,6},{6,4},{5,7},{7,5},{8,10},{10,8},{9,1... | collective-permute-start | bytes 786440 | tf_op jit(solution)/shard_map/ppermute | solution.py:283
  52.9 1.3 %collective-permute-start.15 = (bf16[512,512]{1,0:T(8,128)(2,1)S(1)}, bf16[512,512]{1,0:T(8,128)(2,1)S(1)}, u32[]{:S(2)}, u32[]{:S(2)}) collective-permute-start(bf16[512,512]{1,0:T(8,128)(2,1)S(1)} %total3.1), channel_id=1, source_target_pairs={{8,0},{9,1},{10,2},{11,3},{24,16},{25,17},{26,18},{27,19}} | collective-permute-start | bytes 1572872 | tf_op jit(solution)/shard_map/ppermute | solution.py:263
  54.2 4.4 %collective-permute-done.13.refs_1_ = bf16[1024,256]{1,0:T(8,128)(2,1)S(1)} collective-permute-done((bf16[1024,256]{1,0:T(8,128)(2,1)S(1)}, bf16[1024,256]{1,0:T(8,128)(2,1)S(1)}, u32[]{:S(2)}, u32[]{:S(2)}) %collective-permute-start.13) | collective-permute-done | bytes 524320 | tf_op jit(solution)/shard_map/ppermute | solution.py:263
  59.1 3.6 %collective-permute-start.14 = (bf16[512,256]{1,0:T(8,128)(2,1)S(1)}, bf16[512,256]{1,0:T(8,128)(2,1)S(1)}, u32[]{:S(2)}, u32[]{:S(2)}) collective-permute-start(bf16[512,256]{1,0:T(8,128)(2,1)S(1)} %far_a.1.refs_3_), channel_id=1, source_target_pairs={{0,2},{2,0},{4,6},{6,4},{1,3},{3,1},{5,7},{7,5},{16,18},{18,16},{2... | collective-permute-start | bytes 786440 | tf_op jit(solution)/shard_map/ppermute | solution.py:290
  63.3 5.0 %collective-permute-done.11.refs_2_ = bf16[512,512]{1,0:T(8,128)(2,1)S(1)} collective-permute-done((bf16[512,512]{1,0:T(8,128)(2,1)S(1)}, bf16[512,512]{1,0:T(8,128)(2,1)S(1)}, u32[]{:S(2)}, u32[]{:S(2)}) %collective-permute-start.11) | collective-permute-done | bytes 524320 | tf_op jit(solution)/shard_map/ppermute | solution.py:283
  69.1 2.0 %collective-permute-done.14.refs_2_ = bf16[512,256]{1,0:T(8,128)(2,1)S(1)} collective-permute-done((bf16[512,256]{1,0:T(8,128)(2,1)S(1)}, bf16[512,256]{1,0:T(8,128)(2,1)S(1)}, u32[]{:S(2)}, u32[]{:S(2)}) %collective-permute-start.14) | collective-permute-done | bytes 262176 | tf_op jit(solution)/shard_map/ppermute | solution.py:290
  71.6 1.8 %collective-permute-done.15.fourth = bf16[512,512]{1,0:T(8,128)(2,1)S(1)} collective-permute-done((bf16[512,512]{1,0:T(8,128)(2,1)S(1)}, bf16[512,512]{1,0:T(8,128)(2,1)S(1)}, u32[]{:S(2)}, u32[]{:S(2)}) %collective-permute-start.15) | collective-permute-done | bytes 524320 | tf_op jit(solution)/shard_map/ppermute | solution.py:263
  73.4 1.9 %interleave.1 = bf16[512,4,512]{2,1,0:T(4,128)(2,1)} custom-call(bf16[512,512]{1,0:T(8,128)(2,1)S(1)} %total0.1.refs_0_.first, bf16[512,512]{1,0:T(8,128)(2,1)S(1)} %total1.1.refs_3_.second, bf16[512,256]{1,0:T(8,128)(2,1)S(1)} %total2a.1.third_a, bf16[512,256]{1,0:T(8,128)(2,1)S(1)} %total2b.1.refs_0_.third_b, ...), custom_call_target="tpu_custom_call" | custom-call | tf_op jit(solution)/shard_map/interleave/pallas_call | solution.py:160
  (33 shorter events, 8.8 us)
Async XLA Ops:
  0.0 1.6 %copy-start = (s32[1024,512]{1,0:T(8,128)S(1)}, s32[1024,512]{1,0:T(8,128)}, u32[]{:S(2)}) copy-start(s32[1024,512]{1,0:T(8,128)} %refs_0_.1) | copy-start | bytes 6291460
  1.6 1.6 %copy-start.1 = (s32[1024,512]{1,0:T(8,128)S(1)}, s32[1024,512]{1,0:T(8,128)}, u32[]{:S(2)}) copy-start(s32[1024,512]{1,0:T(8,128)} %refs_1_.1) | copy-start | bytes 6291460
  4.3 17.7 %collective-permute-start.3 = (bf16[1024,256]{1,0:T(8,128)(2,1)S(1)}, bf16[1024,256]{1,0:T(8,128)(2,1)S(1)}, u32[]{:S(2)}, u32[]{:S(2)}) collective-permute-start(bf16[1024,256]{1,0:T(8,128)(2,1)S(1)} %get-tuple-element.34.refs_0_), channel_id=1, source_target_pairs={{4,0},{8,4},{12,8},{5,1},{9,5},{13,9},{6,2},{10,6},{14,10},{7,3},{... | collective-permute-start | bytes 1572872 | tf_op jit(solution)/shard_map/ppermute | solution.py:263
  5.6 8.6 %collective-permute-start = (s32[8,512]{1,0:T(8,128)S(1)}, s32[8,512]{1,0:T(8,128)S(1)}, u32[]{:S(2)}, u32[]{:S(2)}) collective-permute-start(s32[8,512]{1,0:T(8,128)S(1)} %get-tuple-element.27.refs_2_), channel_id=1, source_target_pairs={{0,2},{2,0},{1,3},{3,1},{4,6},{6,4},{5,7},{7,5},{8,10},{10,8},{9,1... | collective-permute-start | bytes 49160 | tf_op jit(solution)/shard_map/ppermute | solution.py:283
  8.6 26.0 %collective-permute-start.5 = (bf16[1024,256]{1,0:T(8,128)(2,1)S(1)}, bf16[1024,256]{1,0:T(8,128)(2,1)S(1)}, u32[]{:S(2)}, u32[]{:S(2)}) collective-permute-start(bf16[1024,256]{1,0:T(8,128)(2,1)S(1)} %get-tuple-element.34.refs_0_), channel_id=1, source_target_pairs={{0,8},{1,9},{2,10},{3,11},{16,24},{17,25},{18,26},{19,27}} | collective-permute-start | bytes 1572872 | tf_op jit(solution)/shard_map/ppermute | solution.py:263
  14.6 21.5 %collective-permute-start.6 = (bf16[1040,256]{1,0:T(8,128)(2,1)S(1)}, bf16[1040,256]{1,0:T(8,128)(2,1)S(1)}, u32[]{:S(2)}, u32[]{:S(2)}) collective-permute-start(bf16[1040,256]{1,0:T(8,128)(2,1)S(1)} %get-tuple-element.29), channel_id=1, source_target_pairs={{0,8},{1,9},{2,10},{3,11},{16,24},{17,25},{18,26},{19,27}} | collective-permute-start | bytes 1597448 | tf_op jit(solution)/shard_map/ppermute | solution.py:263
  16.9 15.7 %collective-permute-start.1 = (bf16[1040,256]{1,0:T(8,128)(2,1)S(1)}, bf16[1040,256]{1,0:T(8,128)(2,1)S(1)}, u32[]{:S(2)}, u32[]{:S(2)}) collective-permute-start(bf16[1040,256]{1,0:T(8,128)(2,1)S(1)} %get-tuple-element.29), channel_id=1, source_target_pairs={{4,0},{8,4},{12,8},{5,1},{9,5},{13,9},{6,2},{10,6},{14,10},{7,3},{... | collective-permute-start | bytes 1597448 | tf_op jit(solution)/shard_map/ppermute | solution.py:263
  18.2 3.8 %collective-permute-start.2 = (bf16[1024,512]{1,0:T(8,128)(2,1)S(1)}, bf16[1024,512]{1,0:T(8,128)(2,1)S(1)}, u32[]{:S(2)}, u32[]{:S(2)}) collective-permute-start(bf16[1024,512]{1,0:T(8,128)(2,1)S(1)} %get-tuple-element.30.refs_0_.refs_2_.refs_1_), channel_id=1, source_target_pairs={{0,1},{1,0},{2,3},{3,2},{4,5},{5,4},{6,7},{7,6},{8,9},{9,8},{10,11... | collective-permute-start | bytes 3145736 | tf_op jit(solution)/shard_map/ppermute | solution.py:283
  22.9 15.3 %collective-permute-start.4 = (bf16[512,512]{1,0:T(8,128)(2,1)S(1)}, bf16[512,512]{1,0:T(8,128)(2,1)S(1)}, u32[]{:S(2)}, u32[]{:S(2)}) collective-permute-start(bf16[512,512]{1,0:T(8,128)(2,1)S(1)} %get-tuple-element.33), channel_id=1, source_target_pairs={{0,2},{2,0},{1,3},{3,1},{4,6},{6,4},{5,7},{7,5},{8,10},{10,8},{9,1... | collective-permute-start | bytes 1572872 | tf_op jit(solution)/shard_map/ppermute | solution.py:283
  32.5 16.9 %collective-permute-start.10 = (bf16[1040,256]{1,0:T(8,128)(2,1)S(1)}, bf16[1040,256]{1,0:T(8,128)(2,1)S(1)}, u32[]{:S(2)}, u32[]{:S(2)}) collective-permute-start(bf16[1040,256]{1,0:T(8,128)(2,1)S(1)} %collective-permute-done.1.refs_2_), channel_id=1, source_target_pairs={{4,0},{8,4},{5,1},{9,5},{6,2},{10,6},{7,3},{11,7},{20,16},{24,20},... | collective-permute-start | bytes 1597448 | tf_op jit(solution)/shard_map/ppermute | solution.py:263
  36.4 2.7 %collective-permute-start.8 = (bf16[512,512]{1,0:T(8,128)(2,1)S(1)}, bf16[512,512]{1,0:T(8,128)(2,1)S(1)}, u32[]{:S(2)}, u32[]{:S(2)}) collective-permute-start(bf16[512,512]{1,0:T(8,128)(2,1)S(1)} %get-tuple-element.43), channel_id=1, source_target_pairs={{0,1},{1,0},{2,3},{3,2},{4,5},{5,4},{6,7},{7,6},{8,9},{9,8},{10,11... | collective-permute-start | bytes 1572872 | tf_op jit(solution)/shard_map/ppermute | solution.py:283
  36.5 2.6 %collective-permute-start.7 = (bf16[512,512]{1,0:T(8,128)(2,1)S(1)}, bf16[512,512]{1,0:T(8,128)(2,1)S(1)}, u32[]{:S(2)}, u32[]{:S(2)}) collective-permute-start(bf16[512,512]{1,0:T(8,128)(2,1)S(1)} %get-tuple-element.44), channel_id=1, source_target_pairs={{0,1},{1,0},{2,3},{3,2},{4,5},{5,4},{6,7},{7,6},{8,9},{9,8},{10,11... | collective-permute-start | bytes 1572872 | tf_op jit(solution)/shard_map/ppermute | solution.py:283
  37.0 21.6 %collective-permute-start.13 = (bf16[1024,256]{1,0:T(8,128)(2,1)S(1)}, bf16[1024,256]{1,0:T(8,128)(2,1)S(1)}, u32[]{:S(2)}, u32[]{:S(2)}) collective-permute-start(bf16[1024,256]{1,0:T(8,128)(2,1)S(1)} %get-tuple-element.41), channel_id=1, source_target_pairs={{4,0},{8,4},{5,1},{9,5},{6,2},{10,6},{7,3},{11,7},{20,16},{24,20},... | collective-permute-start | bytes 1572872 | tf_op jit(solution)/shard_map/ppermute | solution.py:263
  40.1 11.5 %collective-permute-start.9 = (bf16[512,512]{1,0:T(8,128)(2,1)S(1)}, bf16[512,512]{1,0:T(8,128)(2,1)S(1)}, u32[]{:S(2)}, u32[]{:S(2)}) collective-permute-start(bf16[512,512]{1,0:T(8,128)(2,1)S(1)} %get-tuple-element.39), channel_id=1, source_target_pairs={{8,10},{10,8},{9,11},{11,9},{24,26},{26,24},{25,27},{27,25}} | collective-permute-start | bytes 1572872 | tf_op jit(solution)/shard_map/ppermute | solution.py:290
  50.0 12.7 %collective-permute-start.12 = (bf16[512,256]{1,0:T(8,128)(2,1)S(1)}, bf16[512,256]{1,0:T(8,128)(2,1)S(1)}, u32[]{:S(2)}, u32[]{:S(2)}) collective-permute-start(bf16[512,256]{1,0:T(8,128)(2,1)S(1)} %far_b.1.refs_0_), channel_id=1, source_target_pairs={{0,2},{2,0},{1,3},{3,1},{4,6},{6,4},{5,7},{7,5},{8,10},{10,8},{9,1... | collective-permute-start | bytes 786440 | tf_op jit(solution)/shard_map/ppermute | solution.py:283
  52.5 15.8 %collective-permute-start.11 = (bf16[512,512]{1,0:T(8,128)(2,1)S(1)}, bf16[512,512]{1,0:T(8,128)(2,1)S(1)}, u32[]{:S(2)}, u32[]{:S(2)}) collective-permute-start(bf16[512,512]{1,0:T(8,128)(2,1)S(1)} %get-tuple-element.40.refs_2_), channel_id=1, source_target_pairs={{0,2},{2,0},{1,3},{3,1},{4,6},{6,4},{5,7},{7,5},{8,10},{10,8},{9,1... | collective-permute-start | bytes 1572872 | tf_op jit(solution)/shard_map/ppermute | solution.py:283
  52.9 20.4 %collective-permute-start.15 = (bf16[512,512]{1,0:T(8,128)(2,1)S(1)}, bf16[512,512]{1,0:T(8,128)(2,1)S(1)}, u32[]{:S(2)}, u32[]{:S(2)}) collective-permute-start(bf16[512,512]{1,0:T(8,128)(2,1)S(1)} %total3.1), channel_id=1, source_target_pairs={{8,0},{9,1},{10,2},{11,3},{24,16},{25,17},{26,18},{27,19}} | collective-permute-start | bytes 1572872 | tf_op jit(solution)/shard_map/ppermute | solution.py:263
  59.1 11.9 %collective-permute-start.14 = (bf16[512,256]{1,0:T(8,128)(2,1)S(1)}, bf16[512,256]{1,0:T(8,128)(2,1)S(1)}, u32[]{:S(2)}, u32[]{:S(2)}) collective-permute-start(bf16[512,256]{1,0:T(8,128)(2,1)S(1)} %far_a.1.refs_3_), channel_id=1, source_target_pairs={{0,2},{2,0},{4,6},{6,4},{1,3},{3,1},{5,7},{7,5},{16,18},{18,16},{2... | collective-permute-start | bytes 786440 | tf_op jit(solution)/shard_map/ppermute | solution.py:290

commit v5 on v4

--- a/solution.py
+++ b/solution.py
@@ -182,8 +182,24 @@
         ref[...] = product(whole, cols, d + 1).astype(jnp.bfloat16)
 
 
-def gather_body(n_sub, n_held, *refs):
-    held, cols, whole, parts = refs[:n_held], refs[n_held], refs[n_held + 1], refs[n_held + 2:]
+def holds_three():
+    place = lax.axis_index("var")
+    return jnp.logical_and(place >= 2, place + 1 < lax.axis_size("var"))
+
+
+def choose(condition, when_true, when_false):
+    pl.when(condition)(when_true)
+    pl.when(jnp.logical_not(condition))(when_false)
+
+
+def copy_parts(spare, parts):
+    for source, ref in zip(spare, parts):
+        ref[...] = source[...]
+
+
+def gather_body(n_sub, n_held, n_spare, *refs):
+    held, (cols, *rest) = refs[:n_held], refs[n_held:]
+    spare, whole, parts = rest[:n_spare], rest[n_spare], rest[n_spare + 1:]
     width = held[0].shape[1]
     pieces = (n_held - 1) // (n_sub - 1)
     count = whole.shape[0] // pieces
@@ -197,7 +213,14 @@
     for d in range(1, n_sub):
         for i in range(pieces):
             whole[i * count:(i + 1) * count, span(d)] = held[1 + (d - 1) * pieces + i][...]
-    send_parts(whole, cols[...], parts)
+    if not spare:
+        send_parts(whole, cols[...], parts)
+        return
+    choose(
+        holds_three(),
+        lambda: send_parts(whole, cols[...], parts),
+        lambda: copy_parts(spare, parts),
+    )
 
 
 def from_tail(tail):
@@ -217,16 +240,52 @@
     send_parts(whole, cols[...], parts)
 
 
-def far_body(whole, cols, *parts):
-    send_parts(whole, cols[:whole.shape[0]], parts)
+def far_body(begin, n_spare, whole, cols, *refs):
+    spare, parts = refs[:n_spare], refs[n_spare:]
+
+    def own():
+        send_parts(whole, cols[:whole.shape[0]], parts)
+
+    if not spare:
+        own()
+        return
+    span = slice(begin, begin + cols.shape[1])
+    choose(holds_three(), lambda: copy_parts([r.at[:, span] for r in spare], parts), own)
+
+
+def summed(whole, cols, arrived):
+    total = product(whole, cols, 0).astype(jnp.bfloat16).astype(jnp.float32)
+    for part in arrived:
+        total = total + part.astype(jnp.float32)
+    return total.astype(jnp.bfloat16)
 
 
 def total_body(whole, cols, *refs):
     *arrived, out = refs
-    total = product(whole, cols[:whole.shape[0]], 0).astype(jnp.bfloat16).astype(jnp.float32)
-    for ref in arrived:
-        total = total + ref[...].astype(jnp.float32)
-    out[...] = total.astype(jnp.bfloat16)
+    out[...] = summed(whole, cols[:whole.shape[0]], [r[...] for r in arrived])
+
+
+def total_or_none_body(whole, cols, *refs):
+    out = refs[-1]
+
+    def none():
+        out[...] = jnp.zeros_like(out)
+
+    choose(holds_three(), none, lambda: total_body(whole, cols, *refs))
+
+
+def total_near_body(n_parts, whole, cols, *refs):
+    first, later, out = refs[:n_parts], refs[n_parts:-1], refs[-1]
+
+    def displaced():
+        begin = 0
+        for i in range(0, len(later), n_parts):
+            group = later[i:i + n_parts]
+            span = slice(begin, begin + group[0].shape[1])
+            out[:, span] = summed(whole, cols[:, span], [r[...] for r in group])
+            begin = span.stop
+
+    choose(holds_three(), displaced, lambda: total_body(whole, cols, *first, out))
 
 
 def fence_body(*refs):
@@ -271,11 +330,13 @@
     def up_two(x):
         return along(x, 2, lambda i: i + 3 < n_var)
 
-    def holds_three(i):
+    def holds(i):
         return i >= 2 and i + 1 < n_var
 
+    shared = not any(holds(i) and i + 2 < n_var for i in range(n_var))
+
     def down_two(x):
-        return along(x, -2, holds_three)
+        return along(x, -2, holds)
 
     def swapped(x, axis, distance, keep=None):
         n = lax.axis_size(axis)
@@ -300,16 +361,22 @@
     def part_shapes(columns):
         return [((rows_owned, columns), jnp.bfloat16)] * (n_smp - 1)
 
-    def gather(part, others, cols, name, events):
+    def gather(part, others, cols, name, events, spare=()):
         block = ((samples, width * n_sub), jnp.bfloat16)
-        body = functools.partial(gather_body, n_sub, 1 + len(others))
+        body = functools.partial(gather_body, n_sub, 1 + len(others), len(spare))
         shapes = [block] + part_shapes(width)
-        whole, *parts = call(body, name, shapes, [part, *others, cols], events=events)
+        inputs = [part, *others, cols, *spare]
+        whole, *parts = call(body, name, shapes, inputs, events=events)
         return whole, parts
 
-    def total(whole, cols, arrived, name, events):
+    def far_parts(cols, begin, name, events):
+        spare = part1 if shared else []
+        body = functools.partial(far_body, begin, len(spare))
+        return call(body, name, part_shapes(width // 2), [whole, cols, *spare], events=events)
+
+    def total(whole, cols, arrived, name, events, body=total_body):
         shape = ((rows_owned, cols.shape[1]), jnp.bfloat16)
-        return call(total_body, name, [shape], [whole, cols, *arrived], events=events)[0]
+        return call(body, name, [shape], [whole, cols, *arrived], events=events)[0]
 
     first, second, sums_own = encode(dosages, observed)
     near_a = down(first)
@@ -344,23 +411,31 @@
     )
     others3 = others_of(rows3, 2)
     panel0 = total(whole, own, got0, "total0", [rows3])
-    whole3, part3 = gather(rows3, others3, cols1, "gather3", [fence(3, panel0)])
-    got3 = sent(part3, holds_three)
-    part2_b = call(far_body, "far_b", part_shapes(width // 2), [whole, far_b], events=[whole3])
+    whole3, part3 = gather(rows3, others3, cols1, "gather3", [fence(3, panel0)], part1)
+    got3 = sent(part3)
+    part2_b = far_parts(far_b, width // 2, "far_b", [whole3])
     got2_b = sent(part2_b)
-    step = fence(12, *part2_b)
-    panel3 = total(whole3, cols1, got3, "total3", [step])
-    *part1, panel3 = together(*part1, panel3)
-    got1 = sent(part1)
+    panel3 = total(whole3, cols1, got3, "total3", [fence(12, *part2_b)])
+    later = []
+    if not shared:
+        *part1, panel3 = together(*part1, panel3)
+        later = sent(part1, holds)
+    part2_a = far_parts(far_a, 0, "far_a", [panel3])
     panel3 = down_two(panel3)
-    part2_a = call(
-        far_body, "far_a", part_shapes(width // 2), [whole, far_a], events=[*part1]
-    )
-    got2_a = sent(part2_a, lambda v: v + 2 < n_var)
-    panel2_b = total(whole, far_b, got2_b, "total2b", [*part2_a])
-    step = fence(3, panel2_b)
-    panel1 = total(whole, cols1, got1, "total1", [step])
-    panel2_a = total(whole, far_a, got2_a, "total2a", [panel1])
+    got2_a = sent(part2_a)
+    if shared:
+        later = got2_a + got2_b
+    ending = total_or_none_body if shared else total_body
+    panel2_b = total(whole, far_b, got2_b, "total2b", [*part2_a], ending)
+    panel1 = total(
+        whole,
+        cols1,
+        got3 + later,
+        "total1",
+        [fence(3, panel2_b)],
+        functools.partial(total_near_body, n_smp - 1),
+    )
+    panel2_a = total(whole, far_a, got2_a, "total2a", [panel1], ending)
     return interleave([panel0, panel1, panel2_a, panel2_b, panel3])
 
 

time: 75.8 us -> 73.2 us (0.966)
  starting transfers between devices: 26.3 us -> 23.9 us
  Pallas kernels: 10.8 us -> 10 us
  waiting for transfers between devices: 34.6 us -> 35.4 us
    ppermute x2 -> x0, starting transfers between devices: 4.25 us -> none  [swapped(): return lax.ppermute(x, ('var', axis), route)]
    ppermute x2 -> x0, waiting for transfers between devices: 2.01 us -> none  [swapped(): return lax.ppermute(x, ('var', axis), route)]
    ppermute x7 -> x8, starting transfers between devices: 7.81 us -> 9.68 us  [swapped(): return lax.ppermute(x, axis, [(i, (i + distance) % n) for i in range(n)])]
    ppermute x7 -> x8, waiting for transfers between devices: 5.05 us -> 6.71 us  [swapped(): return lax.ppermute(x, axis, [(i, (i + distance) % n) for i in range(n)])]
    ppermute x7, waiting for transfers between devices: 27.5 us -> 28.7 us  [along(): return lax.ppermute(x, 'var', route)]
    pallas_call x13, Pallas kernels: 8.95 us -> 8.15 us  [call(): pl.pallas_call(with_events, in_specs=[pl.BlockSpec(memory_space=place)] *...]
  transfers between devices with their start and end apart: 16 -> 15, of which waited for: 8 -> 8; matrix products, arithmetic and copies ran while one was open for 0% -> 0% of each run, Pallas kernels for 11% -> 10%
where the time goes in v5:
time: 73.2 us; the launch traced here: 72.9 us
  waiting for transfers between devices  35.4 us (48%)
  starting transfers between devices  23.9 us (33%)
  Pallas kernels  10 us (14%)
  local copies, waits for them, and re-layouts  3.25 us (4%)
    ppermute x7, waiting for transfers between devices, along(): return lax.ppermute(x, 'var', route)  28.7 us
    ppermute x7, starting transfers between devices, along(): return lax.ppermute(x, 'var', route)  14.2 us
    ppermute x8, starting transfers between devices, swapped(): return lax.ppermute(x, axis, [(i, (i + distance) % n) for i in range(n)])  9.68 us
    pallas_call x13, Pallas kernels, call(): pl.pallas_call(with_events, in_specs=[pl.BlockSpec(memory_space=place)] *...  8.15 us
    ppermute x8, waiting for transfers between devices, swapped(): return lax.ppermute(x, axis, [(i, (i + distance) % n) for i in range(n)])  6.71 us
    unnamed x4, local copies, waits for them, and re-layouts  3.18 us
    pallas_call x1, Pallas kernels, interleave(): pl.pallas_call(interleave_body, grid=(rows // tile,), in_specs=[pl.BlockS...  1.87 us
  transfers between devices with their start and end apart: 15, of which 8 were waited for; matrix products, arithmetic and copies ran while one was open for 0% of the time, Pallas kernels for 10%

profile of v5, /device:TPU:0, one launch (start us, length us, event | category | flops | bytes accessed | tf_op | source)
XLA Modules:
  0.0 72.9 jit_solution(3934544172757189917)
XLA Ops:
  0.0 1.6 %copy-done = s32[1024,512]{1,0:T(8,128)S(1)} copy-done((s32[1024,512]{1,0:T(8,128)S(1)}, s32[1024,512]{1,0:T(8,128)}, u32[]{:S(2)}) %copy-start) | copy-done | bytes 2097176
  1.6 1.6 %copy-done.1 = s32[1024,512]{1,0:T(8,128)S(1)} copy-done((s32[1024,512]{1,0:T(8,128)S(1)}, s32[1024,512]{1,0:T(8,128)}, u32[]{:S(2)}) %copy-start.1) | copy-done | bytes 2097176
  3.2 1.1 %encode.1 = (bf16[1024,256]{1,0:T(8,128)(2,1)S(1)}, bf16[1024,256]{1,0:T(8,128)(2,1)S(1)}, s32[8,512]{1,0:T(8,128)S(1)}) custom-call(s32[1024,512]{1,0:T(8,128)S(1)} %copy-done, s32[1024,512]{1,0:T(8,128)S(1)} %copy-done.1), custom_call_target="tpu_custom_call" | custom-call | tf_op jit(solution)/shard_map/encode/pallas_call | solution.py:64
  4.3 1.3 %collective-permute-start.3 = (bf16[1024,256]{1,0:T(8,128)(2,1)S(1)}, bf16[1024,256]{1,0:T(8,128)(2,1)S(1)}, u32[]{:S(2)}, u32[]{:S(2)}) collective-permute-start(bf16[1024,256]{1,0:T(8,128)(2,1)S(1)} %get-tuple-element.32.refs_0_), channel_id=1, source_target_pairs={{4,0},{8,4},{12,8},{5,1},{9,5},{13,9},{6,2},{10,6},{14,10},{7,3},{... | collective-permute-start | bytes 1572872 | tf_op jit(solution)/shard_map/ppermute | solution.py:322
  5.6 3.0 %collective-permute-start = (s32[8,512]{1,0:T(8,128)S(1)}, s32[8,512]{1,0:T(8,128)S(1)}, u32[]{:S(2)}, u32[]{:S(2)}) collective-permute-start(s32[8,512]{1,0:T(8,128)S(1)} %get-tuple-element.25.refs_2_), channel_id=1, source_target_pairs={{0,2},{2,0},{1,3},{3,1},{4,6},{6,4},{5,7},{7,5},{8,10},{10,8},{9,1... | collective-permute-start | bytes 49160 | tf_op jit(solution)/shard_map/ppermute | solution.py:344
  8.6 5.6 %collective-permute-start.5 = (bf16[1024,256]{1,0:T(8,128)(2,1)S(1)}, bf16[1024,256]{1,0:T(8,128)(2,1)S(1)}, u32[]{:S(2)}, u32[]{:S(2)}) collective-permute-start(bf16[1024,256]{1,0:T(8,128)(2,1)S(1)} %get-tuple-element.32.refs_0_), channel_id=1, source_target_pairs={{0,8},{1,9},{2,10},{3,11},{16,24},{17,25},{18,26},{19,27}} | collective-permute-start | bytes 1572872 | tf_op jit(solution)/shard_map/ppermute | solution.py:322
  14.6 2.2 %collective-permute-start.6 = (bf16[1040,256]{1,0:T(8,128)(2,1)S(1)}, bf16[1040,256]{1,0:T(8,128)(2,1)S(1)}, u32[]{:S(2)}, u32[]{:S(2)}) collective-permute-start(bf16[1040,256]{1,0:T(8,128)(2,1)S(1)} %get-tuple-element.27), channel_id=1, source_target_pairs={{0,8},{1,9},{2,10},{3,11},{16,24},{17,25},{18,26},{19,27}} | collective-permute-start | bytes 1597448 | tf_op jit(solution)/shard_map/ppermute | solution.py:322
  16.9 1.3 %collective-permute-start.1 = (bf16[1040,256]{1,0:T(8,128)(2,1)S(1)}, bf16[1040,256]{1,0:T(8,128)(2,1)S(1)}, u32[]{:S(2)}, u32[]{:S(2)}) collective-permute-start(bf16[1040,256]{1,0:T(8,128)(2,1)S(1)} %get-tuple-element.27), channel_id=1, source_target_pairs={{4,0},{8,4},{12,8},{5,1},{9,5},{13,9},{6,2},{10,6},{14,10},{7,3},{... | collective-permute-start | bytes 1597448 | tf_op jit(solution)/shard_map/ppermute | solution.py:322
  18.2 3.7 %collective-permute-done.3.refs_3_.refs_1_ = bf16[1024,256]{1,0:T(8,128)(2,1)S(1)} collective-permute-done((bf16[1024,256]{1,0:T(8,128)(2,1)S(1)}, bf16[1024,256]{1,0:T(8,128)(2,1)S(1)}, u32[]{:S(2)}, u32[]{:S(2)}) %collective-permute-start.3) | collective-permute-done | bytes 524320 | tf_op jit(solution)/shard_map/ppermute | solution.py:322
  21.9 1.0 %gather0.1 = (bf16[1024,1024]{1,0:T(8,128)(2,1)S(1)}, bf16[512,512]{1,0:T(8,128)(2,1)S(1)}) custom-call(bf16[1024,512]{1,0:T(8,128)(2,1)S(1)} %get-tuple-element.28.refs_0_.refs_2_.refs_1_, bf16[1024,512]{1,0:T(8,128)(2,1)S(1)} %collective-permute-done.2.refs_1_, bf16[1024,512]{1,0:T(8,128)(2,1)S(1)} %get-tuple-element.28.refs_0_.refs_2_.refs_1_, ...), custom_call_target="tpu_custom_call" | custom-call | tf_op jit(solution)/shard_map/gather0/pallas_call | solution.py:64
  22.9 2.0 %collective-permute-start.4 = (bf16[512,512]{1,0:T(8,128)(2,1)S(1)}, bf16[512,512]{1,0:T(8,128)(2,1)S(1)}, u32[]{:S(2)}, u32[]{:S(2)}) collective-permute-start(bf16[512,512]{1,0:T(8,128)(2,1)S(1)} %get-tuple-element.31), channel_id=1, source_target_pairs={{0,2},{2,0},{1,3},{3,1},{4,6},{6,4},{5,7},{7,5},{8,10},{10,8},{9,1... | collective-permute-start | bytes 1572872 | tf_op jit(solution)/shard_map/ppermute | solution.py:344
  25.0 7.6 %collective-permute-done.1.refs_2_ = bf16[1040,256]{1,0:T(8,128)(2,1)S(1)} collective-permute-done((bf16[1040,256]{1,0:T(8,128)(2,1)S(1)}, bf16[1040,256]{1,0:T(8,128)(2,1)S(1)}, u32[]{:S(2)}, u32[]{:S(2)}) %collective-permute-start.1) | collective-permute-done | bytes 532512 | tf_op jit(solution)/shard_map/ppermute | solution.py:322
  32.5 1.3 %collective-permute-start.11 = (bf16[1040,256]{1,0:T(8,128)(2,1)S(1)}, bf16[1040,256]{1,0:T(8,128)(2,1)S(1)}, u32[]{:S(2)}, u32[]{:S(2)}) collective-permute-start(bf16[1040,256]{1,0:T(8,128)(2,1)S(1)} %collective-permute-done.1.refs_2_), channel_id=1, source_target_pairs={{4,0},{8,4},{5,1},{9,5},{6,2},{10,6},{7,3},{11,7},{20,16},{24,20},... | collective-permute-start | bytes 1597448 | tf_op jit(solution)/shard_map/ppermute | solution.py:322
  34.6 1.5 %collective-permute-done.6.refs_1_ = bf16[1040,256]{1,0:T(8,128)(2,1)S(1)} collective-permute-done((bf16[1040,256]{1,0:T(8,128)(2,1)S(1)}, bf16[1040,256]{1,0:T(8,128)(2,1)S(1)}, u32[]{:S(2)}, u32[]{:S(2)}) %collective-permute-start.6) | collective-permute-done | bytes 532512 | tf_op jit(solution)/shard_map/ppermute | solution.py:322
  37.0 1.3 %collective-permute-start.10 = (bf16[1024,256]{1,0:T(8,128)(2,1)S(1)}, bf16[1024,256]{1,0:T(8,128)(2,1)S(1)}, u32[]{:S(2)}, u32[]{:S(2)}) collective-permute-start(bf16[1024,256]{1,0:T(8,128)(2,1)S(1)} %get-tuple-element.37), channel_id=1, source_target_pairs={{4,0},{8,4},{5,1},{9,5},{6,2},{10,6},{7,3},{11,7},{20,16},{24,20},... | collective-permute-start | bytes 1572872 | tf_op jit(solution)/shard_map/ppermute | solution.py:322
  39.9 9.5 %collective-permute-done.11.refs_1_ = bf16[1040,256]{1,0:T(8,128)(2,1)S(1)} collective-permute-done((bf16[1040,256]{1,0:T(8,128)(2,1)S(1)}, bf16[1040,256]{1,0:T(8,128)(2,1)S(1)}, u32[]{:S(2)}, u32[]{:S(2)}) %collective-permute-start.11) | collective-permute-done | bytes 532512 | tf_op jit(solution)/shard_map/ppermute | solution.py:322
  50.0 1.7 %collective-permute-start.13 = (bf16[512,256]{1,0:T(8,128)(2,1)S(1)}, bf16[512,256]{1,0:T(8,128)(2,1)S(1)}, u32[]{:S(2)}, u32[]{:S(2)}) collective-permute-start(bf16[512,256]{1,0:T(8,128)(2,1)S(1)} %far_b.1.refs_0_), channel_id=1, source_target_pairs={{0,2},{2,0},{1,3},{3,1},{4,6},{6,4},{5,7},{7,5},{8,10},{10,8},{9,1... | collective-permute-start | bytes 786440 | tf_op jit(solution)/shard_map/ppermute | solution.py:344
  51.7 2.5 %collective-permute-done.9.refs_2_ = bf16[512,512]{1,0:T(8,128)(2,1)S(1)} collective-permute-done((bf16[512,512]{1,0:T(8,128)(2,1)S(1)}, bf16[512,512]{1,0:T(8,128)(2,1)S(1)}, u32[]{:S(2)}, u32[]{:S(2)}) %collective-permute-start.9) | collective-permute-done | bytes 524320 | tf_op jit(solution)/shard_map/ppermute | solution.py:344
  55.0 1.3 %collective-permute-start.14 = (bf16[512,512]{1,0:T(8,128)(2,1)S(1)}, bf16[512,512]{1,0:T(8,128)(2,1)S(1)}, u32[]{:S(2)}, u32[]{:S(2)}) collective-permute-start(bf16[512,512]{1,0:T(8,128)(2,1)S(1)} %total3.1.refs_3_), channel_id=1, source_target_pairs={{8,0},{9,1},{10,2},{11,3},{24,16},{25,17},{26,18},{27,19}} | collective-permute-start | bytes 1572872 | tf_op jit(solution)/shard_map/ppermute | solution.py:322
  56.3 2.3 %collective-permute-done.10.refs_1_ = bf16[1024,256]{1,0:T(8,128)(2,1)S(1)} collective-permute-done((bf16[1024,256]{1,0:T(8,128)(2,1)S(1)}, bf16[1024,256]{1,0:T(8,128)(2,1)S(1)}, u32[]{:S(2)}, u32[]{:S(2)}) %collective-permute-start.10) | collective-permute-done | bytes 524320 | tf_op jit(solution)/shard_map/ppermute | solution.py:322
  59.1 1.7 %collective-permute-start.12 = (bf16[512,256]{1,0:T(8,128)(2,1)S(1)}, bf16[512,256]{1,0:T(8,128)(2,1)S(1)}, u32[]{:S(2)}, u32[]{:S(2)}) collective-permute-start(bf16[512,256]{1,0:T(8,128)(2,1)S(1)} %far_a.1.refs_3_), channel_id=1, source_target_pairs={{0,2},{2,0},{1,3},{3,1},{4,6},{6,4},{5,7},{7,5},{8,10},{10,8},{9,1... | collective-permute-start | bytes 786440 | tf_op jit(solution)/shard_map/ppermute | solution.py:344
  61.4 4.2 %collective-permute-done.12.refs_3_.refs_2_ = bf16[512,256]{1,0:T(8,128)(2,1)S(1)} collective-permute-done((bf16[512,256]{1,0:T(8,128)(2,1)S(1)}, bf16[512,256]{1,0:T(8,128)(2,1)S(1)}, u32[]{:S(2)}, u32[]{:S(2)}) %collective-permute-start.12) | collective-permute-done | bytes 262176 | tf_op jit(solution)/shard_map/ppermute | solution.py:344
  66.9 4.1 %collective-permute-done.14.fourth = bf16[512,512]{1,0:T(8,128)(2,1)S(1)} collective-permute-done((bf16[512,512]{1,0:T(8,128)(2,1)S(1)}, bf16[512,512]{1,0:T(8,128)(2,1)S(1)}, u32[]{:S(2)}, u32[]{:S(2)}) %collective-permute-start.14) | collective-permute-done | bytes 524320 | tf_op jit(solution)/shard_map/ppermute | solution.py:322
  71.0 1.9 %interleave.1 = bf16[512,4,512]{2,1,0:T(4,128)(2,1)} custom-call(bf16[512,512]{1,0:T(8,128)(2,1)S(1)} %total0.1.refs_0_.first, bf16[512,512]{1,0:T(8,128)(2,1)S(1)} %total1.1.refs_3_.second, bf16[512,256]{1,0:T(8,128)(2,1)S(1)} %total2a.1.third_a, bf16[512,256]{1,0:T(8,128)(2,1)S(1)} %total2b.1.refs_0_.third_b, ...), custom_call_target="tpu_custom_call" | custom-call | tf_op jit(solution)/shard_map/interleave/pallas_call | solution.py:160
  (31 shorter events, 7.5 us)
Async XLA Ops:
  0.0 1.6 %copy-start = (s32[1024,512]{1,0:T(8,128)S(1)}, s32[1024,512]{1,0:T(8,128)}, u32[]{:S(2)}) copy-start(s32[1024,512]{1,0:T(8,128)} %refs_0_.1) | copy-start | bytes 6291460
  1.6 1.6 %copy-start.1 = (s32[1024,512]{1,0:T(8,128)S(1)}, s32[1024,512]{1,0:T(8,128)}, u32[]{:S(2)}) copy-start(s32[1024,512]{1,0:T(8,128)} %refs_1_.1) | copy-start | bytes 6291460
  4.3 17.7 %collective-permute-start.3 = (bf16[1024,256]{1,0:T(8,128)(2,1)S(1)}, bf16[1024,256]{1,0:T(8,128)(2,1)S(1)}, u32[]{:S(2)}, u32[]{:S(2)}) collective-permute-start(bf16[1024,256]{1,0:T(8,128)(2,1)S(1)} %get-tuple-element.32.refs_0_), channel_id=1, source_target_pairs={{4,0},{8,4},{12,8},{5,1},{9,5},{13,9},{6,2},{10,6},{14,10},{7,3},{... | collective-permute-start | bytes 1572872 | tf_op jit(solution)/shard_map/ppermute | solution.py:322
  5.6 8.6 %collective-permute-start = (s32[8,512]{1,0:T(8,128)S(1)}, s32[8,512]{1,0:T(8,128)S(1)}, u32[]{:S(2)}, u32[]{:S(2)}) collective-permute-start(s32[8,512]{1,0:T(8,128)S(1)} %get-tuple-element.25.refs_2_), channel_id=1, source_target_pairs={{0,2},{2,0},{1,3},{3,1},{4,6},{6,4},{5,7},{7,5},{8,10},{10,8},{9,1... | collective-permute-start | bytes 49160 | tf_op jit(solution)/shard_map/ppermute | solution.py:344
  8.6 26.0 %collective-permute-start.5 = (bf16[1024,256]{1,0:T(8,128)(2,1)S(1)}, bf16[1024,256]{1,0:T(8,128)(2,1)S(1)}, u32[]{:S(2)}, u32[]{:S(2)}) collective-permute-start(bf16[1024,256]{1,0:T(8,128)(2,1)S(1)} %get-tuple-element.32.refs_0_), channel_id=1, source_target_pairs={{0,8},{1,9},{2,10},{3,11},{16,24},{17,25},{18,26},{19,27}} | collective-permute-start | bytes 1572872 | tf_op jit(solution)/shard_map/ppermute | solution.py:322
  14.6 21.5 %collective-permute-start.6 = (bf16[1040,256]{1,0:T(8,128)(2,1)S(1)}, bf16[1040,256]{1,0:T(8,128)(2,1)S(1)}, u32[]{:S(2)}, u32[]{:S(2)}) collective-permute-start(bf16[1040,256]{1,0:T(8,128)(2,1)S(1)} %get-tuple-element.27), channel_id=1, source_target_pairs={{0,8},{1,9},{2,10},{3,11},{16,24},{17,25},{18,26},{19,27}} | collective-permute-start | bytes 1597448 | tf_op jit(solution)/shard_map/ppermute | solution.py:322
  16.9 15.7 %collective-permute-start.1 = (bf16[1040,256]{1,0:T(8,128)(2,1)S(1)}, bf16[1040,256]{1,0:T(8,128)(2,1)S(1)}, u32[]{:S(2)}, u32[]{:S(2)}) collective-permute-start(bf16[1040,256]{1,0:T(8,128)(2,1)S(1)} %get-tuple-element.27), channel_id=1, source_target_pairs={{4,0},{8,4},{12,8},{5,1},{9,5},{13,9},{6,2},{10,6},{14,10},{7,3},{... | collective-permute-start | bytes 1597448 | tf_op jit(solution)/shard_map/ppermute | solution.py:322
  18.2 3.8 %collective-permute-start.2 = (bf16[1024,512]{1,0:T(8,128)(2,1)S(1)}, bf16[1024,512]{1,0:T(8,128)(2,1)S(1)}, u32[]{:S(2)}, u32[]{:S(2)}) collective-permute-start(bf16[1024,512]{1,0:T(8,128)(2,1)S(1)} %get-tuple-element.28.refs_0_.refs_2_.refs_1_), channel_id=1, source_target_pairs={{0,1},{1,0},{2,3},{3,2},{4,5},{5,4},{6,7},{7,6},{8,9},{9,8},{10,11... | collective-permute-start | bytes 3145736 | tf_op jit(solution)/shard_map/ppermute | solution.py:344
  22.9 15.3 %collective-permute-start.4 = (bf16[512,512]{1,0:T(8,128)(2,1)S(1)}, bf16[512,512]{1,0:T(8,128)(2,1)S(1)}, u32[]{:S(2)}, u32[]{:S(2)}) collective-permute-start(bf16[512,512]{1,0:T(8,128)(2,1)S(1)} %get-tuple-element.31), channel_id=1, source_target_pairs={{0,2},{2,0},{1,3},{3,1},{4,6},{6,4},{5,7},{7,5},{8,10},{10,8},{9,1... | collective-permute-start | bytes 1572872 | tf_op jit(solution)/shard_map/ppermute | solution.py:344
  32.5 16.9 %collective-permute-start.11 = (bf16[1040,256]{1,0:T(8,128)(2,1)S(1)}, bf16[1040,256]{1,0:T(8,128)(2,1)S(1)}, u32[]{:S(2)}, u32[]{:S(2)}) collective-permute-start(bf16[1040,256]{1,0:T(8,128)(2,1)S(1)} %collective-permute-done.1.refs_2_), channel_id=1, source_target_pairs={{4,0},{8,4},{5,1},{9,5},{6,2},{10,6},{7,3},{11,7},{20,16},{24,20},... | collective-permute-start | bytes 1597448 | tf_op jit(solution)/shard_map/ppermute | solution.py:322
  36.4 2.7 %collective-permute-start.8 = (bf16[512,512]{1,0:T(8,128)(2,1)S(1)}, bf16[512,512]{1,0:T(8,128)(2,1)S(1)}, u32[]{:S(2)}, u32[]{:S(2)}) collective-permute-start(bf16[512,512]{1,0:T(8,128)(2,1)S(1)} %get-tuple-element.39), channel_id=1, source_target_pairs={{0,1},{1,0},{2,3},{3,2},{4,5},{5,4},{6,7},{7,6},{8,9},{9,8},{10,11... | collective-permute-start | bytes 1572872 | tf_op jit(solution)/shard_map/ppermute | solution.py:344
  36.5 2.6 %collective-permute-start.7 = (bf16[512,512]{1,0:T(8,128)(2,1)S(1)}, bf16[512,512]{1,0:T(8,128)(2,1)S(1)}, u32[]{:S(2)}, u32[]{:S(2)}) collective-permute-start(bf16[512,512]{1,0:T(8,128)(2,1)S(1)} %get-tuple-element.40), channel_id=1, source_target_pairs={{0,1},{1,0},{2,3},{3,2},{4,5},{5,4},{6,7},{7,6},{8,9},{9,8},{10,11... | collective-permute-start | bytes 1572872 | tf_op jit(solution)/shard_map/ppermute | solution.py:344
  37.0 21.6 %collective-permute-start.10 = (bf16[1024,256]{1,0:T(8,128)(2,1)S(1)}, bf16[1024,256]{1,0:T(8,128)(2,1)S(1)}, u32[]{:S(2)}, u32[]{:S(2)}) collective-permute-start(bf16[1024,256]{1,0:T(8,128)(2,1)S(1)} %get-tuple-element.37), channel_id=1, source_target_pairs={{4,0},{8,4},{5,1},{9,5},{6,2},{10,6},{7,3},{11,7},{20,16},{24,20},... | collective-permute-start | bytes 1572872 | tf_op jit(solution)/shard_map/ppermute | solution.py:322
  39.3 14.8 %collective-permute-start.9 = (bf16[512,512]{1,0:T(8,128)(2,1)S(1)}, bf16[512,512]{1,0:T(8,128)(2,1)S(1)}, u32[]{:S(2)}, u32[]{:S(2)}) collective-permute-start(bf16[512,512]{1,0:T(8,128)(2,1)S(1)} %get-tuple-element.36), channel_id=1, source_target_pairs={{0,2},{2,0},{1,3},{3,1},{4,6},{6,4},{5,7},{7,5},{8,10},{10,8},{9,1... | collective-permute-start | bytes 1572872 | tf_op jit(solution)/shard_map/ppermute | solution.py:344
  50.0 10.9 %collective-permute-start.13 = (bf16[512,256]{1,0:T(8,128)(2,1)S(1)}, bf16[512,256]{1,0:T(8,128)(2,1)S(1)}, u32[]{:S(2)}, u32[]{:S(2)}) collective-permute-start(bf16[512,256]{1,0:T(8,128)(2,1)S(1)} %far_b.1.refs_0_), channel_id=1, source_target_pairs={{0,2},{2,0},{1,3},{3,1},{4,6},{6,4},{5,7},{7,5},{8,10},{10,8},{9,1... | collective-permute-start | bytes 786440 | tf_op jit(solution)/shard_map/ppermute | solution.py:344
  55.0 16.0 %collective-permute-start.14 = (bf16[512,512]{1,0:T(8,128)(2,1)S(1)}, bf16[512,512]{1,0:T(8,128)(2,1)S(1)}, u32[]{:S(2)}, u32[]{:S(2)}) collective-permute-start(bf16[512,512]{1,0:T(8,128)(2,1)S(1)} %total3.1.refs_3_), channel_id=1, source_target_pairs={{8,0},{9,1},{10,2},{11,3},{24,16},{25,17},{26,18},{27,19}} | collective-permute-start | bytes 1572872 | tf_op jit(solution)/shard_map/ppermute | solution.py:322
  59.1 6.4 %collective-permute-start.12 = (bf16[512,256]{1,0:T(8,128)(2,1)S(1)}, bf16[512,256]{1,0:T(8,128)(2,1)S(1)}, u32[]{:S(2)}, u32[]{:S(2)}) collective-permute-start(bf16[512,256]{1,0:T(8,128)(2,1)S(1)} %far_a.1.refs_3_), channel_id=1, source_target_pairs={{0,2},{2,0},{1,3},{3,1},{4,6},{6,4},{5,7},{7,5},{8,10},{10,8},{9,1... | collective-permute-start | bytes 786440 | tf_op jit(solution)/shard_map/ppermute | solution.py:344

commit v6 on v5

--- a/solution.py
+++ b/solution.py
@@ -87,6 +87,7 @@
             ((8, width), jnp.int32),
         ],
         [dosages, observed],
+        mib=52,
         in_hbm=True,
         scratch=[
             pltpu.VMEM((samples, width), jnp.int32),

time: 73.2 us -> 71.2 us (0.973)
  local copies, waits for them, and re-layouts: 3.25 us -> 0.07 us
  Pallas kernels: 10 us -> 11.3 us
    unnamed x4 -> x0, local copies, waits for them, and re-layouts: 3.18 us -> none
    pallas_call x13, Pallas kernels: 8.15 us -> 9.43 us  [call(): pl.pallas_call(with_events, in_specs=[pl.BlockSpec(memory_space=place)] *...]
where the time goes in v6:
time: 71.2 us; the launch traced here: 71 us
  waiting for transfers between devices  35.4 us (50%)
  starting transfers between devices  23.9 us (34%)
  Pallas kernels  11.3 us (16%)
    ppermute x7, waiting for transfers between devices, along(): return lax.ppermute(x, 'var', route)  28.7 us
    ppermute x7, starting transfers between devices, along(): return lax.ppermute(x, 'var', route)  14.2 us
    ppermute x8, starting transfers between devices, swapped(): return lax.ppermute(x, axis, [(i, (i + distance) % n) for i in range(n)])  9.7 us
    pallas_call x13, Pallas kernels, call(): pl.pallas_call(with_events, in_specs=[pl.BlockSpec(memory_space=place)] *...  9.43 us
    ppermute x8, waiting for transfers between devices, swapped(): return lax.ppermute(x, axis, [(i, (i + distance) % n) for i in range(n)])  6.71 us
    pallas_call x1, Pallas kernels, interleave(): pl.pallas_call(interleave_body, grid=(rows // tile,), in_specs=[pl.BlockS...  1.87 us
  transfers between devices with their start and end apart: 15, of which 8 were waited for; matrix products, arithmetic and copies ran while one was open for 0% of the time, Pallas kernels for 10%

profile of v6, /device:TPU:0, one launch (start us, length us, event | category | flops | bytes accessed | tf_op | source)
XLA Modules:
  0.0 71.0 jit_solution(2928655684090572101)
XLA Ops:
  0.0 2.4 %encode.1 = (bf16[1024,256]{1,0:T(8,128)(2,1)S(1)}, bf16[1024,256]{1,0:T(8,128)(2,1)S(1)}, s32[8,512]{1,0:T(8,128)S(1)}) custom-call(s32[1024,512]{1,0:T(8,128)} %refs_0_.1, s32[1024,512]{1,0:T(8,128)} %refs_1_.1), custom_call_target="tpu_custom_call" | custom-call | tf_op jit(solution)/shard_map/encode/pallas_call | solution.py:64
  2.4 1.3 %collective-permute-start.3 = (bf16[1024,256]{1,0:T(8,128)(2,1)S(1)}, bf16[1024,256]{1,0:T(8,128)(2,1)S(1)}, u32[]{:S(2)}, u32[]{:S(2)}) collective-permute-start(bf16[1024,256]{1,0:T(8,128)(2,1)S(1)} %get-tuple-element.32.refs_0_), channel_id=1, source_target_pairs={{4,0},{8,4},{12,8},{5,1},{9,5},{13,9},{6,2},{10,6},{14,10},{7,3},{... | collective-permute-start | bytes 1572872 | tf_op jit(solution)/shard_map/ppermute | solution.py:323
  3.7 3.0 %collective-permute-start = (s32[8,512]{1,0:T(8,128)S(1)}, s32[8,512]{1,0:T(8,128)S(1)}, u32[]{:S(2)}, u32[]{:S(2)}) collective-permute-start(s32[8,512]{1,0:T(8,128)S(1)} %get-tuple-element.25.refs_2_), channel_id=1, source_target_pairs={{0,2},{2,0},{1,3},{3,1},{4,6},{6,4},{5,7},{7,5},{8,10},{10,8},{9,1... | collective-permute-start | bytes 49160 | tf_op jit(solution)/shard_map/ppermute | solution.py:345
  6.7 5.6 %collective-permute-start.5 = (bf16[1024,256]{1,0:T(8,128)(2,1)S(1)}, bf16[1024,256]{1,0:T(8,128)(2,1)S(1)}, u32[]{:S(2)}, u32[]{:S(2)}) collective-permute-start(bf16[1024,256]{1,0:T(8,128)(2,1)S(1)} %get-tuple-element.32.refs_0_), channel_id=1, source_target_pairs={{0,8},{1,9},{2,10},{3,11},{16,24},{17,25},{18,26},{19,27}} | collective-permute-start | bytes 1572872 | tf_op jit(solution)/shard_map/ppermute | solution.py:323
  12.7 2.2 %collective-permute-start.6 = (bf16[1040,256]{1,0:T(8,128)(2,1)S(1)}, bf16[1040,256]{1,0:T(8,128)(2,1)S(1)}, u32[]{:S(2)}, u32[]{:S(2)}) collective-permute-start(bf16[1040,256]{1,0:T(8,128)(2,1)S(1)} %get-tuple-element.27), channel_id=1, source_target_pairs={{0,8},{1,9},{2,10},{3,11},{16,24},{17,25},{18,26},{19,27}} | collective-permute-start | bytes 1597448 | tf_op jit(solution)/shard_map/ppermute | solution.py:323
  15.0 1.3 %collective-permute-start.1 = (bf16[1040,256]{1,0:T(8,128)(2,1)S(1)}, bf16[1040,256]{1,0:T(8,128)(2,1)S(1)}, u32[]{:S(2)}, u32[]{:S(2)}) collective-permute-start(bf16[1040,256]{1,0:T(8,128)(2,1)S(1)} %get-tuple-element.27), channel_id=1, source_target_pairs={{4,0},{8,4},{12,8},{5,1},{9,5},{13,9},{6,2},{10,6},{14,10},{7,3},{... | collective-permute-start | bytes 1597448 | tf_op jit(solution)/shard_map/ppermute | solution.py:323
  16.4 3.7 %collective-permute-done.3.refs_3_.refs_1_ = bf16[1024,256]{1,0:T(8,128)(2,1)S(1)} collective-permute-done((bf16[1024,256]{1,0:T(8,128)(2,1)S(1)}, bf16[1024,256]{1,0:T(8,128)(2,1)S(1)}, u32[]{:S(2)}, u32[]{:S(2)}) %collective-permute-start.3) | collective-permute-done | bytes 524320 | tf_op jit(solution)/shard_map/ppermute | solution.py:323
  20.0 1.0 %gather0.1 = (bf16[1024,1024]{1,0:T(8,128)(2,1)S(1)}, bf16[512,512]{1,0:T(8,128)(2,1)S(1)}) custom-call(bf16[1024,512]{1,0:T(8,128)(2,1)S(1)} %get-tuple-element.28.refs_0_.refs_2_.refs_1_, bf16[1024,512]{1,0:T(8,128)(2,1)S(1)} %collective-permute-done.2.refs_1_, bf16[1024,512]{1,0:T(8,128)(2,1)S(1)} %get-tuple-element.28.refs_0_.refs_2_.refs_1_, ...), custom_call_target="tpu_custom_call" | custom-call | tf_op jit(solution)/shard_map/gather0/pallas_call | solution.py:64
  21.0 2.0 %collective-permute-start.4 = (bf16[512,512]{1,0:T(8,128)(2,1)S(1)}, bf16[512,512]{1,0:T(8,128)(2,1)S(1)}, u32[]{:S(2)}, u32[]{:S(2)}) collective-permute-start(bf16[512,512]{1,0:T(8,128)(2,1)S(1)} %get-tuple-element.31), channel_id=1, source_target_pairs={{0,2},{2,0},{1,3},{3,1},{4,6},{6,4},{5,7},{7,5},{8,10},{10,8},{9,1... | collective-permute-start | bytes 1572872 | tf_op jit(solution)/shard_map/ppermute | solution.py:345
  23.1 7.6 %collective-permute-done.1.refs_2_ = bf16[1040,256]{1,0:T(8,128)(2,1)S(1)} collective-permute-done((bf16[1040,256]{1,0:T(8,128)(2,1)S(1)}, bf16[1040,256]{1,0:T(8,128)(2,1)S(1)}, u32[]{:S(2)}, u32[]{:S(2)}) %collective-permute-start.1) | collective-permute-done | bytes 532512 | tf_op jit(solution)/shard_map/ppermute | solution.py:323
  30.6 1.3 %collective-permute-start.11 = (bf16[1040,256]{1,0:T(8,128)(2,1)S(1)}, bf16[1040,256]{1,0:T(8,128)(2,1)S(1)}, u32[]{:S(2)}, u32[]{:S(2)}) collective-permute-start(bf16[1040,256]{1,0:T(8,128)(2,1)S(1)} %collective-permute-done.1.refs_2_), channel_id=1, source_target_pairs={{4,0},{8,4},{5,1},{9,5},{6,2},{10,6},{7,3},{11,7},{20,16},{24,20},... | collective-permute-start | bytes 1597448 | tf_op jit(solution)/shard_map/ppermute | solution.py:323
  32.7 1.5 %collective-permute-done.6.refs_1_ = bf16[1040,256]{1,0:T(8,128)(2,1)S(1)} collective-permute-done((bf16[1040,256]{1,0:T(8,128)(2,1)S(1)}, bf16[1040,256]{1,0:T(8,128)(2,1)S(1)}, u32[]{:S(2)}, u32[]{:S(2)}) %collective-permute-start.6) | collective-permute-done | bytes 532512 | tf_op jit(solution)/shard_map/ppermute | solution.py:323
  35.1 1.3 %collective-permute-start.10 = (bf16[1024,256]{1,0:T(8,128)(2,1)S(1)}, bf16[1024,256]{1,0:T(8,128)(2,1)S(1)}, u32[]{:S(2)}, u32[]{:S(2)}) collective-permute-start(bf16[1024,256]{1,0:T(8,128)(2,1)S(1)} %get-tuple-element.37), channel_id=1, source_target_pairs={{4,0},{8,4},{5,1},{9,5},{6,2},{10,6},{7,3},{11,7},{20,16},{24,20},... | collective-permute-start | bytes 1572872 | tf_op jit(solution)/shard_map/ppermute | solution.py:323
  36.4 0.8 %total0.1.refs_0_.first = bf16[512,512]{1,0:T(8,128)(2,1)S(1)} custom-call(bf16[1024,1024]{1,0:T(8,128)(2,1)S(1)} %get-tuple-element.30.refs_0_, bf16[1024,512]{1,0:T(8,128)(2,1)S(1)} %get-tuple-element.28.refs_0_.refs_2_.refs_1_, bf16[512,512]{1,0:T(8,128)(2,1)S(1)} %collective-permute-done.4.refs_2_, bf16[1024,512]{1,0:T(8,128)(2,1)S(1)} %rows3.1.refs_3_.refs_0_), custom_call_target="tpu_custom_call" | custom-call | tf_op jit(solution)/shard_map/total0/pallas_call | solution.py:64
  38.0 9.5 %collective-permute-done.11.refs_1_ = bf16[1040,256]{1,0:T(8,128)(2,1)S(1)} collective-permute-done((bf16[1040,256]{1,0:T(8,128)(2,1)S(1)}, bf16[1040,256]{1,0:T(8,128)(2,1)S(1)}, u32[]{:S(2)}, u32[]{:S(2)}) %collective-permute-start.11) | collective-permute-done | bytes 532512 | tf_op jit(solution)/shard_map/ppermute | solution.py:323
  48.1 1.7 %collective-permute-start.13 = (bf16[512,256]{1,0:T(8,128)(2,1)S(1)}, bf16[512,256]{1,0:T(8,128)(2,1)S(1)}, u32[]{:S(2)}, u32[]{:S(2)}) collective-permute-start(bf16[512,256]{1,0:T(8,128)(2,1)S(1)} %far_b.1.refs_0_), channel_id=1, source_target_pairs={{0,2},{2,0},{1,3},{3,1},{4,6},{6,4},{5,7},{7,5},{8,10},{10,8},{9,1... | collective-permute-start | bytes 786440 | tf_op jit(solution)/shard_map/ppermute | solution.py:345
  49.8 2.5 %collective-permute-done.9.refs_2_ = bf16[512,512]{1,0:T(8,128)(2,1)S(1)} collective-permute-done((bf16[512,512]{1,0:T(8,128)(2,1)S(1)}, bf16[512,512]{1,0:T(8,128)(2,1)S(1)}, u32[]{:S(2)}, u32[]{:S(2)}) %collective-permute-start.9) | collective-permute-done | bytes 524320 | tf_op jit(solution)/shard_map/ppermute | solution.py:345
  52.3 0.8 %total3.1.refs_3_ = bf16[512,512]{1,0:T(8,128)(2,1)S(1)} custom-call(bf16[1024,1024]{1,0:T(8,128)(2,1)S(1)} %get-tuple-element.38.refs_3_.refs_0_, bf16[1024,512]{1,0:T(8,128)(2,1)S(1)} %get-tuple-element.34.refs_2_.refs_3_.refs_1_, bf16[512,512]{1,0:T(8,128)(2,1)S(1)} %collective-permute-done.9.refs_2_, f32[8,128]{1,0:T(8,128)S(1)} %fence.10.refs_3_), custom_call_target="tpu_custom_call" | custom-call | tf_op jit(solution)/shard_map/total3/pallas_call | solution.py:64
  53.1 1.3 %collective-permute-start.14 = (bf16[512,512]{1,0:T(8,128)(2,1)S(1)}, bf16[512,512]{1,0:T(8,128)(2,1)S(1)}, u32[]{:S(2)}, u32[]{:S(2)}) collective-permute-start(bf16[512,512]{1,0:T(8,128)(2,1)S(1)} %total3.1.refs_3_), channel_id=1, source_target_pairs={{8,0},{9,1},{10,2},{11,3},{24,16},{25,17},{26,18},{27,19}} | collective-permute-start | bytes 1572872 | tf_op jit(solution)/shard_map/ppermute | solution.py:323
  54.4 2.3 %collective-permute-done.10.refs_1_ = bf16[1024,256]{1,0:T(8,128)(2,1)S(1)} collective-permute-done((bf16[1024,256]{1,0:T(8,128)(2,1)S(1)}, bf16[1024,256]{1,0:T(8,128)(2,1)S(1)}, u32[]{:S(2)}, u32[]{:S(2)}) %collective-permute-start.10) | collective-permute-done | bytes 524320 | tf_op jit(solution)/shard_map/ppermute | solution.py:323
  57.2 1.7 %collective-permute-start.12 = (bf16[512,256]{1,0:T(8,128)(2,1)S(1)}, bf16[512,256]{1,0:T(8,128)(2,1)S(1)}, u32[]{:S(2)}, u32[]{:S(2)}) collective-permute-start(bf16[512,256]{1,0:T(8,128)(2,1)S(1)} %far_a.1.refs_3_), channel_id=1, source_target_pairs={{0,2},{2,0},{1,3},{3,1},{4,6},{6,4},{5,7},{7,5},{8,10},{10,8},{9,1... | collective-permute-start | bytes 786440 | tf_op jit(solution)/shard_map/ppermute | solution.py:345
  59.5 4.2 %collective-permute-done.12.refs_3_.refs_2_ = bf16[512,256]{1,0:T(8,128)(2,1)S(1)} collective-permute-done((bf16[512,256]{1,0:T(8,128)(2,1)S(1)}, bf16[512,256]{1,0:T(8,128)(2,1)S(1)}, u32[]{:S(2)}, u32[]{:S(2)}) %collective-permute-start.12) | collective-permute-done | bytes 262176 | tf_op jit(solution)/shard_map/ppermute | solution.py:345
  65.0 4.1 %collective-permute-done.14.fourth = bf16[512,512]{1,0:T(8,128)(2,1)S(1)} collective-permute-done((bf16[512,512]{1,0:T(8,128)(2,1)S(1)}, bf16[512,512]{1,0:T(8,128)(2,1)S(1)}, u32[]{:S(2)}, u32[]{:S(2)}) %collective-permute-start.14) | collective-permute-done | bytes 524320 | tf_op jit(solution)/shard_map/ppermute | solution.py:323
  69.1 1.9 %interleave.1 = bf16[512,4,512]{2,1,0:T(4,128)(2,1)} custom-call(bf16[512,512]{1,0:T(8,128)(2,1)S(1)} %total0.1.refs_0_.first, bf16[512,512]{1,0:T(8,128)(2,1)S(1)} %total1.1.refs_3_.second, bf16[512,256]{1,0:T(8,128)(2,1)S(1)} %total2a.1.third_a, bf16[512,256]{1,0:T(8,128)(2,1)S(1)} %total2b.1.refs_0_.third_b, ...), custom_call_target="tpu_custom_call" | custom-call | tf_op jit(solution)/shard_map/interleave/pallas_call | solution.py:161
  (27 shorter events, 5.9 us)
Async XLA Ops:
  2.4 17.7 %collective-permute-start.3 = (bf16[1024,256]{1,0:T(8,128)(2,1)S(1)}, bf16[1024,256]{1,0:T(8,128)(2,1)S(1)}, u32[]{:S(2)}, u32[]{:S(2)}) collective-permute-start(bf16[1024,256]{1,0:T(8,128)(2,1)S(1)} %get-tuple-element.32.refs_0_), channel_id=1, source_target_pairs={{4,0},{8,4},{12,8},{5,1},{9,5},{13,9},{6,2},{10,6},{14,10},{7,3},{... | collective-permute-start | bytes 1572872 | tf_op jit(solution)/shard_map/ppermute | solution.py:323
  3.7 8.6 %collective-permute-start = (s32[8,512]{1,0:T(8,128)S(1)}, s32[8,512]{1,0:T(8,128)S(1)}, u32[]{:S(2)}, u32[]{:S(2)}) collective-permute-start(s32[8,512]{1,0:T(8,128)S(1)} %get-tuple-element.25.refs_2_), channel_id=1, source_target_pairs={{0,2},{2,0},{1,3},{3,1},{4,6},{6,4},{5,7},{7,5},{8,10},{10,8},{9,1... | collective-permute-start | bytes 49160 | tf_op jit(solution)/shard_map/ppermute | solution.py:345
  6.7 26.0 %collective-permute-start.5 = (bf16[1024,256]{1,0:T(8,128)(2,1)S(1)}, bf16[1024,256]{1,0:T(8,128)(2,1)S(1)}, u32[]{:S(2)}, u32[]{:S(2)}) collective-permute-start(bf16[1024,256]{1,0:T(8,128)(2,1)S(1)} %get-tuple-element.32.refs_0_), channel_id=1, source_target_pairs={{0,8},{1,9},{2,10},{3,11},{16,24},{17,25},{18,26},{19,27}} | collective-permute-start | bytes 1572872 | tf_op jit(solution)/shard_map/ppermute | solution.py:323
  12.7 21.5 %collective-permute-start.6 = (bf16[1040,256]{1,0:T(8,128)(2,1)S(1)}, bf16[1040,256]{1,0:T(8,128)(2,1)S(1)}, u32[]{:S(2)}, u32[]{:S(2)}) collective-permute-start(bf16[1040,256]{1,0:T(8,128)(2,1)S(1)} %get-tuple-element.27), channel_id=1, source_target_pairs={{0,8},{1,9},{2,10},{3,11},{16,24},{17,25},{18,26},{19,27}} | collective-permute-start | bytes 1597448 | tf_op jit(solution)/shard_map/ppermute | solution.py:323
  15.0 15.7 %collective-permute-start.1 = (bf16[1040,256]{1,0:T(8,128)(2,1)S(1)}, bf16[1040,256]{1,0:T(8,128)(2,1)S(1)}, u32[]{:S(2)}, u32[]{:S(2)}) collective-permute-start(bf16[1040,256]{1,0:T(8,128)(2,1)S(1)} %get-tuple-element.27), channel_id=1, source_target_pairs={{4,0},{8,4},{12,8},{5,1},{9,5},{13,9},{6,2},{10,6},{14,10},{7,3},{... | collective-permute-start | bytes 1597448 | tf_op jit(solution)/shard_map/ppermute | solution.py:323
  16.3 3.8 %collective-permute-start.2 = (bf16[1024,512]{1,0:T(8,128)(2,1)S(1)}, bf16[1024,512]{1,0:T(8,128)(2,1)S(1)}, u32[]{:S(2)}, u32[]{:S(2)}) collective-permute-start(bf16[1024,512]{1,0:T(8,128)(2,1)S(1)} %get-tuple-element.28.refs_0_.refs_2_.refs_1_), channel_id=1, source_target_pairs={{0,1},{1,0},{2,3},{3,2},{4,5},{5,4},{6,7},{7,6},{8,9},{9,8},{10,11... | collective-permute-start | bytes 3145736 | tf_op jit(solution)/shard_map/ppermute | solution.py:345
  21.0 15.4 %collective-permute-start.4 = (bf16[512,512]{1,0:T(8,128)(2,1)S(1)}, bf16[512,512]{1,0:T(8,128)(2,1)S(1)}, u32[]{:S(2)}, u32[]{:S(2)}) collective-permute-start(bf16[512,512]{1,0:T(8,128)(2,1)S(1)} %get-tuple-element.31), channel_id=1, source_target_pairs={{0,2},{2,0},{1,3},{3,1},{4,6},{6,4},{5,7},{7,5},{8,10},{10,8},{9,1... | collective-permute-start | bytes 1572872 | tf_op jit(solution)/shard_map/ppermute | solution.py:345
  30.6 16.9 %collective-permute-start.11 = (bf16[1040,256]{1,0:T(8,128)(2,1)S(1)}, bf16[1040,256]{1,0:T(8,128)(2,1)S(1)}, u32[]{:S(2)}, u32[]{:S(2)}) collective-permute-start(bf16[1040,256]{1,0:T(8,128)(2,1)S(1)} %collective-permute-done.1.refs_2_), channel_id=1, source_target_pairs={{4,0},{8,4},{5,1},{9,5},{6,2},{10,6},{7,3},{11,7},{20,16},{24,20},... | collective-permute-start | bytes 1597448 | tf_op jit(solution)/shard_map/ppermute | solution.py:323
  34.5 2.7 %collective-permute-start.8 = (bf16[512,512]{1,0:T(8,128)(2,1)S(1)}, bf16[512,512]{1,0:T(8,128)(2,1)S(1)}, u32[]{:S(2)}, u32[]{:S(2)}) collective-permute-start(bf16[512,512]{1,0:T(8,128)(2,1)S(1)} %get-tuple-element.39), channel_id=1, source_target_pairs={{0,1},{1,0},{2,3},{3,2},{4,5},{5,4},{6,7},{7,6},{8,9},{9,8},{10,11... | collective-permute-start | bytes 1572872 | tf_op jit(solution)/shard_map/ppermute | solution.py:345
  34.6 2.6 %collective-permute-start.7 = (bf16[512,512]{1,0:T(8,128)(2,1)S(1)}, bf16[512,512]{1,0:T(8,128)(2,1)S(1)}, u32[]{:S(2)}, u32[]{:S(2)}) collective-permute-start(bf16[512,512]{1,0:T(8,128)(2,1)S(1)} %get-tuple-element.40), channel_id=1, source_target_pairs={{0,1},{1,0},{2,3},{3,2},{4,5},{5,4},{6,7},{7,6},{8,9},{9,8},{10,11... | collective-permute-start | bytes 1572872 | tf_op jit(solution)/shard_map/ppermute | solution.py:345
  35.1 21.6 %collective-permute-start.10 = (bf16[1024,256]{1,0:T(8,128)(2,1)S(1)}, bf16[1024,256]{1,0:T(8,128)(2,1)S(1)}, u32[]{:S(2)}, u32[]{:S(2)}) collective-permute-start(bf16[1024,256]{1,0:T(8,128)(2,1)S(1)} %get-tuple-element.37), channel_id=1, source_target_pairs={{4,0},{8,4},{5,1},{9,5},{6,2},{10,6},{7,3},{11,7},{20,16},{24,20},... | collective-permute-start | bytes 1572872 | tf_op jit(solution)/shard_map/ppermute | solution.py:323
  37.4 14.8 %collective-permute-start.9 = (bf16[512,512]{1,0:T(8,128)(2,1)S(1)}, bf16[512,512]{1,0:T(8,128)(2,1)S(1)}, u32[]{:S(2)}, u32[]{:S(2)}) collective-permute-start(bf16[512,512]{1,0:T(8,128)(2,1)S(1)} %get-tuple-element.36), channel_id=1, source_target_pairs={{0,2},{2,0},{1,3},{3,1},{4,6},{6,4},{5,7},{7,5},{8,10},{10,8},{9,1... | collective-permute-start | bytes 1572872 | tf_op jit(solution)/shard_map/ppermute | solution.py:345
  48.1 10.9 %collective-permute-start.13 = (bf16[512,256]{1,0:T(8,128)(2,1)S(1)}, bf16[512,256]{1,0:T(8,128)(2,1)S(1)}, u32[]{:S(2)}, u32[]{:S(2)}) collective-permute-start(bf16[512,256]{1,0:T(8,128)(2,1)S(1)} %far_b.1.refs_0_), channel_id=1, source_target_pairs={{0,2},{2,0},{1,3},{3,1},{4,6},{6,4},{5,7},{7,5},{8,10},{10,8},{9,1... | collective-permute-start | bytes 786440 | tf_op jit(solution)/shard_map/ppermute | solution.py:345
  53.1 16.0 %collective-permute-start.14 = (bf16[512,512]{1,0:T(8,128)(2,1)S(1)}, bf16[512,512]{1,0:T(8,128)(2,1)S(1)}, u32[]{:S(2)}, u32[]{:S(2)}) collective-permute-start(bf16[512,512]{1,0:T(8,128)(2,1)S(1)} %total3.1.refs_3_), channel_id=1, source_target_pairs={{8,0},{9,1},{10,2},{11,3},{24,16},{25,17},{26,18},{27,19}} | collective-permute-start | bytes 1572872 | tf_op jit(solution)/shard_map/ppermute | solution.py:323
  57.2 6.4 %collective-permute-start.12 = (bf16[512,256]{1,0:T(8,128)(2,1)S(1)}, bf16[512,256]{1,0:T(8,128)(2,1)S(1)}, u32[]{:S(2)}, u32[]{:S(2)}) collective-permute-start(bf16[512,256]{1,0:T(8,128)(2,1)S(1)} %far_a.1.refs_3_), channel_id=1, source_target_pairs={{0,2},{2,0},{1,3},{3,1},{4,6},{6,4},{5,7},{7,5},{8,10},{10,8},{9,1... | collective-permute-start | bytes 786440 | tf_op jit(solution)/shard_map/ppermute | solution.py:345

commit v7 on v6

--- a/solution.py
+++ b/solution.py
@@ -9,6 +9,7 @@
 
 BAND = 4
 TAIL = 16
+WEIGHTS = {'step1': 40, 'step2': 6, 'step3': 20, 'step4': 3, 'step5': 1, 'step6': 1, 'step7': 25, 'total0': 14, 'gather0': 8, 'total2b': 0, 'total1': 4}
 
 
 def params(mib):
@@ -69,7 +70,9 @@
         out_shape=[jax.ShapeDtypeStruct(shape, kind) for shape, kind in shapes],
         scratch_shapes=scratch,
         compiler_params=params(mib),
-        cost_estimate=pl.CostEstimate(flops=0, bytes_accessed=0, transcendentals=0),
+        cost_estimate=pl.CostEstimate(
+            flops=WEIGHTS.get(name, 0) * 10**9, bytes_accessed=0, transcendentals=0
+        ),
         name=name,
     )(*inputs, *events)
 
@@ -114,7 +117,7 @@
 
 
 def finish_body(first, second, *refs):
-    sums_refs, (own, message) = refs[:-2], refs[-2:]
+    sums_refs, (own, message, short, last) = refs[:-4], refs[-4:]
     samples, cut = first.shape
     sums = [sum(r[i:i + 1] for r in sums_refs) for i in range(3)]
     means, scales = variant_stats(sums)
@@ -122,23 +125,35 @@
     rest = standardize(second[...], means[:, cut:], scales[:, cut:])
     own[:, cut:] = rest
     message[:samples] = rest
+    middle = short.shape[1]
+    short[:samples] = rest[:, :middle]
+    last[...] = rest[:, middle:]
     rows = split3(means[:, :cut]) + split3(scales[:, :cut])
-    rows.append(jnp.zeros((TAIL - len(rows), cut), jnp.bfloat16))
-    message[samples:] = jnp.concatenate(rows, axis=0)
+    none = jnp.zeros((TAIL, cut), jnp.bfloat16)
+    message[samples:] = jnp.concatenate(rows + [none[len(rows):]], axis=0)
+    spans = [slice(i, i + middle) for i in range(0, cut, middle)]
+    rows = [row[:, span] for span in spans for row in rows]
+    short[samples:] = jnp.concatenate(rows + [none[len(rows):, :middle]], axis=0)
 
 
 def finish(first, second, all_sums, events):
     samples, cut = first.shape
+    shapes = [
+        (samples, 2 * cut),
+        (samples + TAIL, cut),
+        (samples + TAIL, cut // 2),
+        (samples, cut // 2),
+    ]
     return call(
         finish_body,
         "finish",
-        [((samples, 2 * cut), jnp.bfloat16), ((samples + TAIL, cut), jnp.bfloat16)],
+        [(s, jnp.bfloat16) for s in shapes],
         [first, second, *all_sums],
         events=events,
     )
 
 
-def interleave_body(first, second, third_a, third_b, fourth, out):
+def interleave_body(first, second, third_a, third_b, fourth_a, fourth_b, out):
     tile, width = first.shape
     count = min(tile, 64)
     size = BAND * count
@@ -150,7 +165,8 @@
     for i in range(tile // count):
         span = slice(i * count, (i + 1) * count)
         third = jnp.concatenate([third_a[span], third_b[span]], axis=1)
-        rows = jnp.concatenate([first[span], second[span], third, fourth[span]], axis=0)
+        fourth = jnp.concatenate([fourth_a[span], fourth_b[span]], axis=1)
+        rows = jnp.concatenate([first[span], second[span], third, fourth], axis=0)
         turned = jnp.dot(order, rows, preferred_element_type=jnp.float32)
         out[span] = turned.astype(jnp.bfloat16).reshape(count, BAND, width)
 
@@ -217,11 +233,15 @@
     if not spare:
         send_parts(whole, cols[...], parts)
         return
-    choose(
-        holds_three(),
-        lambda: send_parts(whole, cols[...], parts),
-        lambda: copy_parts(spare, parts),
-    )
+    cut = parts[0].shape[1]
+    for i in range(width // cut):
+        span = slice(i * cut, (i + 1) * cut)
+        group = parts[i * n_spare:(i + 1) * n_spare]
+        choose(
+            holds_three(),
+            functools.partial(send_parts, whole, cols[:, span], group),
+            functools.partial(copy_parts, [r.at[:, span] for r in spare], group),
+        )
 
 
 def from_tail(tail):
@@ -235,9 +255,20 @@
     out[:, cut:] = message[:samples]
 
 
-def near_body(whole, first, message, cols, half, *parts):
-    assemble_body(first, message, cols)
-    half[...] = cols[:, :half.shape[1]]
+def ahead_body(first, short, out):
+    samples, width = short.shape[0] - TAIL, short.shape[1]
+    for i in range(first.shape[1] // width):
+        span = slice(i * width, (i + 1) * width)
+        tail = short[samples + 6 * i:samples + 6 * i + 6]
+        out[:, span] = standardize(first[:, span], *from_tail(tail))
+
+
+def near_body(whole, first, short, last, cols, second, *parts):
+    cut, width = first.shape[1], short.shape[1]
+    second[:, :width] = short[:whole.shape[0]]
+    second[:, width:] = last[...]
+    cols[:, :cut] = first[...]
+    cols[:, cut:] = second[...]
     send_parts(whole, cols[...], parts)
 
 
@@ -266,6 +297,10 @@
     out[...] = summed(whole, cols[:whole.shape[0]], [r[...] for r in arrived])
 
 
+def total_span_body(begin, whole, cols, *refs):
+    total_body(whole, cols.at[:, begin:begin + refs[-1].shape[1]], *refs)
+
+
 def total_or_none_body(whole, cols, *refs):
     out = refs[-1]
 
@@ -275,18 +310,18 @@
     choose(holds_three(), none, lambda: total_body(whole, cols, *refs))
 
 
-def total_near_body(n_parts, whole, cols, *refs):
-    first, later, out = refs[:n_parts], refs[n_parts:-1], refs[-1]
-
-    def displaced():
+def total_near_body(n_parts, n_first, whole, cols, *refs):
+    first, later, out = refs[:n_first], refs[n_first:-1], refs[-1]
+
+    def total(parts):
         begin = 0
-        for i in range(0, len(later), n_parts):
-            group = later[i:i + n_parts]
+        for i in range(0, len(parts), n_parts):
+            group = parts[i:i + n_parts]
             span = slice(begin, begin + group[0].shape[1])
             out[:, span] = summed(whole, cols[:, span], [r[...] for r in group])
             begin = span.stop
 
-    choose(holds_three(), displaced, lambda: total_body(whole, cols, *first, out))
+    choose(holds_three(), lambda: total(later), lambda: total(first))
 
 
 def fence_body(*refs):
@@ -365,7 +400,7 @@
     def gather(part, others, cols, name, events, spare=()):
         block = ((samples, width * n_sub), jnp.bfloat16)
         body = functools.partial(gather_body, n_sub, 1 + len(others), len(spare))
-        shapes = [block] + part_shapes(width)
+        shapes = [block] + (part_shapes(width // 2) * 2 if spare else part_shapes(width))
         inputs = [part, *others, cols, *spare]
         whole, *parts = call(body, name, shapes, inputs, events=events)
         return whole, parts
@@ -381,28 +416,32 @@
 
     first, second, sums_own = encode(dosages, observed)
     near_a = down(first)
-    step = fence(20, first)
+    step = fence(WEIGHTS["step1"], first)
     sums_own, first_up, step = together(sums_own, first, step)
     up_a = up_two(first_up)
     arrived_sums = [swapped(sums_own, "smp", d) for d in range(1, n_smp)]
-    step = fence(20, step)
-    own, message = finish(first, second, [sums_own] + arrived_sums, [step])
-    near_b, up_b = down(message), up_two(message)
+    step = fence(WEIGHTS["step2"], step)
+    own, message, short, last = finish(first, second, [sums_own] + arrived_sums, [step])
+    near_b, up_b = down(short), up_two(message)
     others = others_of(own, 1)
-    step = fence(20, own)
+    step = fence(WEIGHTS["step3"], own)
+    last, *others = together(last, *others)
+    near_c = down(last)
 
     whole, part0 = gather(own, others, own, "gather0", [near_a, step])
     got0 = sent(part0)
     near_b, whole = together(near_b, whole)
-    far_b = down_again(near_b)
     half = ((samples, width // 2), jnp.bfloat16)
-    cols1, near_a, *part1 = call(
+    (near_a,) = call(ahead_body, "ahead", [half], [near_a, near_b])
+    far_a = down_again(near_a)
+    near_c, near_a = together(near_c, near_a)
+    cols1, second, *part1 = call(
         near_body,
         "near",
         [((samples, width), jnp.bfloat16), half] + part_shapes(width),
-        [whole, near_a, near_b],
-    )
-    far_a = down_again(near_a)
+        [whole, near_a, near_b, near_c],
+    )
+    far_b = down_again(second)
     (rows3,) = call(
         assemble_body,
         "rows3",
@@ -412,32 +451,39 @@
     )
     others3 = others_of(rows3, 2)
     panel0 = total(whole, own, got0, "total0", [rows3])
-    whole3, part3 = gather(rows3, others3, cols1, "gather3", [fence(3, panel0)], part1)
-    got3 = sent(part3)
-    part2_b = far_parts(far_b, width // 2, "far_b", [whole3])
-    got2_b = sent(part2_b)
-    panel3 = total(whole3, cols1, got3, "total3", [fence(12, *part2_b)])
+    whole3, part3 = gather(rows3, others3, cols1, "gather3", [fence(WEIGHTS["step4"], panel0)], part1)
+    count = n_smp - 1
+    got3 = [sent(part3[:count]), sent(part3[count:])]
+    part2_a = far_parts(far_a, 0, "far_a", [whole3])
+    got2_a = sent(part2_a)
+    panel3 = []
+    step = fence(WEIGHTS["step5"], *part2_a)
+    for i in range(2):
+        shape = ((rows_owned, width // 2), jnp.bfloat16)
+        body = functools.partial(total_span_body, i * (width // 2))
+        (panel,) = call(body, "total3", [shape], [whole3, cols1, *got3[i]], events=[step])
+        step = fence(WEIGHTS["step6"], panel)
+        panel3.append(down_two(panel))
     later = []
     if not shared:
-        *part1, panel3 = together(*part1, panel3)
+        *part1, step = together(*part1, step)
         later = sent(part1, holds)
-    part2_a = far_parts(far_a, 0, "far_a", [panel3])
-    panel3 = down_two(panel3)
-    got2_a = sent(part2_a)
+    part2_b = far_parts(far_b, width // 2, "far_b", [step])
+    got2_b = sent(part2_b)
     if shared:
         later = got2_a + got2_b
     ending = total_or_none_body if shared else total_body
-    panel2_b = total(whole, far_b, got2_b, "total2b", [*part2_a], ending)
+    panel2_a = total(whole, far_a, got2_a, "total2a", [*part2_b], ending)
     panel1 = total(
         whole,
         cols1,
-        got3 + later,
+        got3[0] + got3[1] + later,
         "total1",
-        [fence(3, panel2_b)],
-        functools.partial(total_near_body, n_smp - 1),
-    )
-    panel2_a = total(whole, far_a, got2_a, "total2a", [panel1], ending)
-    return interleave([panel0, panel1, panel2_a, panel2_b, panel3])
+        [fence(WEIGHTS["step7"], panel2_a)],
+        functools.partial(total_near_body, count, 2 * count),
+    )
+    panel2_b = total(whole, far_b, got2_b, "total2b", [panel1], ending)
+    return interleave([panel0, panel1, panel2_a, panel2_b, *panel3])
 
 
 def solution(mesh):

time: 71.2 us -> 67.6 us (0.949)
  waiting for transfers between devices: 35.4 us -> 26.4 us
  starting transfers between devices: 23.9 us -> 28.5 us
    ppermute x7 -> x9, waiting for transfers between devices: 28.7 us -> 13.6 us  [along(): return lax.ppermute(x, 'var', route)]
    ppermute x8 -> x9, waiting for transfers between devices: 6.71 us -> 12.8 us  [swapped(): return lax.ppermute(x, axis, [(i, (i + distance) % n) for i in range(n)])]
    ppermute x7 -> x9, starting transfers between devices: 14.2 us -> 17.5 us  [along(): return lax.ppermute(x, 'var', route)]
    ppermute x8 -> x9, starting transfers between devices: 9.7 us -> 11.1 us  [swapped(): return lax.ppermute(x, axis, [(i, (i + distance) % n) for i in range(n)])]
    pallas_call x13 -> x15, Pallas kernels: 9.43 us -> 10.1 us  [call(): pl.pallas_call(with_events, in_specs=[pl.BlockSpec(memory_space=place)] *...]
  transfers between devices with their start and end apart: 15 -> 18, of which waited for: 8 -> 12; matrix products, arithmetic and copies ran while one was open for 0% -> 0% of each run, Pallas kernels for 10% -> 12%
where the time goes in v7:
time: 67.6 us; the launch traced here: 67.3 us
  starting transfers between devices  28.5 us (42%)
  waiting for transfers between devices  26.4 us (39%)
  Pallas kernels  12 us (18%)
    ppermute x9, starting transfers between devices, along(): return lax.ppermute(x, 'var', route)  17.5 us
    ppermute x9, waiting for transfers between devices, along(): return lax.ppermute(x, 'var', route)  13.6 us
    ppermute x9, waiting for transfers between devices, swapped(): return lax.ppermute(x, axis, [(i, (i + distance) % n) for i in range(n)])  12.8 us
    ppermute x9, starting transfers between devices, swapped(): return lax.ppermute(x, axis, [(i, (i + distance) % n) for i in range(n)])  11.1 us
    pallas_call x15, Pallas kernels, call(): pl.pallas_call(with_events, in_specs=[pl.BlockSpec(memory_space=place)] *...  10.1 us
    pallas_call x1, Pallas kernels, interleave(): pl.pallas_call(interleave_body, grid=(rows // tile,), in_specs=[pl.BlockS...  1.87 us
  transfers between devices with their start and end apart: 18, of which 12 were waited for; matrix products, arithmetic and copies ran while one was open for 0% of the time, Pallas kernels for 12%

profile of v7, /device:TPU:0, one launch (start us, length us, event | category | flops | bytes accessed | tf_op | source)
XLA Modules:
  0.0 67.3 jit_solution(2367905983608838791)
XLA Ops:
  0.0 2.4 %encode.1 = (bf16[1024,256]{1,0:T(8,128)(2,1)S(1)}, bf16[1024,256]{1,0:T(8,128)(2,1)S(1)}, s32[8,512]{1,0:T(8,128)S(1)}) custom-call(s32[1024,512]{1,0:T(8,128)} %refs_0_.1, s32[1024,512]{1,0:T(8,128)} %refs_1_.1), custom_call_target="tpu_custom_call" | custom-call | tf_op jit(solution)/shard_map/encode/pallas_call | solution.py:65
  2.4 1.3 %collective-permute-start.3 = (bf16[1024,256]{1,0:T(8,128)(2,1)S(1)}, bf16[1024,256]{1,0:T(8,128)(2,1)S(1)}, u32[]{:S(2)}, u32[]{:S(2)}) collective-permute-start(bf16[1024,256]{1,0:T(8,128)(2,1)S(1)} %get-tuple-element.41.refs_0_), channel_id=1, source_target_pairs={{4,0},{8,4},{12,8},{5,1},{9,5},{13,9},{6,2},{10,6},{14,10},{7,3},{... | collective-permute-start | bytes 1572872 | tf_op jit(solution)/shard_map/ppermute | solution.py:358
  3.7 3.0 %collective-permute-start = (s32[8,512]{1,0:T(8,128)S(1)}, s32[8,512]{1,0:T(8,128)S(1)}, u32[]{:S(2)}, u32[]{:S(2)}) collective-permute-start(s32[8,512]{1,0:T(8,128)S(1)} %get-tuple-element.32.refs_2_), channel_id=1, source_target_pairs={{0,2},{2,0},{1,3},{3,1},{4,6},{6,4},{5,7},{7,5},{8,10},{10,8},{9,1... | collective-permute-start | bytes 49160 | tf_op jit(solution)/shard_map/ppermute | solution.py:380
  6.7 5.6 %collective-permute-start.5 = (bf16[1024,256]{1,0:T(8,128)(2,1)S(1)}, bf16[1024,256]{1,0:T(8,128)(2,1)S(1)}, u32[]{:S(2)}, u32[]{:S(2)}) collective-permute-start(bf16[1024,256]{1,0:T(8,128)(2,1)S(1)} %get-tuple-element.41.refs_0_), channel_id=1, source_target_pairs={{0,8},{1,9},{2,10},{3,11},{16,24},{17,25},{18,26},{19,27}} | collective-permute-start | bytes 1572872 | tf_op jit(solution)/shard_map/ppermute | solution.py:358
  12.9 1.3 %collective-permute-start.1 = (bf16[1040,128]{1,0:T(8,128)(2,1)S(1)}, bf16[1040,128]{1,0:T(8,128)(2,1)S(1)}, u32[]{:S(2)}, u32[]{:S(2)}) collective-permute-start(bf16[1040,128]{1,0:T(8,128)(2,1)S(1)} %get-tuple-element.34), channel_id=1, source_target_pairs={{4,0},{8,4},{12,8},{5,1},{9,5},{13,9},{6,2},{10,6},{14,10},{7,3},{... | collective-permute-start | bytes 798728 | tf_op jit(solution)/shard_map/ppermute | solution.py:358
  14.2 2.9 %collective-permute-start.6 = (bf16[1040,256]{1,0:T(8,128)(2,1)S(1)}, bf16[1040,256]{1,0:T(8,128)(2,1)S(1)}, u32[]{:S(2)}, u32[]{:S(2)}) collective-permute-start(bf16[1040,256]{1,0:T(8,128)(2,1)S(1)} %get-tuple-element.42), channel_id=1, source_target_pairs={{0,8},{1,9},{2,10},{3,11},{16,24},{17,25},{18,26},{19,27}} | collective-permute-start | bytes 1597448 | tf_op jit(solution)/shard_map/ppermute | solution.py:358
  17.1 1.3 %collective-permute-start.7 = (bf16[1024,128]{1,0:T(8,128)(2,1)S(1)}, bf16[1024,128]{1,0:T(8,128)(2,1)S(1)}, u32[]{:S(2)}, u32[]{:S(2)}) collective-permute-start(bf16[1024,128]{1,0:T(8,128)(2,1)S(1)} %get-tuple-element.43), channel_id=1, source_target_pairs={{4,0},{8,4},{12,8},{5,1},{9,5},{13,9},{6,2},{10,6},{14,10},{7,3},{... | collective-permute-start | bytes 786440 | tf_op jit(solution)/shard_map/ppermute | solution.py:358
  18.4 1.7 %collective-permute-done.3.refs_3_.refs_0_ = bf16[1024,256]{1,0:T(8,128)(2,1)S(1)} collective-permute-done((bf16[1024,256]{1,0:T(8,128)(2,1)S(1)}, bf16[1024,256]{1,0:T(8,128)(2,1)S(1)}, u32[]{:S(2)}, u32[]{:S(2)}) %collective-permute-start.3) | collective-permute-done | bytes 524320 | tf_op jit(solution)/shard_map/ppermute | solution.py:358
  21.0 2.1 %collective-permute-start.4 = (bf16[512,512]{1,0:T(8,128)(2,1)S(1)}, bf16[512,512]{1,0:T(8,128)(2,1)S(1)}, u32[]{:S(2)}, u32[]{:S(2)}) collective-permute-start(bf16[512,512]{1,0:T(8,128)(2,1)S(1)} %get-tuple-element.40), channel_id=1, source_target_pairs={{0,2},{2,0},{1,3},{3,1},{4,6},{6,4},{5,7},{7,5},{8,10},{10,8},{9,1... | collective-permute-start | bytes 1572872 | tf_op jit(solution)/shard_map/ppermute | solution.py:380
  23.1 2.7 %collective-permute-done.1.refs_1_.refs_2_ = bf16[1040,128]{1,0:T(8,128)(2,1)S(1)} collective-permute-done((bf16[1040,128]{1,0:T(8,128)(2,1)S(1)}, bf16[1040,128]{1,0:T(8,128)(2,1)S(1)}, u32[]{:S(2)}, u32[]{:S(2)}) %collective-permute-start.1) | collective-permute-done | bytes 266272 | tf_op jit(solution)/shard_map/ppermute | solution.py:358
  26.0 1.3 %collective-permute-start.12 = (bf16[1024,256]{1,0:T(8,128)(2,1)S(1)}, bf16[1024,256]{1,0:T(8,128)(2,1)S(1)}, u32[]{:S(2)}, u32[]{:S(2)}) collective-permute-start(bf16[1024,256]{1,0:T(8,128)(2,1)S(1)} %ahead.1.refs_1_), channel_id=1, source_target_pairs={{4,0},{8,4},{5,1},{9,5},{6,2},{10,6},{7,3},{11,7},{20,16},{24,20},... | collective-permute-start | bytes 1572872 | tf_op jit(solution)/shard_map/ppermute | solution.py:358
  27.3 4.1 %collective-permute-done.7.refs_3_ = bf16[1024,128]{1,0:T(8,128)(2,1)S(1)} collective-permute-done((bf16[1024,128]{1,0:T(8,128)(2,1)S(1)}, bf16[1024,128]{1,0:T(8,128)(2,1)S(1)}, u32[]{:S(2)}, u32[]{:S(2)}) %collective-permute-start.7) | collective-permute-done | bytes 262176 | tf_op jit(solution)/shard_map/ppermute | solution.py:358
  32.2 1.3 %collective-permute-start.14 = (bf16[1024,256]{1,0:T(8,128)(2,1)S(1)}, bf16[1024,256]{1,0:T(8,128)(2,1)S(1)}, u32[]{:S(2)}, u32[]{:S(2)}) collective-permute-start(bf16[1024,256]{1,0:T(8,128)(2,1)S(1)} %get-tuple-element.52), channel_id=1, source_target_pairs={{4,0},{8,4},{5,1},{9,5},{6,2},{10,6},{7,3},{11,7},{20,16},{24,20},... | collective-permute-start | bytes 1572872 | tf_op jit(solution)/shard_map/ppermute | solution.py:358
  37.5 1.3 %collective-permute-start.10 = (bf16[512,256]{1,0:T(8,128)(2,1)S(1)}, bf16[512,256]{1,0:T(8,128)(2,1)S(1)}, u32[]{:S(2)}, u32[]{:S(2)}) collective-permute-start(bf16[512,256]{1,0:T(8,128)(2,1)S(1)} %get-tuple-element.49), channel_id=1, source_target_pairs={{0,2},{2,0},{1,3},{3,1},{4,6},{6,4},{5,7},{7,5},{8,10},{10,8},{9,1... | collective-permute-start | bytes 786440 | tf_op jit(solution)/shard_map/ppermute | solution.py:380
  39.6 3.2 %collective-permute-done.12.refs_1_ = bf16[1024,256]{1,0:T(8,128)(2,1)S(1)} collective-permute-done((bf16[1024,256]{1,0:T(8,128)(2,1)S(1)}, bf16[1024,256]{1,0:T(8,128)(2,1)S(1)}, u32[]{:S(2)}, u32[]{:S(2)}) %collective-permute-start.12) | collective-permute-done | bytes 524320 | tf_op jit(solution)/shard_map/ppermute | solution.py:358
  43.3 2.0 %collective-permute-start.13 = (bf16[512,256]{1,0:T(8,128)(2,1)S(1)}, bf16[512,256]{1,0:T(8,128)(2,1)S(1)}, u32[]{:S(2)}, u32[]{:S(2)}) collective-permute-start(bf16[512,256]{1,0:T(8,128)(2,1)S(1)} %far_a.1.refs_0_), channel_id=1, source_target_pairs={{0,2},{2,0},{1,3},{3,1},{4,6},{6,4},{5,7},{7,5},{8,10},{10,8},{9,1... | collective-permute-start | bytes 786440 | tf_op jit(solution)/shard_map/ppermute | solution.py:380
  45.3 1.4 %collective-permute-done.10.refs_2_ = bf16[512,256]{1,0:T(8,128)(2,1)S(1)} collective-permute-done((bf16[512,256]{1,0:T(8,128)(2,1)S(1)}, bf16[512,256]{1,0:T(8,128)(2,1)S(1)}, u32[]{:S(2)}, u32[]{:S(2)}) %collective-permute-start.10) | collective-permute-done | bytes 262176 | tf_op jit(solution)/shard_map/ppermute | solution.py:380
  47.3 1.3 %collective-permute-start.16 = (bf16[512,256]{1,0:T(8,128)(2,1)S(1)}, bf16[512,256]{1,0:T(8,128)(2,1)S(1)}, u32[]{:S(2)}, u32[]{:S(2)}) collective-permute-start(bf16[512,256]{1,0:T(8,128)(2,1)S(1)} %total3.2.refs_0_), channel_id=1, source_target_pairs={{8,0},{9,1},{10,2},{11,3},{24,16},{25,17},{26,18},{27,19}} | collective-permute-start | bytes 786440 | tf_op jit(solution)/shard_map/ppermute | solution.py:358
  48.6 3.8 %collective-permute-done.11.refs_2_.refs_3_ = bf16[512,256]{1,0:T(8,128)(2,1)S(1)} collective-permute-done((bf16[512,256]{1,0:T(8,128)(2,1)S(1)}, bf16[512,256]{1,0:T(8,128)(2,1)S(1)}, u32[]{:S(2)}, u32[]{:S(2)}) %collective-permute-start.11) | collective-permute-done | bytes 262176 | tf_op jit(solution)/shard_map/ppermute | solution.py:380
  52.9 1.3 %collective-permute-start.17 = (bf16[512,256]{1,0:T(8,128)(2,1)S(1)}, bf16[512,256]{1,0:T(8,128)(2,1)S(1)}, u32[]{:S(2)}, u32[]{:S(2)}) collective-permute-start(bf16[512,256]{1,0:T(8,128)(2,1)S(1)} %total3.3.refs_0_), channel_id=1, source_target_pairs={{8,0},{9,1},{10,2},{11,3},{24,16},{25,17},{26,18},{27,19}} | collective-permute-start | bytes 786440 | tf_op jit(solution)/shard_map/ppermute | solution.py:358
  54.7 1.3 %collective-permute-start.15 = (bf16[512,256]{1,0:T(8,128)(2,1)S(1)}, bf16[512,256]{1,0:T(8,128)(2,1)S(1)}, u32[]{:S(2)}, u32[]{:S(2)}) collective-permute-start(bf16[512,256]{1,0:T(8,128)(2,1)S(1)} %far_b.1.refs_3_), channel_id=1, source_target_pairs={{0,2},{2,0},{1,3},{3,1},{4,6},{6,4},{5,7},{7,5},{8,10},{10,8},{9,1... | collective-permute-start | bytes 786440 | tf_op jit(solution)/shard_map/ppermute | solution.py:380
  56.0 1.9 %collective-permute-done.13.refs_2_.refs_4_ = bf16[512,256]{1,0:T(8,128)(2,1)S(1)} collective-permute-done((bf16[512,256]{1,0:T(8,128)(2,1)S(1)}, bf16[512,256]{1,0:T(8,128)(2,1)S(1)}, u32[]{:S(2)}, u32[]{:S(2)}) %collective-permute-start.13) | collective-permute-done | bytes 262176 | tf_op jit(solution)/shard_map/ppermute | solution.py:380
  58.5 4.3 %collective-permute-done.15.refs_5_.refs_2_ = bf16[512,256]{1,0:T(8,128)(2,1)S(1)} collective-permute-done((bf16[512,256]{1,0:T(8,128)(2,1)S(1)}, bf16[512,256]{1,0:T(8,128)(2,1)S(1)}, u32[]{:S(2)}, u32[]{:S(2)}) %collective-permute-start.15) | collective-permute-done | bytes 262176 | tf_op jit(solution)/shard_map/ppermute | solution.py:380
  65.4 1.9 %interleave.1 = bf16[512,4,512]{2,1,0:T(4,128)(2,1)} custom-call(bf16[512,512]{1,0:T(8,128)(2,1)S(1)} %total0.1.refs_0_.first, bf16[512,512]{1,0:T(8,128)(2,1)S(1)} %total1.1.refs_3_.second, bf16[512,256]{1,0:T(8,128)(2,1)S(1)} %total2a.1.refs_0_.third_a, bf16[512,256]{1,0:T(8,128)(2,1)S(1)} %total2b.1.third_b, ...), custom_call_target="tpu_custom_call" | custom-call | tf_op jit(solution)/shard_map/interleave/pallas_call | solution.py:177
  (37 shorter events, 12.6 us)
Async XLA Ops:
  2.4 17.7 %collective-permute-start.3 = (bf16[1024,256]{1,0:T(8,128)(2,1)S(1)}, bf16[1024,256]{1,0:T(8,128)(2,1)S(1)}, u32[]{:S(2)}, u32[]{:S(2)}) collective-permute-start(bf16[1024,256]{1,0:T(8,128)(2,1)S(1)} %get-tuple-element.41.refs_0_), channel_id=1, source_target_pairs={{4,0},{8,4},{12,8},{5,1},{9,5},{13,9},{6,2},{10,6},{14,10},{7,3},{... | collective-permute-start | bytes 1572872 | tf_op jit(solution)/shard_map/ppermute | solution.py:358
  3.7 8.6 %collective-permute-start = (s32[8,512]{1,0:T(8,128)S(1)}, s32[8,512]{1,0:T(8,128)S(1)}, u32[]{:S(2)}, u32[]{:S(2)}) collective-permute-start(s32[8,512]{1,0:T(8,128)S(1)} %get-tuple-element.32.refs_2_), channel_id=1, source_target_pairs={{0,2},{2,0},{1,3},{3,1},{4,6},{6,4},{5,7},{7,5},{8,10},{10,8},{9,1... | collective-permute-start | bytes 49160 | tf_op jit(solution)/shard_map/ppermute | solution.py:380
  6.7 26.8 %collective-permute-start.5 = (bf16[1024,256]{1,0:T(8,128)(2,1)S(1)}, bf16[1024,256]{1,0:T(8,128)(2,1)S(1)}, u32[]{:S(2)}, u32[]{:S(2)}) collective-permute-start(bf16[1024,256]{1,0:T(8,128)(2,1)S(1)} %get-tuple-element.41.refs_0_), channel_id=1, source_target_pairs={{0,8},{1,9},{2,10},{3,11},{16,24},{17,25},{18,26},{19,27}} | collective-permute-start | bytes 1572872 | tf_op jit(solution)/shard_map/ppermute | solution.py:358
  12.8 4.3 %collective-permute-start.2 = (bf16[1024,512]{1,0:T(8,128)(2,1)S(1)}, bf16[1024,512]{1,0:T(8,128)(2,1)S(1)}, u32[]{:S(2)}, u32[]{:S(2)}) collective-permute-start(bf16[1024,512]{1,0:T(8,128)(2,1)S(1)} %get-tuple-element.35.refs_0_.refs_2_.refs_1_), channel_id=1, source_target_pairs={{0,1},{1,0},{2,3},{3,2},{4,5},{5,4},{6,7},{7,6},{8,9},{9,8},{10,11... | collective-permute-start | bytes 3145736 | tf_op jit(solution)/shard_map/ppermute | solution.py:380
  12.9 12.9 %collective-permute-start.1 = (bf16[1040,128]{1,0:T(8,128)(2,1)S(1)}, bf16[1040,128]{1,0:T(8,128)(2,1)S(1)}, u32[]{:S(2)}, u32[]{:S(2)}) collective-permute-start(bf16[1040,128]{1,0:T(8,128)(2,1)S(1)} %get-tuple-element.34), channel_id=1, source_target_pairs={{4,0},{8,4},{12,8},{5,1},{9,5},{13,9},{6,2},{10,6},{14,10},{7,3},{... | collective-permute-start | bytes 798728 | tf_op jit(solution)/shard_map/ppermute | solution.py:358
  14.2 20.1 %collective-permute-start.6 = (bf16[1040,256]{1,0:T(8,128)(2,1)S(1)}, bf16[1040,256]{1,0:T(8,128)(2,1)S(1)}, u32[]{:S(2)}, u32[]{:S(2)}) collective-permute-start(bf16[1040,256]{1,0:T(8,128)(2,1)S(1)} %get-tuple-element.42), channel_id=1, source_target_pairs={{0,8},{1,9},{2,10},{3,11},{16,24},{17,25},{18,26},{19,27}} | collective-permute-start | bytes 1597448 | tf_op jit(solution)/shard_map/ppermute | solution.py:358
  17.1 14.3 %collective-permute-start.7 = (bf16[1024,128]{1,0:T(8,128)(2,1)S(1)}, bf16[1024,128]{1,0:T(8,128)(2,1)S(1)}, u32[]{:S(2)}, u32[]{:S(2)}) collective-permute-start(bf16[1024,128]{1,0:T(8,128)(2,1)S(1)} %get-tuple-element.43), channel_id=1, source_target_pairs={{4,0},{8,4},{12,8},{5,1},{9,5},{13,9},{6,2},{10,6},{14,10},{7,3},{... | collective-permute-start | bytes 786440 | tf_op jit(solution)/shard_map/ppermute | solution.py:358
  21.0 14.1 %collective-permute-start.4 = (bf16[512,512]{1,0:T(8,128)(2,1)S(1)}, bf16[512,512]{1,0:T(8,128)(2,1)S(1)}, u32[]{:S(2)}, u32[]{:S(2)}) collective-permute-start(bf16[512,512]{1,0:T(8,128)(2,1)S(1)} %get-tuple-element.40), channel_id=1, source_target_pairs={{0,2},{2,0},{1,3},{3,1},{4,6},{6,4},{5,7},{7,5},{8,10},{10,8},{9,1... | collective-permute-start | bytes 1572872 | tf_op jit(solution)/shard_map/ppermute | solution.py:380
  26.0 16.8 %collective-permute-start.12 = (bf16[1024,256]{1,0:T(8,128)(2,1)S(1)}, bf16[1024,256]{1,0:T(8,128)(2,1)S(1)}, u32[]{:S(2)}, u32[]{:S(2)}) collective-permute-start(bf16[1024,256]{1,0:T(8,128)(2,1)S(1)} %ahead.1.refs_1_), channel_id=1, source_target_pairs={{4,0},{8,4},{5,1},{9,5},{6,2},{10,6},{7,3},{11,7},{20,16},{24,20},... | collective-permute-start | bytes 1572872 | tf_op jit(solution)/shard_map/ppermute | solution.py:358
  32.2 22.0 %collective-permute-start.14 = (bf16[1024,256]{1,0:T(8,128)(2,1)S(1)}, bf16[1024,256]{1,0:T(8,128)(2,1)S(1)}, u32[]{:S(2)}, u32[]{:S(2)}) collective-permute-start(bf16[1024,256]{1,0:T(8,128)(2,1)S(1)} %get-tuple-element.52), channel_id=1, source_target_pairs={{4,0},{8,4},{5,1},{9,5},{6,2},{10,6},{7,3},{11,7},{20,16},{24,20},... | collective-permute-start | bytes 1572872 | tf_op jit(solution)/shard_map/ppermute | solution.py:358
  34.5 2.0 %collective-permute-start.9 = (bf16[512,512]{1,0:T(8,128)(2,1)S(1)}, bf16[512,512]{1,0:T(8,128)(2,1)S(1)}, u32[]{:S(2)}, u32[]{:S(2)}) collective-permute-start(bf16[512,512]{1,0:T(8,128)(2,1)S(1)} %get-tuple-element.53), channel_id=1, source_target_pairs={{0,1},{1,0},{2,3},{3,2},{4,5},{5,4},{6,7},{7,6},{8,9},{9,8},{10,11... | collective-permute-start | bytes 1572872 | tf_op jit(solution)/shard_map/ppermute | solution.py:380
  34.6 2.6 %collective-permute-start.8 = (bf16[512,512]{1,0:T(8,128)(2,1)S(1)}, bf16[512,512]{1,0:T(8,128)(2,1)S(1)}, u32[]{:S(2)}, u32[]{:S(2)}) collective-permute-start(bf16[512,512]{1,0:T(8,128)(2,1)S(1)} %get-tuple-element.54), channel_id=1, source_target_pairs={{0,1},{1,0},{2,3},{3,2},{4,5},{5,4},{6,7},{7,6},{8,9},{9,8},{10,11... | collective-permute-start | bytes 1572872 | tf_op jit(solution)/shard_map/ppermute | solution.py:380
  37.5 9.2 %collective-permute-start.10 = (bf16[512,256]{1,0:T(8,128)(2,1)S(1)}, bf16[512,256]{1,0:T(8,128)(2,1)S(1)}, u32[]{:S(2)}, u32[]{:S(2)}) collective-permute-start(bf16[512,256]{1,0:T(8,128)(2,1)S(1)} %get-tuple-element.49), channel_id=1, source_target_pairs={{0,2},{2,0},{1,3},{3,1},{4,6},{6,4},{5,7},{7,5},{8,10},{10,8},{9,1... | collective-permute-start | bytes 786440 | tf_op jit(solution)/shard_map/ppermute | solution.py:380
  38.8 13.5 %collective-permute-start.11 = (bf16[512,256]{1,0:T(8,128)(2,1)S(1)}, bf16[512,256]{1,0:T(8,128)(2,1)S(1)}, u32[]{:S(2)}, u32[]{:S(2)}) collective-permute-start(bf16[512,256]{1,0:T(8,128)(2,1)S(1)} %get-tuple-element.50), channel_id=1, source_target_pairs={{0,2},{2,0},{1,3},{3,1},{4,6},{6,4},{5,7},{7,5},{8,10},{10,8},{9,1... | collective-permute-start | bytes 786440 | tf_op jit(solution)/shard_map/ppermute | solution.py:380
  43.3 14.7 %collective-permute-start.13 = (bf16[512,256]{1,0:T(8,128)(2,1)S(1)}, bf16[512,256]{1,0:T(8,128)(2,1)S(1)}, u32[]{:S(2)}, u32[]{:S(2)}) collective-permute-start(bf16[512,256]{1,0:T(8,128)(2,1)S(1)} %far_a.1.refs_0_), channel_id=1, source_target_pairs={{0,2},{2,0},{1,3},{3,1},{4,6},{6,4},{5,7},{7,5},{8,10},{10,8},{9,1... | collective-permute-start | bytes 786440 | tf_op jit(solution)/shard_map/ppermute | solution.py:380
  47.3 16.9 %collective-permute-start.16 = (bf16[512,256]{1,0:T(8,128)(2,1)S(1)}, bf16[512,256]{1,0:T(8,128)(2,1)S(1)}, u32[]{:S(2)}, u32[]{:S(2)}) collective-permute-start(bf16[512,256]{1,0:T(8,128)(2,1)S(1)} %total3.2.refs_0_), channel_id=1, source_target_pairs={{8,0},{9,1},{10,2},{11,3},{24,16},{25,17},{26,18},{27,19}} | collective-permute-start | bytes 786440 | tf_op jit(solution)/shard_map/ppermute | solution.py:358
  52.9 12.6 %collective-permute-start.17 = (bf16[512,256]{1,0:T(8,128)(2,1)S(1)}, bf16[512,256]{1,0:T(8,128)(2,1)S(1)}, u32[]{:S(2)}, u32[]{:S(2)}) collective-permute-start(bf16[512,256]{1,0:T(8,128)(2,1)S(1)} %total3.3.refs_0_), channel_id=1, source_target_pairs={{8,0},{9,1},{10,2},{11,3},{24,16},{25,17},{26,18},{27,19}} | collective-permute-start | bytes 786440 | tf_op jit(solution)/shard_map/ppermute | solution.py:358
  54.7 8.0 %collective-permute-start.15 = (bf16[512,256]{1,0:T(8,128)(2,1)S(1)}, bf16[512,256]{1,0:T(8,128)(2,1)S(1)}, u32[]{:S(2)}, u32[]{:S(2)}) collective-permute-start(bf16[512,256]{1,0:T(8,128)(2,1)S(1)} %far_b.1.refs_3_), channel_id=1, source_target_pairs={{0,2},{2,0},{1,3},{3,1},{4,6},{6,4},{5,7},{7,5},{8,10},{10,8},{9,1... | collective-permute-start | bytes 786440 | tf_op jit(solution)/shard_map/ppermute | solution.py:380
